TPU v7x, 256 devices: a whole 4x4x8 slice. The times are simulated.
256 devices in a mesh: dp: 32 (over x_lo, z, core), tensor: 8 (over y, x_hi).
Axes of the slice: x: 4 (x_hi: 2, x_lo: 2; x = x_hi * 2 + x_lo), y: 4, z: 8, core: 2. Of those that a mesh axis runs over, the one named last changes fastest.
Arguments:
- activations: bfloat16 [64, 512, 9216], P('dp', 'tensor'), may hold values from -6 to 6
- w_query: bfloat16 [9216, 4608], P('dp', 'tensor'), may hold values from -0.0625 to 0.0625
- key_weight_latent: bfloat16 [9216, 768], P('dp', 'tensor'), may hold values from -0.0625 to 0.0625
- query_exponent: int32 [4608], P('tensor'), may hold values from -13 to -11
- key_column_exponent: int32 [768], P('tensor'), may hold values from -13 to -11
- queries: bfloat16 [64, 512, 4608], P('dp', None, 'tensor'), may hold values from -6 to 6
- keys: bfloat16 [64, 512, 768], P('dp', None, 'tensor'), may hold values from -6 to 6
- teacher_attention_logits: bfloat16 [64, 48, 512, 512], P('dp', 'tensor'), may hold values from -8 to 8
- document_length: int32 [64, 4], P('dp'), may hold values from 1 to 256, 512 in all within a row
Outputs:
- grad_query: float32 [9216, 4608], P('dp', 'tensor')
- grad_key: float32 [9216, 768], P('dp', 'tensor')
Inputs may be any that keep to these rules, and one draw needn't show every extreme that they name: `document_length`: each group's lengths sum to 512.
All inputs are finite; a program needn't handle non-finite values.
Results may differ from a plain program's by a relative error of at most 0.029.
Values may be sent and summed in bfloat16 or wider, within the bound.
No kernel may reach another device: no remote copies, remote signals or barrier semaphores. Data moves between devices by JAX's collectives and lax.ppermute only.
A program may use at most 128 MiB of HBM per device.

v0:
```python
import math

import jax
import jax.numpy as jnp
from jax import lax
from jax.sharding import PartitionSpec as P

SOFT_CAP = 30.0
LOSS_SCALE = 64.0


def inside_mask(latent, exponent):
    quant_step = jnp.exp2(exponent.astype(jnp.float32))
    levels = jnp.floor(latent.astype(jnp.float32) / quant_step + 0.5)
    return (jnp.abs(levels) <= 127.0).astype(jnp.float32)


def allowed_pairs(length_row, token_inputs):
    doc_ends = jnp.cumsum(length_row)
    position = jnp.arange(token_inputs, dtype=jnp.int32)
    segment = jnp.sum((position[:, None] >= doc_ends[None, :]).astype(jnp.int32), axis=1)
    return (segment[:, None] == segment[None, :]) & (position[None, :] <= position[:, None])


def softmax_with_mask(logits, attend_mask):
    weights = jnp.where(attend_mask, jnp.exp(logits), 0.0)
    return weights / jnp.sum(weights, axis=-1, keepdims=True)


def joined_grads(
    query_token_rows, key_token_rows, teacher_token_rows, length_row, head_count, head_size
):
    token_inputs = query_token_rows.shape[0]
    query_head_split = query_token_rows.reshape(token_inputs, head_count, head_size)
    scores = jnp.einsum(
        "tnd,sd->nts", query_head_split, key_token_rows, preferred_element_type=jnp.float32
    ) / math.sqrt(head_size)
    capped = SOFT_CAP * jnp.tanh(scores / SOFT_CAP)
    attend_mask = allowed_pairs(length_row, token_inputs)
    student = softmax_with_mask(capped, attend_mask)
    teacher_probs = softmax_with_mask(teacher_token_rows.astype(jnp.float32), attend_mask)
    slope = 1.0 - (capped / SOFT_CAP) ** 2
    logit_gradient = (
        (student - teacher_probs) * slope * (LOSS_SCALE / math.sqrt(head_size))
    ).astype(jnp.bfloat16)
    query_grad = jnp.einsum(
        "nts,sd->tnd", logit_gradient, key_token_rows, preferred_element_type=jnp.float32
    )
    query_grad = query_grad.reshape(token_inputs, head_count * head_size).astype(jnp.bfloat16)
    key_gradient = jnp.einsum(
        "nts,tnd->sd", logit_gradient, query_head_split, preferred_element_type=jnp.float32
    ).astype(jnp.bfloat16)
    return jnp.concatenate([query_grad, key_gradient], axis=1)


def on_device(
    activations,
    w_query,
    key_weight_latent,
    query_exponent,
    key_column_exponent,
    queries,
    keys,
    teacher_attention_logits,
    document_length,
):
    query_inside = inside_mask(w_query, query_exponent[None, :])
    key_inside = inside_mask(key_weight_latent, key_column_exponent[None, :])
    query_width = w_query.shape[1]
    head_size = key_weight_latent.shape[1]
    head_count = query_width // head_size
    group_count = activations.shape[0]
    model_width = activations.shape[2]
    joined_list = []
    for member in range(group_count):
        joined_list.append(
            joined_grads(
                queries[member],
                keys[member],
                teacher_attention_logits[member],
                document_length[member],
                head_count,
                head_size,
            )
        )
    joined_stack = jnp.stack(joined_list, axis=0)
    token_inputs = joined_stack.shape[1]
    joined_width = joined_stack.shape[2]
    whole_rows = lax.all_gather(activations, "tensor", axis=1, tiled=True)
    whole_flat = whole_rows.reshape(group_count * token_inputs, model_width)
    joined_flat = joined_stack.reshape(group_count * token_inputs, joined_width)
    weight_total = lax.psum_scatter(
        lax.dot_general(
            whole_flat, joined_flat, (((0,), (0,)), ((), ())), preferred_element_type=jnp.float32
        ).astype(jnp.bfloat16),
        "dp",
        scatter_dimension=0,
        tiled=True,
    ).astype(jnp.float32)
    grad_query = query_inside * weight_total[:, :query_width] / LOSS_SCALE
    grad_key = key_inside * weight_total[:, query_width:] / LOSS_SCALE
    return (grad_query, grad_key)


def solution(mesh):
    in_specs = (
        P("dp", "tensor", None),
        P("dp", "tensor"),
        P("dp", "tensor"),
        P("tensor"),
        P("tensor"),
        P("dp", None, "tensor"),
        P("dp", None, "tensor"),
        P("dp", "tensor", None, None),
        P("dp", None),
    )
    out_specs = (P("dp", "tensor"), P("dp", "tensor"))
    return jax.shard_map(
        on_device, mesh=mesh, in_specs=in_specs, out_specs=out_specs, check_vma=False
    )
```

profile of v0, /device:TPU:8, one launch (start us, length us, event | category | flops | bytes accessed | tf_op | source)
XLA Modules:
  0.0 407.2 jit_solution(4015036117641982259)
XLA Ops:
  7.2 0.7 all-gather.2.cloned.1.call-update
  7.9 5.8 %fusion.73 = (bf16[1,6,512,512]{3,2,1,0:T(8,128)(2,1)}, bf16[1,6,512,512]{3,2,1,0:T(8,128)(2,1)}) fusion(bf16[2,6,512,512]{3,2,1,0:T(8,128)(2,1)} %param.16), kind=kLoop, calls=%fused_computation.87 | loop fusion | bytes 12582912 | tf_op jit(solution)/shard_map/slice | solution.py:80
  13.8 3.2 copy.48
  17.0 5.4 %copy.47 = bf16[1,6,512,512]{2,3,1,0:T(8,128)(2,1)} copy(bf16[1,6,512,512]{3,2,1,0:T(8,128)(2,1)} %get-tuple-element.8) | data formatting | bytes 6291456
  22.5 0.2 reduce-window.17
  22.7 0.2 reduce-window.16
  22.8 0.1 convert_reduce_fusion
  22.9 0.1 convert_reduce_fusion.1
  23.0 0.2 fusion.30
  23.2 0.2 fusion.31
  23.4 2.3 fusion.74
  25.8 5.1 %fusion = f32[6,512,512]{1,2,0:T(8,128)} fusion(bf16[1,6,512,512]{2,3,1,0:T(8,128)(2,1)S(1)} %copy.48, pred[512,512]{0,1:T(8,128)(4,1)S(1)} %fusion.30), kind=kOutput, calls=%fused_computation | output fusion | flops 3149311 | bytes 9699328 | tf_op jit(solution)/shard_map/div | solution.py:27
  30.8 9.9 %fusion.6 = bf16[6,512,512]{1,2,0:T(8,128)(2,1)S(1)} fusion(f32[6,512,512]{1,2,0:T(8,128)} %fusion, bf16[1,6,512,512]{2,3,1,0:T(8,128)(2,1)} %copy-done.1, pred[512,512]{0,1:T(8,128)(4,1)} %copy-done.3, bf16[512,6,96]{0,2,1:T(8,128)(2,1)} %bitcast.114, bf16[2,512,96]{1,2,0:T(8,128)(2,1)} %param.15), kind=kOutput, calls=%fused_computation.8 | convolution fusion | flops 626003456 | bytes 14483456 | tf_op jit(solution)/shard_map/div | solution.py:27
  40.8 2.3 fusion.29
  43.0 2.3 convolution_convert_fusion
  45.4 4.6 %fusion.2 = f32[6,512,512]{1,2,0:T(8,128)} fusion(bf16[1,6,512,512]{2,3,1,0:T(8,128)(2,1)S(1)} %copy-done, pred[512,512]{0,1:T(8,128)(4,1)S(1)} %fusion.31), kind=kOutput, calls=%fused_computation.2 | output fusion | flops 3149311 | bytes 9699328 | tf_op jit(solution)/shard_map/div | solution.py:27
  50.0 9.9 %fusion.8 = bf16[6,512,512]{1,2,0:T(8,128)(2,1)S(1)} fusion(f32[6,512,512]{1,2,0:T(8,128)} %fusion.2, bf16[1,6,512,512]{2,3,1,0:T(8,128)(2,1)} %copy.47, pred[512,512]{0,1:T(8,128)(4,1)S(1)} %fusion.31, bf16[512,6,96]{0,2,1:T(8,128)(2,1)} %bitcast.112, bf16[2,512,96]{1,2,0:T(8,128)(2,1)} %param.15), kind=kOutput, calls=%fused_computation.13 | convolution fusion | flops 626003456 | bytes 14483456 | tf_op jit(solution)/shard_map/div | solution.py:27
  60.0 2.2 fusion.28
  62.2 1.5 convolution_convert_fusion.1
  63.7 0.1 maximum_bitcast_fusion
  63.8 155.2 %all-gather.2.cloned.1.call-done = bf16[2,512,9216]{2,1,0:T(8,128)(2,1)} async-done(((bf16[2,64,9216]{2,1,0:T(8,128)(2,1)}), bf16[2,512,9216]{2,1,0:T(8,128)(2,1)}) %all-gather.2.cloned.1.call-update) | async-done | bytes 18874384 | tf_op jit(solution)/shard_map/all_gather | solution.py:89
  219.0 21.7 %fusion.4 = bf16[9216,672]{0,1:T(8,128)(2,1)} fusion(bf16[2,512,9216]{2,1,0:T(8,128)(2,1)} %all-gather.2.cloned.1.call-done, bf16[1,512,672]{1,2,0:T(8,128)(2,1)S(1)} %get-tuple-element.15, bf16[1,512,672]{1,2,0:T(8,128)(2,1)S(1)} %get-tuple-element.14), kind=kOutput, calls=%fused_computation.5 | convolution fusion | flops 12690456576 | bytes 32636928 | tf_op jit(solution)/shard_map/dot_general | solution.py:93
  240.7 17.0 %copy.45 = bf16[9216,672]{1,0:T(8,128)(2,1)} copy(bf16[9216,672]{0,1:T(8,128)(2,1)} %fusion.4) | data formatting | bytes 24772608
  257.7 0.9 copy-done.4
  258.7 0.2 copy.31
  258.9 0.1 copy.38
  259.1 137.5 %reduce-scatter.4.cloned.1.call-done = bf16[288,672]{1,0:T(8,128)(2,1)} async-done(((bf16[9216,672]{1,0:T(8,128)(2,1)}), bf16[288,672]{1,0:T(8,128)(2,1)}) %reduce-scatter.4.cloned.1.call-update) | async-done | bytes 387088
  396.6 1.3 copy.46
  398.0 0.3 fusion.32
  398.3 1.2 copy.39
  399.5 0.1 fusion.37
  399.6 0.8 copy.40
  (24 shorter events, 0.2 us)
Async XLA Ops:
  7.2 211.9 %all-gather.2.cloned.1.call-start = ((), (), s32[]{:S(2)}) async-start(), calls=%async_computation.1 | async-start | bytes 21233664 | tf_op jit(solution)/shard_map/all_gather | solution.py:89
  7.9 388.7 %reduce-scatter.4.cloned.1.call-start = ((), (), s32[]{:S(2)}) async-start(), calls=%async_computation.2 | async-start | bytes 14598144
  13.8 8.7 %copy-start.7 = (s32[2,4]{1,0:T(2,128)S(1)}, s32[2,4]{1,0:T(2,128)}, u32[]{:S(2)}) copy-start(s32[2,4]{1,0:T(2,128)} %param.17) | copy-start | bytes 100
  17.0 13.8 %copy-start.1 = (bf16[1,6,512,512]{2,3,1,0:T(8,128)(2,1)}, bf16[1,6,512,512]{2,3,1,0:T(8,128)(2,1)S(1)}, u32[]{:S(2)}) copy-start(bf16[1,6,512,512]{2,3,1,0:T(8,128)(2,1)S(1)} %copy.48) | copy-start | bytes 9437188
  23.2 7.6 %copy-start.3 = (pred[512,512]{0,1:T(8,128)(4,1)}, pred[512,512]{0,1:T(8,128)(4,1)S(1)}, u32[]{:S(2)}) copy-start(pred[512,512]{0,1:T(8,128)(4,1)S(1)} %fusion.30) | copy-start | bytes 786436
  40.7 4.7 %copy-start = (bf16[1,6,512,512]{2,3,1,0:T(8,128)(2,1)S(1)}, bf16[1,6,512,512]{2,3,1,0:T(8,128)(2,1)}, u32[]{:S(2)}) copy-start(bf16[1,6,512,512]{2,3,1,0:T(8,128)(2,1)} %copy.47) | copy-start | bytes 9437188
  60.0 3.7 copy-start.2
  257.7 1.0 copy-start.4
  257.7 1.2 copy-start.5
  257.7 1.4 copy-start.8
  257.7 1.4 copy-start.6
Sparse Core Ops, SparseCore 0:
  10.6 208.3 all-gather.1
  257.9 138.7 reduce-scatter.3
where the time goes:
time: 408 us; the launch traced here: 407 us
  waiting for transfers between devices  293 us (72%)
  matrix products  49.9 us (12%)
  local copies, waits for them, and re-layouts  38.4 us (9%)
  between operations  14.2 us (3%)
  other arithmetic  11.2 us (3%)
    all_gather x1, waiting for transfers between devices, on_device(): whole_rows = lax.all_gather(activations, 'tensor', axis=1, tiled=True)  155 us
    unnamed x3, waiting for transfers between devices  138 us
    unnamed x26, local copies, waits for them, and re-layouts  30.2 us
    dot_general x1, matrix products, on_device(): lax.dot_general(whole_flat, joined_flat, (((0,), (0,)), ((), ())), prefer...  21.7 us
    div x2, matrix products, softmax_with_mask(): return weights / jnp.sum(weights, axis=-1, keepdims=True)  19.8 us
    div x2, other arithmetic, softmax_with_mask(): return weights / jnp.sum(weights, axis=-1, keepdims=True)  9.68 us
  transfers between devices with their start and end apart: 2, of which 2 were waited for; matrix products, arithmetic and copies ran while one was open for 14% of the time, Pallas kernels for 0%

commit v1 on v0

v1 whole, which is shorter than its diff:
```python
import functools
import math

import jax
import jax.numpy as jnp
from jax import lax
from jax.experimental import pallas as pl
from jax.experimental.pallas import tpu as pltpu
from jax.sharding import PartitionSpec as P

SOFT_CAP = 30.0
LOSS_SCALE = 64.0
GROUPS = 2
TOKENS = 512
HEADS = 6
DIM = 96
WIDTH = 672
ROWS = 72
RINGS = 8
BAND = 128
SHARDS = 8
SHARE = 64
NARROW = jnp.bfloat16
MIB = 1024 * 1024
PIECE = 2 * ROWS


def cost(time):
    return pl.CostEstimate(flops=1000, bytes_accessed=int(time * 3.5e6), transcendentals=0)


def spread_tokens(first, second):
    parts = []
    for shard in range(SHARDS):
        parts.append(first[:, shard * SHARE : (shard + 1) * SHARE])
        parts.append(second[:, shard * SHARE : (shard + 1) * SHARE])
    return jnp.concatenate(parts, axis=1).astype(NARROW)


def head_kernel(length_ref, query_ref, key_ref, teacher_ref, *refs):
    out_ref, grad_ref, query_acc, key_acc = refs[-4:]
    head = pl.program_id(0)
    group = pl.program_id(1)

    @pl.when((head == 0) & (group == 0))
    def _():
        grad_ref[...] = jnp.zeros_like(grad_ref)

    ends = [length_ref[group, 0]]
    for document in range(1, length_ref.shape[1]):
        ends.append(ends[-1] + length_ref[group, document])
    query_t = query_ref[0]
    key_t = key_ref[0]
    for first in range(0, TOKENS, BAND):
        low = max(0, first - 2 * BAND)
        high = first + BAND
        token = lax.broadcasted_iota(jnp.int32, (BAND, 1), 0) + first
        start = jnp.zeros_like(token)
        for end in ends:
            start = jnp.where(token >= end, end, start)
        column = lax.broadcasted_iota(jnp.int32, (BAND, high - low), 1) + low
        allowed = (column >= start) & (column <= token)
        dots = lax.dot_general(
            query_t[:, first : first + BAND],
            key_t[:, low:high],
            (((0,), (0,)), ((), ())),
            preferred_element_type=jnp.float32,
        )
        bent = jnp.tanh(dots * (1.0 / (math.sqrt(DIM) * SOFT_CAP)))
        student = jnp.where(allowed, jnp.exp(bent * SOFT_CAP), 0.0)
        logits = teacher_ref[0, 0, first : first + BAND, low:high].astype(jnp.float32)
        teacher = jnp.where(allowed, jnp.exp(logits), 0.0)
        student_scale = 1.0 / jnp.sum(student, axis=1, keepdims=True)
        teacher_scale = 1.0 / jnp.sum(teacher, axis=1, keepdims=True)
        scale = LOSS_SCALE / math.sqrt(DIM)
        slope = scale - scale * (bent * bent)
        grad = (student * student_scale - teacher * teacher_scale) * slope
        grad_ref[first : first + BAND, low:high] = grad.astype(NARROW)
    score_grad = grad_ref[...]
    query_grad = lax.dot_general(
        key_t, score_grad, (((1,), (1,)), ((), ())), preferred_element_type=jnp.float32
    )
    key_grad = lax.dot_general(
        query_t, score_grad, (((1,), (0,)), ((), ())), preferred_element_type=jnp.float32
    )

    @pl.when(head == 0)
    def _():
        key_acc[group] = key_grad

    @pl.when(head != 0)
    def _():
        key_acc[group] = key_acc[group] + key_grad

    @pl.when(group == 0)
    def _():
        query_acc[...] = query_grad

    @pl.when(group == GROUPS - 1)
    def _():
        out_ref[head] = spread_tokens(query_acc[...], query_grad)

    @pl.when((head == HEADS - 1) & (group == GROUPS - 1))
    def _():
        out_ref[HEADS] = spread_tokens(key_acc[0], key_acc[1])


def head_grads(queries, keys, teacher, lengths, after):
    query_t = jnp.swapaxes(queries, 1, 2)
    key_t = jnp.swapaxes(keys, 1, 2)
    shape = (HEADS + 1, DIM, GROUPS * TOKENS)
    out = pl.pallas_call(
        head_kernel,
        out_shape=jax.ShapeDtypeStruct(shape, NARROW),
        grid=(HEADS, GROUPS),
        in_specs=[
            pl.BlockSpec(memory_space=pltpu.SMEM),
            pl.BlockSpec((1, DIM, TOKENS), lambda h, g: (g, h, 0)),
            pl.BlockSpec((1, DIM, TOKENS), lambda h, g: (g, 0, 0)),
            pl.BlockSpec((1, 1, TOKENS, TOKENS), lambda h, g: (g, h, 0, 0)),
        ]
        + [pl.BlockSpec(memory_space=pl.ANY)] * len(after),
        out_specs=pl.BlockSpec(shape, lambda h, g: (0, 0, 0)),
        scratch_shapes=[
            pltpu.VMEM((TOKENS, TOKENS), NARROW),
            pltpu.VMEM((DIM, TOKENS), jnp.float32),
            pltpu.VMEM((GROUPS, DIM, TOKENS), jnp.float32),
        ],
        compiler_params=pltpu.CompilerParams(vmem_limit_bytes=12 * MIB),
        cost_estimate=cost(14),
        name="head_grads",
    )(lengths, query_t, key_t, teacher, *after)
    return out.reshape(WIDTH, GROUPS * TOKENS)


def turn_kernel(place_ref, near_ref, far_ref, *refs):
    turned = refs[4]
    mine = place_ref[0]
    core = place_ref[2]
    lanes = near_ref.shape[2]
    for line, act_ref in enumerate((near_ref, far_ref)):
        block = act_ref[...].reshape(GROUPS * SHARE, lanes).astype(jnp.float32)
        turned[line * lanes : (line + 1) * lanes, :] = block.T
    for ahead in range(4):
        owner = lax.rem(mine + ahead, 4)
        for other in range(2):
            target = core + other - 2 * core * other
            for ring in range(2):
                halves = []
                for line in range(2):
                    start = line * lanes + (ring * 2 + target) * 4 * ROWS + owner * ROWS
                    halves.append(turned[pl.ds(pl.multiple_of(start, 8), ROWS), :])
                refs[ahead][other, ring * PIECE : (ring + 1) * PIECE, :] = jnp.concatenate(halves, axis=0).astype(NARROW)


def turn(place, activations):
    tokens = GROUPS * SHARE
    lanes = 16 * ROWS
    shape = jax.ShapeDtypeStruct((2, RINGS * PIECE, tokens), NARROW)
    return pl.pallas_call(
        turn_kernel,
        out_shape=(shape,) * 4,
        grid=(RINGS // 2,),
        in_specs=[
            pl.BlockSpec(memory_space=pltpu.SMEM),
            pl.BlockSpec((GROUPS, SHARE, lanes), lambda i: (0, 0, i)),
            pl.BlockSpec((GROUPS, SHARE, lanes), lambda i: (0, 0, i + RINGS // 2)),
        ],
        out_specs=(pl.BlockSpec((2, 2 * PIECE, tokens), lambda i: (0, i, 0)),) * 4,
        scratch_shapes=[pltpu.VMEM((2 * lanes, tokens), jnp.float32)],
        compiler_params=pltpu.CompilerParams(vmem_limit_bytes=10 * MIB),
        cost_estimate=cost(3),
        name="turn",
    )(place, activations, activations)


def join_factors(factors, joined):
    @pl.when(pl.program_id(0) == 0)
    def _():
        row = 0
        for factor in factors:
            joined[row : row + factor.shape[0], :] = factor[...]
            row += factor.shape[0]
        if row < joined.shape[0]:
            joined[row:, :] = jnp.zeros((joined.shape[0] - row, joined.shape[1]), NARROW)


def multiply(rows, joined):
    return lax.dot_general(
        rows, joined[...], (((1,), (1,)), ((), ())), preferred_element_type=jnp.float32
    ).astype(NARROW)


def first_kernel(count, place_ref, *refs):
    pieces = refs[:8]
    out_ref, whole_ref, joined = refs[9 + count :]
    join_factors(refs[8 : 8 + count], joined)
    for behind in range(4):
        for across in range(2):
            source = lax.rem(place_ref[0] + 4 - behind, 4) * 2 + lax.rem(place_ref[1] + across, 2)
            lane = pl.multiple_of(source * 128, 128)
            whole_ref[:, pl.ds(lane, 128)] = pieces[behind * 2 + across][0]
    out_ref[...] = multiply(whole_ref[...], joined)


def next_kernel(count, whole_ref, *refs):
    out_ref, joined = refs[1 + count :]
    join_factors(refs[:count], joined)
    out_ref[...] = multiply(whole_ref[...], joined)


TERM_ROWS = 384


def term_call(kernel, count, rows, width, out_shape, out_specs, in_specs, operands):
    return pl.pallas_call(
        functools.partial(kernel, count),
        out_shape=out_shape,
        grid=(rows // TERM_ROWS,),
        in_specs=in_specs,
        out_specs=out_specs,
        scratch_shapes=[pltpu.VMEM((width, GROUPS * TOKENS), NARROW)],
        compiler_params=pltpu.CompilerParams(vmem_limit_bytes=18 * MIB),
        cost_estimate=cost(6),
        name="terms",
    )(*operands)


def factor_specs(factors):
    return [pl.BlockSpec(factor.shape, lambda i: (0, 0)) for factor in factors] + [pl.BlockSpec(memory_space=pl.ANY)]


def padded_width(factors):
    return -(-sum(factor.shape[0] for factor in factors) // 128) * 128


def first_terms(place, other, pieces, factors, after):
    tokens = GROUPS * TOKENS
    rows = RINGS * PIECE
    width = padded_width(factors)
    return term_call(
        first_kernel,
        len(factors),
        rows,
        width,
        (jax.ShapeDtypeStruct((rows, width), NARROW), jax.ShapeDtypeStruct((rows, tokens), NARROW)),
        (pl.BlockSpec((TERM_ROWS, width), lambda i: (i, 0)), pl.BlockSpec((TERM_ROWS, tokens), lambda i: (i, 0))),
        [pl.BlockSpec(memory_space=pltpu.SMEM)]
        + [pl.BlockSpec((1, TERM_ROWS, GROUPS * SHARE), lambda i: (other, i, 0))] * 8
        + factor_specs(factors),
        (place, *pieces, *factors, after),
    )


def next_terms(whole, factors, after):
    rows, tokens = whole.shape
    width = padded_width(factors)
    return term_call(
        next_kernel,
        len(factors),
        rows,
        width,
        jax.ShapeDtypeStruct((rows, width), NARROW),
        pl.BlockSpec((TERM_ROWS, width), lambda i: (i, 0)),
        [pl.BlockSpec((TERM_ROWS, tokens), lambda i: (i, 0))] + factor_specs(factors),
        (whole, *factors, after),
    )


def finish_kernel(place_ref, mask_ref, key_mask_ref, *refs):
    blocks = refs[:4]
    out_ref, key_out_ref = refs[4:]
    query_width = out_ref.shape[1]
    for behind in range(4):
        owner = lax.rem(place_ref[0] + behind, 4)
        rows = pl.ds(pl.multiple_of(owner * ROWS, 8), ROWS)
        total = blocks[behind][...].astype(jnp.float32) * (1.0 / LOSS_SCALE)
        out_ref[rows, :] = total[:, :query_width] * mask_ref[rows, :]
        key_out_ref[rows, :] = total[:, query_width:] * key_mask_ref[rows, :]


def finish(place, mask, key_mask, blocks):
    vmem = pl.BlockSpec(memory_space=pltpu.VMEM)
    return pl.pallas_call(
        finish_kernel,
        out_shape=(
            jax.ShapeDtypeStruct(mask.shape, jnp.float32),
            jax.ShapeDtypeStruct(key_mask.shape, jnp.float32),
        ),
        in_specs=[pl.BlockSpec(memory_space=pltpu.SMEM)] + [vmem] * 6,
        out_specs=(vmem, vmem),
        compiler_params=pltpu.CompilerParams(vmem_limit_bytes=10 * MIB),
        cost_estimate=cost(2),
        name="finish",
    )(place, mask, key_mask, *blocks)


def gate_kernel(x_ref, *refs):
    pass


def gate(x, after):
    anywhere = pl.BlockSpec(memory_space=pl.ANY)
    return pl.pallas_call(
        gate_kernel,
        out_shape=jax.ShapeDtypeStruct(x.shape, x.dtype),
        in_specs=[anywhere] * (1 + len(after)),
        out_specs=anywhere,
        input_output_aliases={0: 0},
        compiler_params=pltpu.CompilerParams(vmem_limit_bytes=MIB),
        cost_estimate=cost(0.1),
        name="gate",
    )(x, *after)


def inside_mask(latent, exponent):
    quant_step = jnp.exp2(exponent.astype(jnp.float32))
    levels = jnp.floor(latent.astype(jnp.float32) / quant_step + 0.5)
    return (jnp.abs(levels) <= 127.0).astype(jnp.float32)


def shifted(x, axis, size, by):
    return lax.ppermute(x, axis, [(at, (at + by) % size) for at in range(size)])


def load_kernel(streams, spot_ref, *refs):
    outs = refs[3 * streams :]
    for at, out_ref in enumerate(outs):
        parts = refs[3 * at : 3 * at + 3]
        total = parts[0][...].astype(jnp.float32) + parts[1][...].astype(jnp.float32)
        if len(parts[2].shape) == 2:
            total = total + parts[2][...].astype(jnp.float32)
        out_ref[...] = total.astype(NARROW)


def loads(spots, keep, got, moving):
    streams = len(moving)
    width = keep.shape[1]

    def local_spec(at):
        return pl.BlockSpec((PIECE, width), lambda i, spot: (spot[at], 0))

    whole = pl.BlockSpec((PIECE, width), lambda i, spot: (0, 0))
    in_specs = []
    operands = []
    for at, there in enumerate(moving):
        in_specs += [local_spec(at), local_spec(at)]
        operands += [keep, got]
        if there is None:
            in_specs.append(pl.BlockSpec(memory_space=pltpu.SMEM))
            operands.append(spots)
        else:
            in_specs.append(whole)
            operands.append(there)
    shape = jax.ShapeDtypeStruct((PIECE, width), NARROW)
    return pl.pallas_call(
        functools.partial(load_kernel, streams),
        out_shape=(shape,) * streams,
        grid_spec=pltpu.PrefetchScalarGridSpec(
            num_scalar_prefetch=1, grid=(1,), in_specs=in_specs, out_specs=(whole,) * streams
        ),
        compiler_params=pltpu.CompilerParams(vmem_limit_bytes=10 * MIB),
        cost_estimate=cost(2),
        name="loads",
    )(spots, *operands)


def settle_kernel(spot_ref, keep_ref, got_ref, one_ref, two_ref, mine_ref, other_ref, total):
    total[...] = (
        keep_ref[...].astype(jnp.float32)
        + got_ref[...].astype(jnp.float32)
        + one_ref[...].astype(jnp.float32)
        + two_ref[...].astype(jnp.float32)
    )
    line = spot_ref[1]
    mine_ref[...] = total[pl.ds(pl.multiple_of(line * ROWS, 8), ROWS), :].astype(NARROW)
    other_ref[...] = total[pl.ds(pl.multiple_of((1 - line) * ROWS, 8), ROWS), :].astype(NARROW)


def settle(spots, keep, got, one, two):
    width = keep.shape[1]
    local = pl.BlockSpec((PIECE, width), lambda i, spot: (spot[0], 0))
    whole = pl.BlockSpec((PIECE, width), lambda i, spot: (0, 0))
    out = pl.BlockSpec((ROWS, width), lambda i, spot: (0, 0))
    shape = jax.ShapeDtypeStruct((ROWS, width), NARROW)
    return pl.pallas_call(
        settle_kernel,
        out_shape=(shape, shape),
        grid_spec=pltpu.PrefetchScalarGridSpec(
            num_scalar_prefetch=1,
            grid=(1,),
            in_specs=[local, local, whole, whole],
            out_specs=(out, out),
            scratch_shapes=[pltpu.VMEM((PIECE, width), jnp.float32)],
        ),
        compiler_params=pltpu.CompilerParams(vmem_limit_bytes=10 * MIB),
        cost_estimate=cost(2),
        name="settle",
    )(spots, keep, got, one, two)


def merge_kernel(mine_ref, got_ref, *outs):
    total = mine_ref[...].astype(jnp.float32) + got_ref[...].astype(jnp.float32)
    for at, out_ref in enumerate(outs):
        out_ref[...] = total[:, at * WIDTH : (at + 1) * WIDTH].astype(NARROW)


def merge(mine, got):
    vmem = pl.BlockSpec(memory_space=pltpu.VMEM)
    count = mine.shape[1] // WIDTH
    return pl.pallas_call(
        merge_kernel,
        out_shape=(jax.ShapeDtypeStruct((ROWS, WIDTH), NARROW),) * count,
        in_specs=[vmem, vmem],
        out_specs=(vmem,) * count,
        compiler_params=pltpu.CompilerParams(vmem_limit_bytes=10 * MIB),
        cost_estimate=cost(1),
        name="merge",
    )(mine, got)


CHUNKS = ((0, 1), (3, 2))


def on_device(
    activations,
    w_query,
    key_weight_latent,
    query_exponent,
    key_column_exponent,
    queries,
    keys,
    teacher_attention_logits,
    document_length,
):
    place = jnp.stack([lax.axis_index("y"), lax.axis_index("xh"), lax.axis_index("core")]).astype(jnp.int32)
    ring = lax.axis_index("z")
    line = lax.axis_index("xl")
    cut = turn(place, activations)
    held = [cut[0]] + [shifted(cut[ahead], "y", 4, ahead) for ahead in (1, 2, 3)]
    swapped = [shifted(cut[0], "xh", 2, 1)]
    own = head_grads(queries, keys, teacher_attention_logits, document_length, [cut[0]])
    own = gate(own, held[1:] + swapped)
    swapped += [shifted(piece, "xh", 2, 1) for piece in held[1:]]
    pieces = []
    for pair in zip(held, swapped):
        pieces += pair
    back = shifted(own, "y", 4, 1)
    fore = shifted(own, "y", 4, 3)
    half = WIDTH // 2
    factors = [
        [own],
        [back],
        [shifted(back[:half], "y", 4, 1), shifted(fore[half:], "y", 4, 3)],
        [fore],
    ]

    mask = inside_mask(w_query, query_exponent[None, :])
    key_mask = inside_mask(key_weight_latent, key_column_exponent[None, :])

    held_terms = []
    after = place
    wholes = []
    for at, chunk in enumerate(CHUNKS):
        parts = []
        for behind in chunk:
            parts += factors[behind]
        made = []
        for other in (1, 0):
            if at == 0:
                after, whole = first_terms(place, other, pieces, parts, after)
                wholes.append(whole)
            else:
                after = next_terms(wholes[1 - other], parts, after)
            made.append(after)
        held_terms.append((made[1], shifted(made[0], "core", 2, 1)))

    def spots(*values):
        return jnp.stack([lax.rem(value + RINGS, RINGS) for value in values]).astype(jnp.int32)

    moving = [[None, None], [None, None]]
    for slot in range(4):
        for at, (keep, got) in enumerate(held_terms):
            way = 1 - 2 * at
            if slot == 0:
                (first,) = loads(spots(ring + 4 * way), keep, got, [None])
                moving[at][0] = shifted(first, "z", RINGS, way)
            else:
                left = 4 - slot
                pair = loads(spots(ring + left * way, ring - left * way), keep, got, moving[at])
                moving[at] = [shifted(pair[0], "z", RINGS, way), shifted(pair[1], "z", RINGS, -way)]
    blocks = {}
    for at, (keep, got) in enumerate(held_terms):
        mine, other = settle(jnp.stack([ring, line]).astype(jnp.int32), keep, got, *moving[at])
        parts = merge(mine, shifted(other, "xl", 2, 1))
        for behind, part in zip(CHUNKS[at], parts):
            blocks[behind] = part if behind == 0 else shifted(part, "y", 4, 4 - behind)
    return finish(place, mask, key_mask, [blocks[behind] for behind in range(4)])


def solution(mesh):
    fine = jax.sharding.Mesh(mesh.devices.reshape(2, 8, 2, 4, 2), ("xl", "z", "core", "y", "xh"))
    dp = ("xl", "z", "core")
    tensor = ("y", "xh")
    in_specs = (
        P(dp, tensor, None),
        P(dp, tensor),
        P(dp, tensor),
        P(tensor),
        P(tensor),
        P(dp, None, tensor),
        P(dp, None, tensor),
        P(dp, tensor, None, None),
        P(dp, None),
    )
    out_specs = (P(dp, tensor), P(dp, tensor))
    return jax.shard_map(on_device, mesh=fine, in_specs=in_specs, out_specs=out_specs, check_vma=False)
```

time: 408 us -> 201 us (0.49)
  waiting for transfers between devices: 293 us -> 70.6 us
  Pallas kernels: 0 us -> 66.3 us
  matrix products: 49.9 us -> 0 us
  starting transfers between devices: 0.08 us -> 47.8 us
  local copies, waits for them, and re-layouts: 38.4 us -> 11.2 us
  between operations: 14.2 us -> 0.88 us
  other arithmetic: 11.2 us -> 1.81 us
    all_gather x1 -> x0, waiting for transfers between devices: 155 us -> none  [on_device(): whole_rows = lax.all_gather(activations, 'tensor', axis=1, tiled=True)]
    unnamed x3 -> x0, waiting for transfers between devices: 138 us -> none
    ppermute x0 -> x32, waiting for transfers between devices: none -> 70.6 us  [shifted(): return lax.ppermute(x, axis, [(at, (at + by) % size) for at in range(size)])]
    pallas_call x0 -> x20, Pallas kernels: none -> 66.3 us  [the longest x4 22.2 us: term_call(): pl.pallas_call(functools.partial(kernel, count), out_shape=out_shape, gri...]
    ppermute x0 -> x32, starting transfers between devices: none -> 47.8 us  [shifted(): return lax.ppermute(x, axis, [(at, (at + by) % size) for at in range(size)])]
    dot_general x5 -> x0, matrix products: 30 us -> none  [the longest x1 21.7 us: on_device(): lax.dot_general(whole_flat, joined_flat, (((0,), (0,)), ((), ())), prefer...]
    div x2 -> x0, matrix products: 19.8 us -> none  [softmax_with_mask(): return weights / jnp.sum(weights, axis=-1, keepdims=True)]
    unnamed x26 -> x42, local copies, waits for them, and re-layouts: 30.2 us -> 11.1 us
  transfers between devices with their start and end apart: 2 -> 32, of which waited for: 2 -> 16; matrix products, arithmetic and copies ran while one was open for 14% -> 1% of each run, Pallas kernels for 0% -> 31%
where the time goes in v1:
time: 201 us; the launch traced here: 199 us
  waiting for transfers between devices  70.6 us (35%)
  Pallas kernels  66.3 us (33%)
  starting transfers between devices  47.8 us (24%)
  local copies, waits for them, and re-layouts  11.2 us (6%)
    ppermute x32, waiting for transfers between devices, shifted(): return lax.ppermute(x, axis, [(at, (at + by) % size) for at in range(size)])  70.6 us
    ppermute x32, starting transfers between devices, shifted(): return lax.ppermute(x, axis, [(at, (at + by) % size) for at in range(size)])  47.8 us
    pallas_call x4, Pallas kernels, term_call(): pl.pallas_call(functools.partial(kernel, count), out_shape=out_shape, gri...  22.2 us
    pallas_call x8, Pallas kernels, loads(): pl.pallas_call(functools.partial(load_kernel, streams), out_shape=(shape,...  22.1 us
    pallas_call x1, Pallas kernels, head_grads(): pl.pallas_call(head_kernel, out_shape=jax.ShapeDtypeStruct(shape, NARROW)...  13.3 us
    unnamed x42, local copies, waits for them, and re-layouts  11.1 us
    pallas_call x2, Pallas kernels, settle(): pl.pallas_call(settle_kernel, out_shape=(shape, shape), grid_spec=pltpu.P...  4.57 us
  transfers between devices with their start and end apart: 32, of which 16 were waited for; matrix products, arithmetic and copies ran while one was open for 1% of the time, Pallas kernels for 31%

profile of v1, /device:TPU:8, one launch (start us, length us, event | category | flops | bytes accessed | tf_op | source)
XLA Modules:
  0.0 198.7 jit_solution(13836893548628006882)
XLA Ops:
  2.4 2.2 %turn.1 = (bf16[2,1152,128]{2,1,0:T(8,128)(2,1)S(1)}, bf16[2,1152,128]{2,1,0:T(8,128)(2,1)S(1)}, bf16[2,1152,128]{2,1,0:T(8,128)(2,1)S(1)}, bf16[2,1152,128]{2,1,0:T(8,128)(2,1)S(1)}) custom-call(s32[3]{0:T(128)S(1)} %pad_add_fusion.place_ref.refs_10_, bf16[2,64,9216]{2,1,0:T(8,128)(2,1)S(1)} %copy-done.5, bf16[2,64,9216]{2,1,0:T(8,128)(2,1)S(1)} %copy-done.5), custom_call_target="tpu_custom_call" | custom-call | flops 1000 | bytes 10500000 | tf_op jit(solution)/shard_map/turn/pallas_call | solution.py:160
  4.6 3.1 %collective-permute-start = (bf16[2,1152,128]{2,1,0:T(8,128)(2,1)S(1)}, bf16[2,1152,128]{2,1,0:T(8,128)(2,1)S(1)}, u32[]{:S(2)}, u32[]{:S(2)}) collective-permute-start(bf16[2,1152,128]{2,1,0:T(8,128)(2,1)S(1)} %get-tuple-element.30.refs_0_), channel_id=1, source_target_pairs={{0,1},{1,0},{2,3},{3,2},{4,5},{5,4},{6,7},{7,6},{8,9},{9,8},{10,11... | collective-permute-start | bytes 1769480 | tf_op jit(solution)/shard_map/ppermute | solution.py:323
  10.2 2.4 %collective-permute-start.5 = (bf16[2,1152,128]{2,1,0:T(8,128)(2,1)S(1)}, bf16[2,1152,128]{2,1,0:T(8,128)(2,1)S(1)}, u32[]{:S(2)}, u32[]{:S(2)}) collective-permute-start(bf16[2,1152,128]{2,1,0:T(8,128)(2,1)S(1)} %get-tuple-element.33), channel_id=1, source_target_pairs={{0,6},{2,0},{4,2},{6,4},{1,7},{3,1},{5,3},{7,5},{8,14},{10,8},{12,... | collective-permute-start | bytes 1769480 | tf_op jit(solution)/shard_map/ppermute | solution.py:323
  12.6 2.8 %copy-done.8 = bf16[2,6,512,512]{3,2,1,0:T(8,128)(2,1)S(1)} copy-done((bf16[2,6,512,512]{3,2,1,0:T(8,128)(2,1)S(1)}, bf16[2,6,512,512]{3,2,1,0:T(8,128)(2,1)}, u32[]{:S(2)}) %copy-start.8) | copy-done | bytes 6291480
  15.4 13.3 %head_grads.1 = bf16[7,96,1024]{2,1,0:T(8,128)(2,1)S(1)} custom-call(s32[2,4]{1,0:T(2,128)S(1)} %copy-done.17, bf16[2,576,512]{2,1,0:T(8,128)(2,1)S(1)} %bitcast.17, bf16[2,96,512]{2,1,0:T(8,128)(2,1)S(1)} %bitcast.18, bf16[2,6,512,512]{3,2,1,0:T(8,128)(2,1)S(1)} %copy-done.8, bf16[2,1152,128]{2,1,0:T(8,128)(2,1)S(1)} %get-tuple-element.30.refs_0_), custom_call_target="tpu_custom_call" | custom-call | flops 1000 | bytes 49000000 | tf_op jit(solution)/shard_map/head_grads/pallas_call | solution.py:112
  28.8 8.4 %collective-permute-done.5.refs_2_.refs_6_ = bf16[2,1152,128]{2,1,0:T(8,128)(2,1)S(1)} collective-permute-done((bf16[2,1152,128]{2,1,0:T(8,128)(2,1)S(1)}, bf16[2,1152,128]{2,1,0:T(8,128)(2,1)S(1)}, u32[]{:S(2)}, u32[]{:S(2)}) %collective-permute-start.5) | collective-permute-done | bytes 589856 | tf_op jit(solution)/shard_map/ppermute | solution.py:323
  39.7 3.0 %collective-permute-start.4 = (bf16[2,1152,128]{2,1,0:T(8,128)(2,1)S(1)}, bf16[2,1152,128]{2,1,0:T(8,128)(2,1)S(1)}, u32[]{:S(2)}, u32[]{:S(2)}) collective-permute-start(bf16[2,1152,128]{2,1,0:T(8,128)(2,1)S(1)} %collective-permute-done.3.refs_1_.refs_4_), channel_id=1, source_target_pairs={{0,1},{1,0},{2,3},{3,2},{4,5},{5,4},{6,7},{7,6},{8,9},{9,8},{10,11... | collective-permute-start | bytes 1769480 | tf_op jit(solution)/shard_map/ppermute | solution.py:323
  43.2 25.2 %collective-permute-done.7.refs_9_ = bf16[672,1024]{1,0:T(8,128)(2,1)S(1)} collective-permute-done((bf16[672,1024]{1,0:T(8,128)(2,1)S(1)}, bf16[672,1024]{1,0:T(8,128)(2,1)S(1)}, u32[]{:S(2)}, u32[]{:S(2)}) %collective-permute-start.7) | collective-permute-done | bytes 1376288 | tf_op jit(solution)/shard_map/ppermute | solution.py:323
  70.7 9.0 %collective-permute-done.6.refs_7_ = bf16[2,1152,128]{2,1,0:T(8,128)(2,1)S(1)} collective-permute-done((bf16[2,1152,128]{2,1,0:T(8,128)(2,1)S(1)}, bf16[2,1152,128]{2,1,0:T(8,128)(2,1)S(1)}, u32[]{:S(2)}, u32[]{:S(2)}) %collective-permute-start.6) | collective-permute-done | bytes 589856 | tf_op jit(solution)/shard_map/ppermute | solution.py:323
  79.8 6.6 %terms.4 = (bf16[1152,1408]{1,0:T(8,128)(2,1)}, bf16[1152,1024]{1,0:T(8,128)(2,1)S(1)}) custom-call(s32[3]{0:T(128)S(1)} %pad_add_fusion.place_ref.refs_10_, bf16[2,1152,128]{2,1,0:T(8,128)(2,1)S(1)} %get-tuple-element.30.refs_0_, bf16[2,1152,128]{2,1,0:T(8,128)(2,1)S(1)} %collective-permute-done.refs_3_.refs_1_, ...), custom_call_target="tpu_custom_call" | custom-call | flops 1000 | bytes 21000000 | tf_op jit(solution)/shard_map/terms/pallas_call | solution.py:216
  86.4 5.6 %terms.5 = (bf16[1152,1408]{1,0:T(8,128)(2,1)S(1)}, bf16[1152,1024]{1,0:T(8,128)(2,1)S(1)}) custom-call(s32[3]{0:T(128)S(1)} %pad_add_fusion.place_ref.refs_10_, bf16[2,1152,128]{2,1,0:T(8,128)(2,1)S(1)} %get-tuple-element.30.refs_0_, bf16[2,1152,128]{2,1,0:T(8,128)(2,1)S(1)} %collective-permute-done.refs_3_.refs_1_, ...), custom_call_target="tpu_custom_call" | custom-call | flops 1000 | bytes 21000000 | tf_op jit(solution)/shard_map/terms/pallas_call | solution.py:216
  93.4 5.6 %terms.6.refs_3_ = bf16[1152,1408]{1,0:T(8,128)(2,1)} custom-call(bf16[1152,1024]{1,0:T(8,128)(2,1)S(1)} %get-tuple-element.47.whole_ref, bf16[672,1024]{1,0:T(8,128)(2,1)S(1)} %collective-permute-done.18.refs_0_, bf16[336,1024]{1,0:T(8,128)(2,1)S(1)} %collective-permute-done.19.refs_1_, bf16[336,1024]{1,0:T(8,128)(2,1)S(1)} %collective-permute-done.20.refs_2_, ...), custom_call_target="tpu_custom_call" | custom-call | flops 1000 | bytes 21000000 | tf_op jit(solution)/shard_map/terms/pallas_call | solution.py:216
  108.5 4.5 %terms.7.refs_0_.refs_3_.keep_ref = bf16[1152,1408]{1,0:T(8,128)(2,1)S(1)} custom-call(bf16[1152,1024]{1,0:T(8,128)(2,1)S(1)} %copy-done.14, bf16[672,1024]{1,0:T(8,128)(2,1)S(1)} %copy-done.7, bf16[336,1024]{1,0:T(8,128)(2,1)S(1)} %copy-done.10, bf16[336,1024]{1,0:T(8,128)(2,1)S(1)} %copy-done.12, bf16[1152,1408]{1,0:T(8,128)(2,1)} %terms.6.refs_3_), custom_call_target="tpu_custom_call" | custom-call | flops 1000 | bytes 21000000 | tf_op jit(solution)/shard_map/terms/pallas_call | solution.py:216
  112.9 2.2 %loads.12 = bf16[144,1408]{1,0:T(8,128)(2,1)} custom-call(s32[1]{0:T(128)} %bitcast.15.spot_ref.refs_2_, bf16[1152,1408]{1,0:T(8,128)(2,1)S(1)} %terms.7.refs_0_.refs_3_.keep_ref, bf16[1152,1408]{1,0:T(8,128)(2,1)} %collective-permute-done.21.refs_1_.refs_4_.got_ref, s32[1]{0:T(128)} %bitcast.15.spot_ref.refs_2_), custom_call_target="tpu_custom_call" | custom-call | flops 1000 | bytes 7000000 | tf_op jit(solution)/shard_map/loads/pallas_call | solution.py:356
  115.1 3.9 %collective-permute-start.22 = (bf16[144,1408]{1,0:T(8,128)(2,1)}, bf16[144,1408]{1,0:T(8,128)(2,1)}, u32[]{:S(2)}, u32[]{:S(2)}) collective-permute-start(bf16[144,1408]{1,0:T(8,128)(2,1)} %loads.12), channel_id=1, source_target_pairs={{0,112},{16,0},{32,16},{48,32},{64,48},{80,64},{96,80},{112,96},{1... | collective-permute-start | bytes 1216520 | tf_op jit(solution)/shard_map/ppermute | solution.py:323
  119.1 3.1 %loads.9 = (bf16[144,1408]{1,0:T(8,128)(2,1)}, bf16[144,1408]{1,0:T(8,128)(2,1)}) custom-call(s32[2]{0:T(128)S(1)} %pad_add_fusion.4.spot_ref.refs_5_, bf16[1152,1408]{1,0:T(8,128)(2,1)S(1)} %get-tuple-element.35.refs_0_.refs_3_.keep_ref, bf16[1152,1408]{1,0:T(8,128)(2,1)} %collective-permute-done.8.refs_1_.refs_4_.got_ref, ...), custom_call_target="tpu_custom_call" | custom-call | flops 1000 | bytes 7000000 | tf_op jit(solution)/shard_map/loads/pallas_call | solution.py:356
  122.2 3.2 %collective-permute-start.11 = (bf16[144,1408]{1,0:T(8,128)(2,1)}, bf16[144,1408]{1,0:T(8,128)(2,1)}, u32[]{:S(2)}, u32[]{:S(2)}) collective-permute-start(bf16[144,1408]{1,0:T(8,128)(2,1)} %get-tuple-element.37), channel_id=1, source_target_pairs={{0,112},{16,0},{32,16},{48,32},{64,48},{80,64},{96,80},{112,96},{1... | collective-permute-start | bytes 1216520 | tf_op jit(solution)/shard_map/ppermute | solution.py:323
  125.6 3.6 %collective-permute-done.22.refs_2_ = bf16[144,1408]{1,0:T(8,128)(2,1)} collective-permute-done((bf16[144,1408]{1,0:T(8,128)(2,1)}, bf16[144,1408]{1,0:T(8,128)(2,1)}, u32[]{:S(2)}, u32[]{:S(2)}) %collective-permute-start.22) | collective-permute-done | bytes 405536 | tf_op jit(solution)/shard_map/ppermute | solution.py:323
  129.1 2.9 %loads.13 = (bf16[144,1408]{1,0:T(8,128)(2,1)}, bf16[144,1408]{1,0:T(8,128)(2,1)}) custom-call(s32[2]{0:T(128)S(1)} %pad_add_fusion.7.spot_ref.refs_5_, bf16[1152,1408]{1,0:T(8,128)(2,1)S(1)} %copy-done.1, bf16[1152,1408]{1,0:T(8,128)(2,1)} %collective-permute-done.21.refs_1_.refs_4_.got_ref, bf16[144,1408]{1,0:T(8,128)(2,1)} %collective-permute-done.22.refs_2_, ...), custom_call_target="tpu_custom_call" | custom-call | flops 1000 | bytes 7000000 | tf_op jit(solution)/shard_map/loads/pallas_call | solution.py:356
  132.1 3.7 %collective-permute-start.23 = (bf16[144,1408]{1,0:T(8,128)(2,1)}, bf16[144,1408]{1,0:T(8,128)(2,1)}, u32[]{:S(2)}, u32[]{:S(2)}) collective-permute-start(bf16[144,1408]{1,0:T(8,128)(2,1)} %get-tuple-element.48), channel_id=1, source_target_pairs={{0,112},{16,0},{32,16},{48,32},{64,48},{80,64},{96,80},{112,96},{1... | collective-permute-start | bytes 1216520 | tf_op jit(solution)/shard_map/ppermute | solution.py:323
  137.8 3.0 %loads.10 = (bf16[144,1408]{1,0:T(8,128)(2,1)}, bf16[144,1408]{1,0:T(8,128)(2,1)}) custom-call(s32[2]{0:T(128)S(1)} %pad_add_fusion.3.spot_ref, bf16[1152,1408]{1,0:T(8,128)(2,1)S(1)} %get-tuple-element.35.refs_0_.refs_3_.keep_ref, bf16[1152,1408]{1,0:T(8,128)(2,1)} %collective-permute-done.8.refs_1_.refs_4_.got_ref, ...), custom_call_target="tpu_custom_call" | custom-call | flops 1000 | bytes 7000000 | tf_op jit(solution)/shard_map/loads/pallas_call | solution.py:356
  141.2 3.2 %collective-permute-start.13 = (bf16[144,1408]{1,0:T(8,128)(2,1)}, bf16[144,1408]{1,0:T(8,128)(2,1)}, u32[]{:S(2)}, u32[]{:S(2)}) collective-permute-start(bf16[144,1408]{1,0:T(8,128)(2,1)} %get-tuple-element.39), channel_id=1, source_target_pairs={{0,112},{16,0},{32,16},{48,32},{64,48},{80,64},{96,80},{112,96},{1... | collective-permute-start | bytes 1216520 | tf_op jit(solution)/shard_map/ppermute | solution.py:323
  146.5 2.6 %collective-permute-done.24.refs_5_ = bf16[144,1408]{1,0:T(8,128)(2,1)} collective-permute-done((bf16[144,1408]{1,0:T(8,128)(2,1)}, bf16[144,1408]{1,0:T(8,128)(2,1)}, u32[]{:S(2)}, u32[]{:S(2)}) %collective-permute-start.24) | collective-permute-done | bytes 405536 | tf_op jit(solution)/shard_map/ppermute | solution.py:323
  149.1 3.0 %loads.14 = (bf16[144,1408]{1,0:T(8,128)(2,1)}, bf16[144,1408]{1,0:T(8,128)(2,1)}) custom-call(s32[2]{0:T(128)S(1)} %pad_add_fusion.6.spot_ref, bf16[1152,1408]{1,0:T(8,128)(2,1)S(1)} %copy-done.2, bf16[1152,1408]{1,0:T(8,128)(2,1)} %collective-permute-done.21.refs_1_.refs_4_.got_ref, bf16[144,1408]{1,0:T(8,128)(2,1)} %collective-permute-done.23.refs_2_, ...), custom_call_target="tpu_custom_call" | custom-call | flops 1000 | bytes 7000000 | tf_op jit(solution)/shard_map/loads/pallas_call | solution.py:356
  155.2 3.0 %loads.11 = (bf16[144,1408]{1,0:T(8,128)(2,1)}, bf16[144,1408]{1,0:T(8,128)(2,1)}) custom-call(s32[2]{0:T(128)S(1)} %pad_add_fusion.2.spot_ref, bf16[1152,1408]{1,0:T(8,128)(2,1)S(1)} %get-tuple-element.35.refs_0_.refs_3_.keep_ref, bf16[1152,1408]{1,0:T(8,128)(2,1)} %collective-permute-done.8.refs_1_.refs_4_.got_ref, ...), custom_call_target="tpu_custom_call" | custom-call | flops 1000 | bytes 7000000 | tf_op jit(solution)/shard_map/loads/pallas_call | solution.py:356
  163.9 2.8 %collective-permute-done.26.refs_5_ = bf16[144,1408]{1,0:T(8,128)(2,1)} collective-permute-done((bf16[144,1408]{1,0:T(8,128)(2,1)}, bf16[144,1408]{1,0:T(8,128)(2,1)}, u32[]{:S(2)}, u32[]{:S(2)}) %collective-permute-start.26) | collective-permute-done | bytes 405536 | tf_op jit(solution)/shard_map/ppermute | solution.py:323
  166.7 3.0 %loads.15 = (bf16[144,1408]{1,0:T(8,128)(2,1)}, bf16[144,1408]{1,0:T(8,128)(2,1)}) custom-call(s32[2]{0:T(128)S(1)} %pad_add_fusion.5.spot_ref, bf16[1152,1408]{1,0:T(8,128)(2,1)S(1)} %copy-done.3, bf16[1152,1408]{1,0:T(8,128)(2,1)} %collective-permute-done.21.refs_1_.refs_4_.got_ref, bf16[144,1408]{1,0:T(8,128)(2,1)} %collective-permute-done.25.refs_2_, ...), custom_call_target="tpu_custom_call" | custom-call | flops 1000 | bytes 7000000 | tf_op jit(solution)/shard_map/loads/pallas_call | solution.py:356
  173.0 2.4 %settle.2 = (bf16[72,1408]{1,0:T(8,128)(2,1)S(1)}, bf16[72,1408]{1,0:T(8,128)(2,1)S(1)}) custom-call(s32[2]{0:T(128)S(1)} %pad_add_fusion.1.spot_ref, bf16[1152,1408]{1,0:T(8,128)(2,1)S(1)} %get-tuple-element.35.refs_0_.refs_3_.keep_ref, bf16[1152,1408]{1,0:T(8,128)(2,1)} %collective-permute-done.8.refs_1_.refs_4_.got_ref, ...), custom_call_target="tpu_custom_call" | custom-call | flops 1000 | bytes 7000000 | tf_op jit(solution)/shard_map/settle/pallas_call | solution.py:386
  176.1 4.2 %collective-permute-done.27.one_ref = bf16[144,1408]{1,0:T(8,128)(2,1)} collective-permute-done((bf16[144,1408]{1,0:T(8,128)(2,1)}, bf16[144,1408]{1,0:T(8,128)(2,1)}, u32[]{:S(2)}, u32[]{:S(2)}) %collective-permute-start.27) | collective-permute-done | bytes 405536 | tf_op jit(solution)/shard_map/ppermute | solution.py:323
  186.5 2.9 %collective-permute-done.29.got_ref = bf16[72,1408]{1,0:T(8,128)(2,1)S(1)} collective-permute-done((bf16[72,1408]{1,0:T(8,128)(2,1)S(1)}, bf16[72,1408]{1,0:T(8,128)(2,1)S(1)}, u32[]{:S(2)}, u32[]{:S(2)}) %collective-permute-start.29) | collective-permute-done | bytes 202784 | tf_op jit(solution)/shard_map/ppermute | solution.py:323
  189.5 2.7 %collective-permute-start.30 = (bf16[72,672]{1,0:T(8,128)(2,1)S(1)}, bf16[72,672]{1,0:T(8,128)(2,1)S(1)}, u32[]{:S(2)}, u32[]{:S(2)}) collective-permute-start(bf16[72,672]{1,0:T(8,128)(2,1)S(1)} %get-tuple-element.56), channel_id=1, source_target_pairs={{0,4},{2,6},{4,0},{6,2},{1,5},{3,7},{5,1},{7,3},{8,12},{10,14},{12... | collective-permute-start | bytes 290312 | tf_op jit(solution)/shard_map/ppermute | solution.py:323
  193.2 2.7 %collective-permute-done.30.refs_2_ = bf16[72,672]{1,0:T(8,128)(2,1)S(1)} collective-permute-done((bf16[72,672]{1,0:T(8,128)(2,1)S(1)}, bf16[72,672]{1,0:T(8,128)(2,1)S(1)}, u32[]{:S(2)}, u32[]{:S(2)}) %collective-permute-start.30) | collective-permute-done | bytes 96800 | tf_op jit(solution)/shard_map/ppermute | solution.py:323
  (108 shorter events, 48.1 us)
Async XLA Ops:
  4.6 24.2 %collective-permute-start = (bf16[2,1152,128]{2,1,0:T(8,128)(2,1)S(1)}, bf16[2,1152,128]{2,1,0:T(8,128)(2,1)S(1)}, u32[]{:S(2)}, u32[]{:S(2)}) collective-permute-start(bf16[2,1152,128]{2,1,0:T(8,128)(2,1)S(1)} %get-tuple-element.30.refs_0_), channel_id=1, source_target_pairs={{0,1},{1,0},{2,3},{3,2},{4,5},{5,4},{6,7},{7,6},{8,9},{9,8},{10,11... | collective-permute-start | bytes 1769480 | tf_op jit(solution)/shard_map/ppermute | solution.py:323
  7.7 21.1 %collective-permute-start.1 = (bf16[2,1152,128]{2,1,0:T(8,128)(2,1)S(1)}, bf16[2,1152,128]{2,1,0:T(8,128)(2,1)S(1)}, u32[]{:S(2)}, u32[]{:S(2)}) collective-permute-start(bf16[2,1152,128]{2,1,0:T(8,128)(2,1)S(1)} %get-tuple-element.31), channel_id=1, source_target_pairs={{0,2},{2,4},{4,6},{6,0},{1,3},{3,5},{5,7},{7,1},{8,10},{10,12},{12... | collective-permute-start | bytes 1769480 | tf_op jit(solution)/shard_map/ppermute | solution.py:323
  9.3 19.5 %collective-permute-start.3 = (bf16[2,1152,128]{2,1,0:T(8,128)(2,1)S(1)}, bf16[2,1152,128]{2,1,0:T(8,128)(2,1)S(1)}, u32[]{:S(2)}, u32[]{:S(2)}) collective-permute-start(bf16[2,1152,128]{2,1,0:T(8,128)(2,1)S(1)} %get-tuple-element.32), channel_id=1, source_target_pairs={{0,4},{2,6},{4,0},{6,2},{1,5},{3,7},{5,1},{7,3},{8,12},{10,14},{12... | collective-permute-start | bytes 1769480 | tf_op jit(solution)/shard_map/ppermute | solution.py:323
  10.2 26.9 %collective-permute-start.5 = (bf16[2,1152,128]{2,1,0:T(8,128)(2,1)S(1)}, bf16[2,1152,128]{2,1,0:T(8,128)(2,1)S(1)}, u32[]{:S(2)}, u32[]{:S(2)}) collective-permute-start(bf16[2,1152,128]{2,1,0:T(8,128)(2,1)S(1)} %get-tuple-element.33), channel_id=1, source_target_pairs={{0,6},{2,0},{4,2},{6,4},{1,7},{3,1},{5,3},{7,5},{8,14},{10,8},{12,... | collective-permute-start | bytes 1769480 | tf_op jit(solution)/shard_map/ppermute | solution.py:323
  37.1 31.3 %collective-permute-start.7 = (bf16[672,1024]{1,0:T(8,128)(2,1)S(1)}, bf16[672,1024]{1,0:T(8,128)(2,1)S(1)}, u32[]{:S(2)}, u32[]{:S(2)}) collective-permute-start(bf16[672,1024]{1,0:T(8,128)(2,1)S(1)} %gate.1.refs_8_), channel_id=1, source_target_pairs={{0,2},{2,4},{4,6},{6,0},{1,3},{3,5},{5,7},{7,1},{8,10},{10,12},{12... | collective-permute-start | bytes 4128776 | tf_op jit(solution)/shard_map/ppermute | solution.py:323
  38.5 31.0 %collective-permute-start.18 = (bf16[672,1024]{1,0:T(8,128)(2,1)S(1)}, bf16[672,1024]{1,0:T(8,128)(2,1)S(1)}, u32[]{:S(2)}, u32[]{:S(2)}) collective-permute-start(bf16[672,1024]{1,0:T(8,128)(2,1)S(1)} %gate.1.refs_8_), channel_id=1, source_target_pairs={{0,6},{2,0},{4,2},{6,4},{1,7},{3,1},{5,3},{7,5},{8,14},{10,8},{12,... | collective-permute-start | bytes 4128776 | tf_op jit(solution)/shard_map/ppermute | solution.py:323
  39.2 31.6 %collective-permute-start.2 = (bf16[2,1152,128]{2,1,0:T(8,128)(2,1)S(1)}, bf16[2,1152,128]{2,1,0:T(8,128)(2,1)S(1)}, u32[]{:S(2)}, u32[]{:S(2)}) collective-permute-start(bf16[2,1152,128]{2,1,0:T(8,128)(2,1)S(1)} %collective-permute-done.1.refs_0_.refs_2_), channel_id=1, source_target_pairs={{0,1},{1,0},{2,3},{3,2},{4,5},{5,4},{6,7},{7,6},{8,9},{9,8},{10,11... | collective-permute-start | bytes 1769480 | tf_op jit(solution)/shard_map/ppermute | solution.py:323
  39.7 31.1 %collective-permute-start.4 = (bf16[2,1152,128]{2,1,0:T(8,128)(2,1)S(1)}, bf16[2,1152,128]{2,1,0:T(8,128)(2,1)S(1)}, u32[]{:S(2)}, u32[]{:S(2)}) collective-permute-start(bf16[2,1152,128]{2,1,0:T(8,128)(2,1)S(1)} %collective-permute-done.3.refs_1_.refs_4_), channel_id=1, source_target_pairs={{0,1},{1,0},{2,3},{3,2},{4,5},{5,4},{6,7},{7,6},{8,9},{9,8},{10,11... | collective-permute-start | bytes 1769480 | tf_op jit(solution)/shard_map/ppermute | solution.py:323
  42.7 37.1 %collective-permute-start.6 = (bf16[2,1152,128]{2,1,0:T(8,128)(2,1)S(1)}, bf16[2,1152,128]{2,1,0:T(8,128)(2,1)S(1)}, u32[]{:S(2)}, u32[]{:S(2)}) collective-permute-start(bf16[2,1152,128]{2,1,0:T(8,128)(2,1)S(1)} %collective-permute-done.5.refs_2_.refs_6_), channel_id=1, source_target_pairs={{0,1},{1,0},{2,3},{3,2},{4,5},{5,4},{6,7},{7,6},{8,9},{9,8},{10,11... | collective-permute-start | bytes 1769480 | tf_op jit(solution)/shard_map/ppermute | solution.py:323
  68.4 25.0 %collective-permute-start.19 = (bf16[336,1024]{1,0:T(8,128)(2,1)S(1)}, bf16[336,1024]{1,0:T(8,128)(2,1)S(1)}, u32[]{:S(2)}, u32[]{:S(2)}) collective-permute-start(bf16[336,1024]{1,0:T(8,128)(2,1)S(1)} %slice.8), channel_id=1, source_target_pairs={{0,2},{2,4},{4,6},{6,0},{1,3},{3,5},{5,7},{7,1},{8,10},{10,12},{12... | collective-permute-start | bytes 2064392 | tf_op jit(solution)/shard_map/ppermute | solution.py:323
  69.6 23.8 %collective-permute-start.20 = (bf16[336,1024]{1,0:T(8,128)(2,1)S(1)}, bf16[336,1024]{1,0:T(8,128)(2,1)S(1)}, u32[]{:S(2)}, u32[]{:S(2)}) collective-permute-start(bf16[336,1024]{1,0:T(8,128)(2,1)S(1)} %slice.9), channel_id=1, source_target_pairs={{0,6},{2,0},{4,2},{6,4},{1,7},{3,1},{5,3},{7,5},{8,14},{10,8},{12,... | collective-permute-start | bytes 2064392 | tf_op jit(solution)/shard_map/ppermute | solution.py:323
  86.4 13.1 %collective-permute-start.8 = (bf16[1152,1408]{1,0:T(8,128)(2,1)}, bf16[1152,1408]{1,0:T(8,128)(2,1)}, u32[]{:S(2)}, u32[]{:S(2)}) collective-permute-start(bf16[1152,1408]{1,0:T(8,128)(2,1)} %get-tuple-element.34.refs_10_), channel_id=1, source_target_pairs={{0,8},{8,0},{1,9},{9,1},{2,10},{10,2},{3,11},{11,3},{4,12},{12,4},... | collective-permute-start | bytes 9732104 | tf_op jit(solution)/shard_map/ppermute | solution.py:323
  99.0 14.0 %collective-permute-start.21 = (bf16[1152,1408]{1,0:T(8,128)(2,1)}, bf16[1152,1408]{1,0:T(8,128)(2,1)}, u32[]{:S(2)}, u32[]{:S(2)}) collective-permute-start(bf16[1152,1408]{1,0:T(8,128)(2,1)} %terms.6.refs_3_), channel_id=1, source_target_pairs={{0,8},{8,0},{1,9},{9,1},{2,10},{10,2},{3,11},{11,3},{4,12},{12,4},... | collective-permute-start | bytes 9732104 | tf_op jit(solution)/shard_map/ppermute | solution.py:323
  101.4 17.8 %collective-permute-start.9 = (bf16[144,1408]{1,0:T(8,128)(2,1)}, bf16[144,1408]{1,0:T(8,128)(2,1)}, u32[]{:S(2)}, u32[]{:S(2)}) collective-permute-start(bf16[144,1408]{1,0:T(8,128)(2,1)} %loads.8), channel_id=1, source_target_pairs={{0,16},{16,32},{32,48},{48,64},{64,80},{80,96},{96,112},{112,0},{1... | collective-permute-start | bytes 1216520 | tf_op jit(solution)/shard_map/ppermute | solution.py:323
  115.1 14.0 %collective-permute-start.22 = (bf16[144,1408]{1,0:T(8,128)(2,1)}, bf16[144,1408]{1,0:T(8,128)(2,1)}, u32[]{:S(2)}, u32[]{:S(2)}) collective-permute-start(bf16[144,1408]{1,0:T(8,128)(2,1)} %loads.12), channel_id=1, source_target_pairs={{0,112},{16,0},{32,16},{48,32},{64,48},{80,64},{96,80},{112,96},{1... | collective-permute-start | bytes 1216520 | tf_op jit(solution)/shard_map/ppermute | solution.py:323
  122.2 13.7 %collective-permute-start.10 = (bf16[144,1408]{1,0:T(8,128)(2,1)}, bf16[144,1408]{1,0:T(8,128)(2,1)}, u32[]{:S(2)}, u32[]{:S(2)}) collective-permute-start(bf16[144,1408]{1,0:T(8,128)(2,1)} %get-tuple-element.36), channel_id=1, source_target_pairs={{0,16},{16,32},{32,48},{48,64},{64,80},{80,96},{96,112},{112,0},{1... | collective-permute-start | bytes 1216520 | tf_op jit(solution)/shard_map/ppermute | solution.py:323
  122.2 15.6 %collective-permute-start.11 = (bf16[144,1408]{1,0:T(8,128)(2,1)}, bf16[144,1408]{1,0:T(8,128)(2,1)}, u32[]{:S(2)}, u32[]{:S(2)}) collective-permute-start(bf16[144,1408]{1,0:T(8,128)(2,1)} %get-tuple-element.37), channel_id=1, source_target_pairs={{0,112},{16,0},{32,16},{48,32},{64,48},{80,64},{96,80},{112,96},{1... | collective-permute-start | bytes 1216520 | tf_op jit(solution)/shard_map/ppermute | solution.py:323
  132.1 14.4 %collective-permute-start.23 = (bf16[144,1408]{1,0:T(8,128)(2,1)}, bf16[144,1408]{1,0:T(8,128)(2,1)}, u32[]{:S(2)}, u32[]{:S(2)}) collective-permute-start(bf16[144,1408]{1,0:T(8,128)(2,1)} %get-tuple-element.48), channel_id=1, source_target_pairs={{0,112},{16,0},{32,16},{48,32},{64,48},{80,64},{96,80},{112,96},{1... | collective-permute-start | bytes 1216520 | tf_op jit(solution)/shard_map/ppermute | solution.py:323
  135.7 13.3 %collective-permute-start.24 = (bf16[144,1408]{1,0:T(8,128)(2,1)}, bf16[144,1408]{1,0:T(8,128)(2,1)}, u32[]{:S(2)}, u32[]{:S(2)}) collective-permute-start(bf16[144,1408]{1,0:T(8,128)(2,1)} %get-tuple-element.49), channel_id=1, source_target_pairs={{0,16},{16,32},{32,48},{48,64},{64,80},{80,96},{96,112},{112,0},{1... | collective-permute-start | bytes 1216520 | tf_op jit(solution)/shard_map/ppermute | solution.py:323
  140.8 14.4 %collective-permute-start.12 = (bf16[144,1408]{1,0:T(8,128)(2,1)}, bf16[144,1408]{1,0:T(8,128)(2,1)}, u32[]{:S(2)}, u32[]{:S(2)}) collective-permute-start(bf16[144,1408]{1,0:T(8,128)(2,1)} %get-tuple-element.38), channel_id=1, source_target_pairs={{0,16},{16,32},{32,48},{48,64},{64,80},{80,96},{96,112},{112,0},{1... | collective-permute-start | bytes 1216520 | tf_op jit(solution)/shard_map/ppermute | solution.py:323
  141.2 14.0 %collective-permute-start.13 = (bf16[144,1408]{1,0:T(8,128)(2,1)}, bf16[144,1408]{1,0:T(8,128)(2,1)}, u32[]{:S(2)}, u32[]{:S(2)}) collective-permute-start(bf16[144,1408]{1,0:T(8,128)(2,1)} %get-tuple-element.39), channel_id=1, source_target_pairs={{0,112},{16,0},{32,16},{48,32},{64,48},{80,64},{96,80},{112,96},{1... | collective-permute-start | bytes 1216520 | tf_op jit(solution)/shard_map/ppermute | solution.py:323
  152.1 11.8 %collective-permute-start.25 = (bf16[144,1408]{1,0:T(8,128)(2,1)}, bf16[144,1408]{1,0:T(8,128)(2,1)}, u32[]{:S(2)}, u32[]{:S(2)}) collective-permute-start(bf16[144,1408]{1,0:T(8,128)(2,1)} %get-tuple-element.50), channel_id=1, source_target_pairs={{0,112},{16,0},{32,16},{48,32},{64,48},{80,64},{96,80},{112,96},{1... | collective-permute-start | bytes 1216520 | tf_op jit(solution)/shard_map/ppermute | solution.py:323
  153.2 13.4 %collective-permute-start.26 = (bf16[144,1408]{1,0:T(8,128)(2,1)}, bf16[144,1408]{1,0:T(8,128)(2,1)}, u32[]{:S(2)}, u32[]{:S(2)}) collective-permute-start(bf16[144,1408]{1,0:T(8,128)(2,1)} %get-tuple-element.51), channel_id=1, source_target_pairs={{0,16},{16,32},{32,48},{48,64},{64,80},{80,96},{96,112},{112,0},{1... | collective-permute-start | bytes 1216520 | tf_op jit(solution)/shard_map/ppermute | solution.py:323
  158.2 14.8 %collective-permute-start.14 = (bf16[144,1408]{1,0:T(8,128)(2,1)}, bf16[144,1408]{1,0:T(8,128)(2,1)}, u32[]{:S(2)}, u32[]{:S(2)}) collective-permute-start(bf16[144,1408]{1,0:T(8,128)(2,1)} %get-tuple-element.40), channel_id=1, source_target_pairs={{0,16},{16,32},{32,48},{48,64},{64,80},{80,96},{96,112},{112,0},{1... | collective-permute-start | bytes 1216520 | tf_op jit(solution)/shard_map/ppermute | solution.py:323
  159.9 13.1 %collective-permute-start.15 = (bf16[144,1408]{1,0:T(8,128)(2,1)}, bf16[144,1408]{1,0:T(8,128)(2,1)}, u32[]{:S(2)}, u32[]{:S(2)}) collective-permute-start(bf16[144,1408]{1,0:T(8,128)(2,1)} %get-tuple-element.41), channel_id=1, source_target_pairs={{0,112},{16,0},{32,16},{48,32},{64,48},{80,64},{96,80},{112,96},{1... | collective-permute-start | bytes 1216520 | tf_op jit(solution)/shard_map/ppermute | solution.py:323
  169.7 10.6 %collective-permute-start.27 = (bf16[144,1408]{1,0:T(8,128)(2,1)}, bf16[144,1408]{1,0:T(8,128)(2,1)}, u32[]{:S(2)}, u32[]{:S(2)}) collective-permute-start(bf16[144,1408]{1,0:T(8,128)(2,1)} %get-tuple-element.52), channel_id=1, source_target_pairs={{0,112},{16,0},{32,16},{48,32},{64,48},{80,64},{96,80},{112,96},{1... | collective-permute-start | bytes 1216520 | tf_op jit(solution)/shard_map/ppermute | solution.py:323
  170.6 10.8 %collective-permute-start.28 = (bf16[144,1408]{1,0:T(8,128)(2,1)}, bf16[144,1408]{1,0:T(8,128)(2,1)}, u32[]{:S(2)}, u32[]{:S(2)}) collective-permute-start(bf16[144,1408]{1,0:T(8,128)(2,1)} %get-tuple-element.53), channel_id=1, source_target_pairs={{0,16},{16,32},{32,48},{48,64},{64,80},{80,96},{96,112},{112,0},{1... | collective-permute-start | bytes 1216520 | tf_op jit(solution)/shard_map/ppermute | solution.py:323
  175.5 8.8 %collective-permute-start.16 = (bf16[72,1408]{1,0:T(8,128)(2,1)S(1)}, bf16[72,1408]{1,0:T(8,128)(2,1)S(1)}, u32[]{:S(2)}, u32[]{:S(2)}) collective-permute-start(bf16[72,1408]{1,0:T(8,128)(2,1)S(1)} %get-tuple-element.43), channel_id=1, source_target_pairs={{0,128},{128,0},{1,129},{129,1},{2,130},{130,2},{3,131},{131,3},{4... | collective-permute-start | bytes 608264 | tf_op jit(solution)/shard_map/ppermute | solution.py:323
  183.6 5.8 %collective-permute-start.29 = (bf16[72,1408]{1,0:T(8,128)(2,1)S(1)}, bf16[72,1408]{1,0:T(8,128)(2,1)S(1)}, u32[]{:S(2)}, u32[]{:S(2)}) collective-permute-start(bf16[72,1408]{1,0:T(8,128)(2,1)S(1)} %get-tuple-element.55), channel_id=1, source_target_pairs={{0,128},{128,0},{1,129},{129,1},{2,130},{130,2},{3,131},{131,3},{4... | collective-permute-start | bytes 608264 | tf_op jit(solution)/shard_map/ppermute | solution.py:323
  184.4 8.8 %collective-permute-start.17 = (bf16[72,672]{1,0:T(8,128)(2,1)S(1)}, bf16[72,672]{1,0:T(8,128)(2,1)S(1)}, u32[]{:S(2)}, u32[]{:S(2)}) collective-permute-start(bf16[72,672]{1,0:T(8,128)(2,1)S(1)} %get-tuple-element.45), channel_id=1, source_target_pairs={{0,6},{2,0},{4,2},{6,4},{1,7},{3,1},{5,3},{7,5},{8,14},{10,8},{12,... | collective-permute-start | bytes 290312 | tf_op jit(solution)/shard_map/ppermute | solution.py:323
  189.5 6.3 %collective-permute-start.30 = (bf16[72,672]{1,0:T(8,128)(2,1)S(1)}, bf16[72,672]{1,0:T(8,128)(2,1)S(1)}, u32[]{:S(2)}, u32[]{:S(2)}) collective-permute-start(bf16[72,672]{1,0:T(8,128)(2,1)S(1)} %get-tuple-element.56), channel_id=1, source_target_pairs={{0,4},{2,6},{4,0},{6,2},{1,5},{3,7},{5,1},{7,3},{8,12},{10,14},{12... | collective-permute-start | bytes 290312 | tf_op jit(solution)/shard_map/ppermute | solution.py:323
  192.2 4.8 %collective-permute-start.31 = (bf16[72,672]{1,0:T(8,128)(2,1)S(1)}, bf16[72,672]{1,0:T(8,128)(2,1)S(1)}, u32[]{:S(2)}, u32[]{:S(2)}) collective-permute-start(bf16[72,672]{1,0:T(8,128)(2,1)S(1)} %get-tuple-element.57), channel_id=1, source_target_pairs={{0,2},{2,4},{4,6},{6,0},{1,3},{3,5},{5,7},{7,1},{8,10},{10,12},{12... | collective-permute-start | bytes 290312 | tf_op jit(solution)/shard_map/ppermute | solution.py:323
  (21 other events, 161.3 us)

commit v2 on v1

--- a/solution.py
+++ b/solution.py
@@ -23,6 +23,8 @@
 NARROW = jnp.bfloat16
 MIB = 1024 * 1024
 PIECE = 2 * ROWS
+LINE_AT = 3
+RING_AT = 4
 
 
 def cost(time):
@@ -168,10 +170,14 @@
         ],
         out_specs=(pl.BlockSpec((2, 2 * PIECE, tokens), lambda i: (0, i, 0)),) * 4,
         scratch_shapes=[pltpu.VMEM((2 * lanes, tokens), jnp.float32)],
-        compiler_params=pltpu.CompilerParams(vmem_limit_bytes=10 * MIB),
+        compiler_params=pltpu.CompilerParams(vmem_limit_bytes=6 * MIB),
         cost_estimate=cost(3),
         name="turn",
     )(place, activations, activations)
+
+
+def far_off(x):
+    return pltpu.with_memory_space_constraint(x, pltpu.HBM)
 
 
 def join_factors(factors, joined):
@@ -289,7 +295,7 @@
         ),
         in_specs=[pl.BlockSpec(memory_space=pltpu.SMEM)] + [vmem] * 6,
         out_specs=(vmem, vmem),
-        compiler_params=pltpu.CompilerParams(vmem_limit_bytes=10 * MIB),
+        compiler_params=pltpu.CompilerParams(vmem_limit_bytes=6 * MIB),
         cost_estimate=cost(2),
         name="finish",
     )(place, mask, key_mask, *blocks)
@@ -333,12 +339,12 @@
         out_ref[...] = total.astype(NARROW)
 
 
-def loads(spots, keep, got, moving):
+def loads(place, aheads, keep, got, moving):
     streams = len(moving)
     width = keep.shape[1]
 
     def local_spec(at):
-        return pl.BlockSpec((PIECE, width), lambda i, spot: (spot[at], 0))
+        return pl.BlockSpec((PIECE, width), lambda i, spot: (spot[RING_AT + aheads[at] % RINGS], 0))
 
     whole = pl.BlockSpec((PIECE, width), lambda i, spot: (0, 0))
     in_specs = []
@@ -348,7 +354,7 @@
         operands += [keep, got]
         if there is None:
             in_specs.append(pl.BlockSpec(memory_space=pltpu.SMEM))
-            operands.append(spots)
+            operands.append(place)
         else:
             in_specs.append(whole)
             operands.append(there)
@@ -359,10 +365,10 @@
         grid_spec=pltpu.PrefetchScalarGridSpec(
             num_scalar_prefetch=1, grid=(1,), in_specs=in_specs, out_specs=(whole,) * streams
         ),
-        compiler_params=pltpu.CompilerParams(vmem_limit_bytes=10 * MIB),
+        compiler_params=pltpu.CompilerParams(vmem_limit_bytes=6 * MIB),
         cost_estimate=cost(2),
         name="loads",
-    )(spots, *operands)
+    )(place, *operands)
 
 
 def settle_kernel(spot_ref, keep_ref, got_ref, one_ref, two_ref, mine_ref, other_ref, total):
@@ -372,14 +378,14 @@
         + one_ref[...].astype(jnp.float32)
         + two_ref[...].astype(jnp.float32)
     )
-    line = spot_ref[1]
+    line = spot_ref[LINE_AT]
     mine_ref[...] = total[pl.ds(pl.multiple_of(line * ROWS, 8), ROWS), :].astype(NARROW)
     other_ref[...] = total[pl.ds(pl.multiple_of((1 - line) * ROWS, 8), ROWS), :].astype(NARROW)
 
 
-def settle(spots, keep, got, one, two):
+def settle(place, keep, got, one, two):
     width = keep.shape[1]
-    local = pl.BlockSpec((PIECE, width), lambda i, spot: (spot[0], 0))
+    local = pl.BlockSpec((PIECE, width), lambda i, spot: (spot[RING_AT], 0))
     whole = pl.BlockSpec((PIECE, width), lambda i, spot: (0, 0))
     out = pl.BlockSpec((ROWS, width), lambda i, spot: (0, 0))
     shape = jax.ShapeDtypeStruct((ROWS, width), NARROW)
@@ -393,10 +399,10 @@
             out_specs=(out, out),
             scratch_shapes=[pltpu.VMEM((PIECE, width), jnp.float32)],
         ),
-        compiler_params=pltpu.CompilerParams(vmem_limit_bytes=10 * MIB),
+        compiler_params=pltpu.CompilerParams(vmem_limit_bytes=6 * MIB),
         cost_estimate=cost(2),
         name="settle",
-    )(spots, keep, got, one, two)
+    )(place, keep, got, one, two)
 
 
 def merge_kernel(mine_ref, got_ref, *outs):
@@ -413,7 +419,7 @@
         out_shape=(jax.ShapeDtypeStruct((ROWS, WIDTH), NARROW),) * count,
         in_specs=[vmem, vmem],
         out_specs=(vmem,) * count,
-        compiler_params=pltpu.CompilerParams(vmem_limit_bytes=10 * MIB),
+        compiler_params=pltpu.CompilerParams(vmem_limit_bytes=6 * MIB),
         cost_estimate=cost(1),
         name="merge",
     )(mine, got)
@@ -433,25 +439,30 @@
     teacher_attention_logits,
     document_length,
 ):
-    place = jnp.stack([lax.axis_index("y"), lax.axis_index("xh"), lax.axis_index("core")]).astype(jnp.int32)
     ring = lax.axis_index("z")
-    line = lax.axis_index("xl")
+    place = [lax.axis_index(axis) for axis in ("y", "xh", "core", "xl")]
+    place = jnp.stack(place + [lax.rem(ring + ahead, RINGS) for ahead in range(RINGS)]).astype(jnp.int32)
     cut = turn(place, activations)
     held = [cut[0]] + [shifted(cut[ahead], "y", 4, ahead) for ahead in (1, 2, 3)]
     swapped = [shifted(cut[0], "xh", 2, 1)]
     own = head_grads(queries, keys, teacher_attention_logits, document_length, [cut[0]])
-    own = gate(own, held[1:] + swapped)
-    swapped += [shifted(piece, "xh", 2, 1) for piece in held[1:]]
+    own = gate(own, [held[1], held[3]] + swapped)
+    sides = [shifted(held[ahead], "xh", 2, 1) for ahead in (1, 3)]
+    swapped += [sides[0], shifted(gate(held[2], sides), "xh", 2, 1), sides[1]]
     pieces = []
     for pair in zip(held, swapped):
         pieces += pair
     back = shifted(own, "y", 4, 1)
     fore = shifted(own, "y", 4, 3)
     half = WIDTH // 2
+    waited = [swapped[2]]
     factors = [
         [own],
         [back],
-        [shifted(back[:half], "y", 4, 1), shifted(fore[half:], "y", 4, 3)],
+        [
+            shifted(gate(back[:half], waited), "y", 4, 1),
+            shifted(gate(fore[half:], waited), "y", 4, 3),
+        ],
         [fore],
     ]
 
@@ -475,23 +486,20 @@
             made.append(after)
         held_terms.append((made[1], shifted(made[0], "core", 2, 1)))
 
-    def spots(*values):
-        return jnp.stack([lax.rem(value + RINGS, RINGS) for value in values]).astype(jnp.int32)
-
     moving = [[None, None], [None, None]]
     for slot in range(4):
         for at, (keep, got) in enumerate(held_terms):
             way = 1 - 2 * at
             if slot == 0:
-                (first,) = loads(spots(ring + 4 * way), keep, got, [None])
+                (first,) = loads(place, [4 * way], keep, got, [None])
                 moving[at][0] = shifted(first, "z", RINGS, way)
             else:
                 left = 4 - slot
-                pair = loads(spots(ring + left * way, ring - left * way), keep, got, moving[at])
+                pair = loads(place, [left * way, -left * way], keep, got, moving[at])
                 moving[at] = [shifted(pair[0], "z", RINGS, way), shifted(pair[1], "z", RINGS, -way)]
     blocks = {}
     for at, (keep, got) in enumerate(held_terms):
-        mine, other = settle(jnp.stack([ring, line]).astype(jnp.int32), keep, got, *moving[at])
+        mine, other = settle(place, keep, got, *moving[at])
         parts = merge(mine, shifted(other, "xl", 2, 1))
         for behind, part in zip(CHUNKS[at], parts):
             blocks[behind] = part if behind == 0 else shifted(part, "y", 4, 4 - behind)

time: 201 us -> 199 us (0.990)
  waiting for transfers between devices: 70.6 us -> 93 us
  Pallas kernels: 66.3 us -> 48.2 us
  local copies, waits for them, and re-layouts: 11.2 us -> 4.69 us
  starting transfers between devices: 47.8 us -> 51.1 us
    ppermute x32, waiting for transfers between devices: 70.6 us -> 93 us  [shifted(): return lax.ppermute(x, axis, [(at, (at + by) % size) for at in range(size)])]
    pallas_call x8, Pallas kernels: 22.1 us -> 8.39 us  [loads(): pl.pallas_call(functools.partial(load_kernel, streams), out_shape=(shape,...]
    unnamed x42 -> x19, local copies, waits for them, and re-layouts: 11.1 us -> 4.51 us
    ppermute x32, starting transfers between devices: 47.8 us -> 51.1 us  [shifted(): return lax.ppermute(x, axis, [(at, (at + by) % size) for at in range(size)])]
    pallas_call x2, Pallas kernels: 4.57 us -> 1.81 us  [settle(): pl.pallas_call(settle_kernel, out_shape=(shape, shape), grid_spec=pltpu.P...]
  transfers between devices with their start and end apart: 32 -> 32, of which waited for: 16 -> 17; matrix products, arithmetic and copies ran while one was open for 1% -> 0% of each run, Pallas kernels for 31% -> 22%
where the time goes in v2:
time: 199 us; the launch traced here: 198 us
  waiting for transfers between devices  93 us (47%)
  starting transfers between devices  51.1 us (26%)
  Pallas kernels  48.2 us (24%)
  local copies, waits for them, and re-layouts  4.69 us (2%)
    ppermute x32, waiting for transfers between devices, shifted(): return lax.ppermute(x, axis, [(at, (at + by) % size) for at in range(size)])  93 us
    ppermute x32, starting transfers between devices, shifted(): return lax.ppermute(x, axis, [(at, (at + by) % size) for at in range(size)])  51.1 us
    pallas_call x4, Pallas kernels, term_call(): pl.pallas_call(functools.partial(kernel, count), out_shape=out_shape, gri...  20.5 us
    pallas_call x1, Pallas kernels, head_grads(): pl.pallas_call(head_kernel, out_shape=jax.ShapeDtypeStruct(shape, NARROW)...  13.4 us
    pallas_call x8, Pallas kernels, loads(): pl.pallas_call(functools.partial(load_kernel, streams), out_shape=(shape,...  8.39 us
    unnamed x19, local copies, waits for them, and re-layouts  4.51 us
  transfers between devices with their start and end apart: 32, of which 17 were waited for; matrix products, arithmetic and copies ran while one was open for 0% of the time, Pallas kernels for 22%

profile of v2, /device:TPU:8, one launch (start us, length us, event | category | flops | bytes accessed | tf_op | source)
XLA Modules:
  0.0 198.2 jit_solution(15642528084215953435)
XLA Ops:
  2.4 2.2 %turn.1 = (bf16[2,1152,128]{2,1,0:T(8,128)(2,1)S(1)}, bf16[2,1152,128]{2,1,0:T(8,128)(2,1)S(1)}, bf16[2,1152,128]{2,1,0:T(8,128)(2,1)S(1)}, bf16[2,1152,128]{2,1,0:T(8,128)(2,1)S(1)}) custom-call(s32[12]{0:T(128)S(1)} %stack.51.place_ref.refs_10_.spot_ref.refs_2_.refs_5_, bf16[2,64,9216]{2,1,0:T(8,128)(2,1)S(1)} %copy-done, bf16[2,64,9216]{2,1,0:T(8,128)(2,1)S(1)} %copy-done), custom_call_target="tpu_custom_call" | custom-call | flops 1000 | bytes 10500000 | tf_op jit(solution)/shard_map/turn/pallas_call | solution.py:162
  4.6 3.1 %collective-permute-start = (bf16[2,1152,128]{2,1,0:T(8,128)(2,1)S(1)}, bf16[2,1152,128]{2,1,0:T(8,128)(2,1)S(1)}, u32[]{:S(2)}, u32[]{:S(2)}) collective-permute-start(bf16[2,1152,128]{2,1,0:T(8,128)(2,1)S(1)} %get-tuple-element.30.refs_0_), channel_id=1, source_target_pairs={{0,1},{1,0},{2,3},{3,2},{4,5},{5,4},{6,7},{7,6},{8,9},{9,8},{10,11... | collective-permute-start | bytes 1769480 | tf_op jit(solution)/shard_map/ppermute | solution.py:329
  9.7 2.8 %copy-done.1 = bf16[2,6,512,512]{3,2,1,0:T(8,128)(2,1)S(1)} copy-done((bf16[2,6,512,512]{3,2,1,0:T(8,128)(2,1)S(1)}, bf16[2,6,512,512]{3,2,1,0:T(8,128)(2,1)}, u32[]{:S(2)}) %copy-start.1) | copy-done | bytes 6291480
  12.5 13.4 %head_grads.1 = bf16[7,96,1024]{2,1,0:T(8,128)(2,1)S(1)} custom-call(s32[2,4]{1,0:T(2,128)S(1)} %copy-done.4, bf16[2,576,512]{2,1,0:T(8,128)(2,1)S(1)} %bitcast.16, bf16[2,96,512]{2,1,0:T(8,128)(2,1)S(1)} %bitcast.17, bf16[2,6,512,512]{3,2,1,0:T(8,128)(2,1)S(1)} %copy-done.1, bf16[2,1152,128]{2,1,0:T(8,128)(2,1)S(1)} %get-tuple-element.30.refs_0_), custom_call_target="tpu_custom_call" | custom-call | flops 1000 | bytes 49000000 | tf_op jit(solution)/shard_map/head_grads/pallas_call | solution.py:114
  28.1 2.3 %collective-permute-start.3 = (bf16[2,1152,128]{2,1,0:T(8,128)(2,1)S(1)}, bf16[2,1152,128]{2,1,0:T(8,128)(2,1)S(1)}, u32[]{:S(2)}, u32[]{:S(2)}) collective-permute-start(bf16[2,1152,128]{2,1,0:T(8,128)(2,1)S(1)} %get-tuple-element.32), channel_id=1, source_target_pairs={{0,4},{2,6},{4,0},{6,2},{1,5},{3,7},{5,1},{7,3},{8,12},{10,14},{12... | collective-permute-start | bytes 1769480 | tf_op jit(solution)/shard_map/ppermute | solution.py:329
  33.9 37.9 %collective-permute-done.3.refs_4_ = bf16[2,1152,128]{2,1,0:T(8,128)(2,1)S(1)} collective-permute-done((bf16[2,1152,128]{2,1,0:T(8,128)(2,1)S(1)}, bf16[2,1152,128]{2,1,0:T(8,128)(2,1)S(1)}, u32[]{:S(2)}, u32[]{:S(2)}) %collective-permute-start.3) | collective-permute-done | bytes 589856 | tf_op jit(solution)/shard_map/ppermute | solution.py:329
  72.6 13.9 %collective-permute-done.6.refs_5_.refs_0_ = bf16[2,1152,128]{2,1,0:T(8,128)(2,1)S(1)} collective-permute-done((bf16[2,1152,128]{2,1,0:T(8,128)(2,1)S(1)}, bf16[2,1152,128]{2,1,0:T(8,128)(2,1)S(1)}, u32[]{:S(2)}, u32[]{:S(2)}) %collective-permute-start.6) | collective-permute-done | bytes 589856 | tf_op jit(solution)/shard_map/ppermute | solution.py:329
  86.5 2.0 %collective-permute-start.20 = (bf16[336,1024]{1,0:T(8,128)(2,1)S(1)}, bf16[336,1024]{1,0:T(8,128)(2,1)S(1)}, u32[]{:S(2)}, u32[]{:S(2)}) collective-permute-start(bf16[336,1024]{1,0:T(8,128)(2,1)S(1)} %gate.7), channel_id=1, source_target_pairs={{0,6},{2,0},{4,2},{6,4},{1,7},{3,1},{5,3},{7,5},{8,14},{10,8},{12,... | collective-permute-start | bytes 2064392 | tf_op jit(solution)/shard_map/ppermute | solution.py:329
  88.5 5.7 %terms.4 = (bf16[1152,1408]{1,0:T(8,128)(2,1)S(1)}, bf16[1152,1024]{1,0:T(8,128)(2,1)S(1)}) custom-call(s32[12]{0:T(128)S(1)} %stack.51.place_ref.refs_10_.spot_ref.refs_2_.refs_5_, bf16[2,1152,128]{2,1,0:T(8,128)(2,1)S(1)} %get-tuple-element.30.refs_0_, bf16[2,1152,128]{2,1,0:T(8,128)(2,1)S(1)} %collective-permute-done.refs_2_.refs_1_, ...), custom_call_target="tpu_custom_call" | custom-call | flops 1000 | bytes 21000000 | tf_op jit(solution)/shard_map/terms/pallas_call | solution.py:222
  94.5 5.7 %terms.5 = (bf16[1152,1408]{1,0:T(8,128)(2,1)S(1)}, bf16[1152,1024]{1,0:T(8,128)(2,1)S(1)}) custom-call(s32[12]{0:T(128)S(1)} %stack.51.place_ref.refs_10_.spot_ref.refs_2_.refs_5_, bf16[2,1152,128]{2,1,0:T(8,128)(2,1)S(1)} %get-tuple-element.30.refs_0_, bf16[2,1152,128]{2,1,0:T(8,128)(2,1)S(1)} %collective-permute-done.refs_2_.refs_1_, ...), custom_call_target="tpu_custom_call" | custom-call | flops 1000 | bytes 21000000 | tf_op jit(solution)/shard_map/terms/pallas_call | solution.py:222
  100.7 4.5 %terms.6.refs_3_ = bf16[1152,1408]{1,0:T(8,128)(2,1)S(1)} custom-call(bf16[1152,1024]{1,0:T(8,128)(2,1)S(1)} %get-tuple-element.47.whole_ref, bf16[672,1024]{1,0:T(8,128)(2,1)S(1)} %collective-permute-done.18.refs_0_, bf16[336,1024]{1,0:T(8,128)(2,1)S(1)} %collective-permute-done.19.refs_1_, bf16[336,1024]{1,0:T(8,128)(2,1)S(1)} %collective-permute-done.20.refs_2_, ...), custom_call_target="tpu_custom_call" | custom-call | flops 1000 | bytes 21000000 | tf_op jit(solution)/shard_map/terms/pallas_call | solution.py:222
  106.6 2.0 %collective-permute-start.9 = (bf16[144,1408]{1,0:T(8,128)(2,1)S(1)}, bf16[144,1408]{1,0:T(8,128)(2,1)S(1)}, u32[]{:S(2)}, u32[]{:S(2)}) collective-permute-start(bf16[144,1408]{1,0:T(8,128)(2,1)S(1)} %loads.8), channel_id=1, source_target_pairs={{0,16},{16,32},{32,48},{48,64},{64,80},{80,96},{96,112},{112,0},{1... | collective-permute-start | bytes 1216520 | tf_op jit(solution)/shard_map/ppermute | solution.py:329
  108.6 4.5 %terms.7.refs_0_.refs_3_.keep_ref = bf16[1152,1408]{1,0:T(8,128)(2,1)S(1)} custom-call(bf16[1152,1024]{1,0:T(8,128)(2,1)S(1)} %get-tuple-element.46.whole_ref, bf16[672,1024]{1,0:T(8,128)(2,1)S(1)} %collective-permute-done.18.refs_0_, bf16[336,1024]{1,0:T(8,128)(2,1)S(1)} %collective-permute-done.19.refs_1_, ...), custom_call_target="tpu_custom_call" | custom-call | flops 1000 | bytes 21000000 | tf_op jit(solution)/shard_map/terms/pallas_call | solution.py:222
  114.3 4.0 %collective-permute-start.22 = (bf16[144,1408]{1,0:T(8,128)(2,1)S(1)}, bf16[144,1408]{1,0:T(8,128)(2,1)S(1)}, u32[]{:S(2)}, u32[]{:S(2)}) collective-permute-start(bf16[144,1408]{1,0:T(8,128)(2,1)S(1)} %loads.12), channel_id=1, source_target_pairs={{0,112},{16,0},{32,16},{48,32},{64,48},{80,64},{96,80},{112,96},{1... | collective-permute-start | bytes 1216520 | tf_op jit(solution)/shard_map/ppermute | solution.py:329
  118.4 4.2 %collective-permute-done.9.refs_2_ = bf16[144,1408]{1,0:T(8,128)(2,1)S(1)} collective-permute-done((bf16[144,1408]{1,0:T(8,128)(2,1)S(1)}, bf16[144,1408]{1,0:T(8,128)(2,1)S(1)}, u32[]{:S(2)}, u32[]{:S(2)}) %collective-permute-start.9) | collective-permute-done | bytes 405536 | tf_op jit(solution)/shard_map/ppermute | solution.py:329
  124.0 3.2 %collective-permute-start.11 = (bf16[144,1408]{1,0:T(8,128)(2,1)S(1)}, bf16[144,1408]{1,0:T(8,128)(2,1)S(1)}, u32[]{:S(2)}, u32[]{:S(2)}) collective-permute-start(bf16[144,1408]{1,0:T(8,128)(2,1)S(1)} %get-tuple-element.37), channel_id=1, source_target_pairs={{0,112},{16,0},{32,16},{48,32},{64,48},{80,64},{96,80},{112,96},{1... | collective-permute-start | bytes 1216520 | tf_op jit(solution)/shard_map/ppermute | solution.py:329
  129.4 3.8 %collective-permute-start.23 = (bf16[144,1408]{1,0:T(8,128)(2,1)S(1)}, bf16[144,1408]{1,0:T(8,128)(2,1)S(1)}, u32[]{:S(2)}, u32[]{:S(2)}) collective-permute-start(bf16[144,1408]{1,0:T(8,128)(2,1)S(1)} %get-tuple-element.48), channel_id=1, source_target_pairs={{0,112},{16,0},{32,16},{48,32},{64,48},{80,64},{96,80},{112,96},{1... | collective-permute-start | bytes 1216520 | tf_op jit(solution)/shard_map/ppermute | solution.py:329
  133.2 3.5 %collective-permute-done.10.refs_2_ = bf16[144,1408]{1,0:T(8,128)(2,1)S(1)} collective-permute-done((bf16[144,1408]{1,0:T(8,128)(2,1)S(1)}, bf16[144,1408]{1,0:T(8,128)(2,1)S(1)}, u32[]{:S(2)}, u32[]{:S(2)}) %collective-permute-start.10) | collective-permute-done | bytes 405536 | tf_op jit(solution)/shard_map/ppermute | solution.py:329
  138.1 3.6 %collective-permute-start.13 = (bf16[144,1408]{1,0:T(8,128)(2,1)S(1)}, bf16[144,1408]{1,0:T(8,128)(2,1)S(1)}, u32[]{:S(2)}, u32[]{:S(2)}) collective-permute-start(bf16[144,1408]{1,0:T(8,128)(2,1)S(1)} %get-tuple-element.39), channel_id=1, source_target_pairs={{0,112},{16,0},{32,16},{48,32},{64,48},{80,64},{96,80},{112,96},{1... | collective-permute-start | bytes 1216520 | tf_op jit(solution)/shard_map/ppermute | solution.py:329
  141.7 4.0 %collective-permute-done.23.refs_2_ = bf16[144,1408]{1,0:T(8,128)(2,1)S(1)} collective-permute-done((bf16[144,1408]{1,0:T(8,128)(2,1)S(1)}, bf16[144,1408]{1,0:T(8,128)(2,1)S(1)}, u32[]{:S(2)}, u32[]{:S(2)}) %collective-permute-start.23) | collective-permute-done | bytes 405536 | tf_op jit(solution)/shard_map/ppermute | solution.py:329
  147.5 3.0 %collective-permute-start.25 = (bf16[144,1408]{1,0:T(8,128)(2,1)S(1)}, bf16[144,1408]{1,0:T(8,128)(2,1)S(1)}, u32[]{:S(2)}, u32[]{:S(2)}) collective-permute-start(bf16[144,1408]{1,0:T(8,128)(2,1)S(1)} %get-tuple-element.50), channel_id=1, source_target_pairs={{0,112},{16,0},{32,16},{48,32},{64,48},{80,64},{96,80},{112,96},{1... | collective-permute-start | bytes 1216520 | tf_op jit(solution)/shard_map/ppermute | solution.py:329
  150.6 4.0 %collective-permute-done.12.refs_2_ = bf16[144,1408]{1,0:T(8,128)(2,1)S(1)} collective-permute-done((bf16[144,1408]{1,0:T(8,128)(2,1)S(1)}, bf16[144,1408]{1,0:T(8,128)(2,1)S(1)}, u32[]{:S(2)}, u32[]{:S(2)}) %collective-permute-start.12) | collective-permute-done | bytes 405536 | tf_op jit(solution)/shard_map/ppermute | solution.py:329
  155.6 3.5 %collective-permute-start.15 = (bf16[144,1408]{1,0:T(8,128)(2,1)S(1)}, bf16[144,1408]{1,0:T(8,128)(2,1)S(1)}, u32[]{:S(2)}, u32[]{:S(2)}) collective-permute-start(bf16[144,1408]{1,0:T(8,128)(2,1)S(1)} %get-tuple-element.41), channel_id=1, source_target_pairs={{0,112},{16,0},{32,16},{48,32},{64,48},{80,64},{96,80},{112,96},{1... | collective-permute-start | bytes 1216520 | tf_op jit(solution)/shard_map/ppermute | solution.py:329
  159.1 4.0 %collective-permute-done.25.refs_2_ = bf16[144,1408]{1,0:T(8,128)(2,1)S(1)} collective-permute-done((bf16[144,1408]{1,0:T(8,128)(2,1)S(1)}, bf16[144,1408]{1,0:T(8,128)(2,1)S(1)}, u32[]{:S(2)}, u32[]{:S(2)}) %collective-permute-start.25) | collective-permute-done | bytes 405536 | tf_op jit(solution)/shard_map/ppermute | solution.py:329
  164.9 2.8 %collective-permute-start.27 = (bf16[144,1408]{1,0:T(8,128)(2,1)S(1)}, bf16[144,1408]{1,0:T(8,128)(2,1)S(1)}, u32[]{:S(2)}, u32[]{:S(2)}) collective-permute-start(bf16[144,1408]{1,0:T(8,128)(2,1)S(1)} %get-tuple-element.52), channel_id=1, source_target_pairs={{0,112},{16,0},{32,16},{48,32},{64,48},{80,64},{96,80},{112,96},{1... | collective-permute-start | bytes 1216520 | tf_op jit(solution)/shard_map/ppermute | solution.py:329
  167.9 4.3 %collective-permute-done.14.one_ref = bf16[144,1408]{1,0:T(8,128)(2,1)S(1)} collective-permute-done((bf16[144,1408]{1,0:T(8,128)(2,1)S(1)}, bf16[144,1408]{1,0:T(8,128)(2,1)S(1)}, u32[]{:S(2)}, u32[]{:S(2)}) %collective-permute-start.14) | collective-permute-done | bytes 405536 | tf_op jit(solution)/shard_map/ppermute | solution.py:329
  173.8 6.0 %collective-permute-done.27.one_ref = bf16[144,1408]{1,0:T(8,128)(2,1)S(1)} collective-permute-done((bf16[144,1408]{1,0:T(8,128)(2,1)S(1)}, bf16[144,1408]{1,0:T(8,128)(2,1)S(1)}, u32[]{:S(2)}, u32[]{:S(2)}) %collective-permute-start.27) | collective-permute-done | bytes 405536 | tf_op jit(solution)/shard_map/ppermute | solution.py:329
  181.5 2.7 %collective-permute-start.17 = (bf16[72,672]{1,0:T(8,128)(2,1)S(1)}, bf16[72,672]{1,0:T(8,128)(2,1)S(1)}, u32[]{:S(2)}, u32[]{:S(2)}) collective-permute-start(bf16[72,672]{1,0:T(8,128)(2,1)S(1)} %get-tuple-element.45), channel_id=1, source_target_pairs={{0,6},{2,0},{4,2},{6,4},{1,7},{3,1},{5,3},{7,5},{8,14},{10,8},{12,... | collective-permute-start | bytes 290312 | tf_op jit(solution)/shard_map/ppermute | solution.py:329
  184.2 2.9 %collective-permute-done.29.got_ref = bf16[72,1408]{1,0:T(8,128)(2,1)S(1)} collective-permute-done((bf16[72,1408]{1,0:T(8,128)(2,1)S(1)}, bf16[72,1408]{1,0:T(8,128)(2,1)S(1)}, u32[]{:S(2)}, u32[]{:S(2)}) %collective-permute-start.29) | collective-permute-done | bytes 202784 | tf_op jit(solution)/shard_map/ppermute | solution.py:329
  187.3 4.5 %collective-permute-start.30 = (bf16[72,672]{1,0:T(8,128)(2,1)S(1)}, bf16[72,672]{1,0:T(8,128)(2,1)S(1)}, u32[]{:S(2)}, u32[]{:S(2)}) collective-permute-start(bf16[72,672]{1,0:T(8,128)(2,1)S(1)} %get-tuple-element.56), channel_id=1, source_target_pairs={{0,4},{2,6},{4,0},{6,2},{1,5},{3,7},{5,1},{7,3},{8,12},{10,14},{12... | collective-permute-start | bytes 290312 | tf_op jit(solution)/shard_map/ppermute | solution.py:329
  191.9 2.7 %collective-permute-done.30.refs_2_ = bf16[72,672]{1,0:T(8,128)(2,1)S(1)} collective-permute-done((bf16[72,672]{1,0:T(8,128)(2,1)S(1)}, bf16[72,672]{1,0:T(8,128)(2,1)S(1)}, u32[]{:S(2)}, u32[]{:S(2)}) %collective-permute-start.30) | collective-permute-done | bytes 96800 | tf_op jit(solution)/shard_map/ppermute | solution.py:329
  194.5 2.0 %collective-permute-done.31.refs_3_ = bf16[72,672]{1,0:T(8,128)(2,1)S(1)} collective-permute-done((bf16[72,672]{1,0:T(8,128)(2,1)S(1)}, bf16[72,672]{1,0:T(8,128)(2,1)S(1)}, u32[]{:S(2)}, u32[]{:S(2)}) %collective-permute-start.31) | collective-permute-done | bytes 96800 | tf_op jit(solution)/shard_map/ppermute | solution.py:329
  (81 shorter events, 28.5 us)
Async XLA Ops:
  4.6 21.4 %collective-permute-start = (bf16[2,1152,128]{2,1,0:T(8,128)(2,1)S(1)}, bf16[2,1152,128]{2,1,0:T(8,128)(2,1)S(1)}, u32[]{:S(2)}, u32[]{:S(2)}) collective-permute-start(bf16[2,1152,128]{2,1,0:T(8,128)(2,1)S(1)} %get-tuple-element.30.refs_0_), channel_id=1, source_target_pairs={{0,1},{1,0},{2,3},{3,2},{4,5},{5,4},{6,7},{7,6},{8,9},{9,8},{10,11... | collective-permute-start | bytes 1769480 | tf_op jit(solution)/shard_map/ppermute | solution.py:329
  7.7 18.3 %collective-permute-start.1 = (bf16[2,1152,128]{2,1,0:T(8,128)(2,1)S(1)}, bf16[2,1152,128]{2,1,0:T(8,128)(2,1)S(1)}, u32[]{:S(2)}, u32[]{:S(2)}) collective-permute-start(bf16[2,1152,128]{2,1,0:T(8,128)(2,1)S(1)} %get-tuple-element.31), channel_id=1, source_target_pairs={{0,2},{2,4},{4,6},{6,0},{1,3},{3,5},{5,7},{7,1},{8,10},{10,12},{12... | collective-permute-start | bytes 1769480 | tf_op jit(solution)/shard_map/ppermute | solution.py:329
  9.3 16.7 %collective-permute-start.4 = (bf16[2,1152,128]{2,1,0:T(8,128)(2,1)S(1)}, bf16[2,1152,128]{2,1,0:T(8,128)(2,1)S(1)}, u32[]{:S(2)}, u32[]{:S(2)}) collective-permute-start(bf16[2,1152,128]{2,1,0:T(8,128)(2,1)S(1)} %get-tuple-element.33), channel_id=1, source_target_pairs={{0,6},{2,0},{4,2},{6,4},{1,7},{3,1},{5,3},{7,5},{8,14},{10,8},{12,... | collective-permute-start | bytes 1769480 | tf_op jit(solution)/shard_map/ppermute | solution.py:329
  26.0 46.5 %collective-permute-start.7 = (bf16[672,1024]{1,0:T(8,128)(2,1)S(1)}, bf16[672,1024]{1,0:T(8,128)(2,1)S(1)}, u32[]{:S(2)}, u32[]{:S(2)}) collective-permute-start(bf16[672,1024]{1,0:T(8,128)(2,1)S(1)} %gate.5.refs_8_), channel_id=1, source_target_pairs={{0,2},{2,4},{4,6},{6,0},{1,3},{3,5},{5,7},{7,1},{8,10},{10,12},{12... | collective-permute-start | bytes 4128776 | tf_op jit(solution)/shard_map/ppermute | solution.py:329
  27.6 44.9 %collective-permute-start.18 = (bf16[672,1024]{1,0:T(8,128)(2,1)S(1)}, bf16[672,1024]{1,0:T(8,128)(2,1)S(1)}, u32[]{:S(2)}, u32[]{:S(2)}) collective-permute-start(bf16[672,1024]{1,0:T(8,128)(2,1)S(1)} %gate.5.refs_8_), channel_id=1, source_target_pairs={{0,6},{2,0},{4,2},{6,4},{1,7},{3,1},{5,3},{7,5},{8,14},{10,8},{12,... | collective-permute-start | bytes 4128776 | tf_op jit(solution)/shard_map/ppermute | solution.py:329
  28.1 43.7 %collective-permute-start.3 = (bf16[2,1152,128]{2,1,0:T(8,128)(2,1)S(1)}, bf16[2,1152,128]{2,1,0:T(8,128)(2,1)S(1)}, u32[]{:S(2)}, u32[]{:S(2)}) collective-permute-start(bf16[2,1152,128]{2,1,0:T(8,128)(2,1)S(1)} %get-tuple-element.32), channel_id=1, source_target_pairs={{0,4},{2,6},{4,0},{6,2},{1,5},{3,7},{5,1},{7,3},{8,12},{10,14},{12... | collective-permute-start | bytes 1769480 | tf_op jit(solution)/shard_map/ppermute | solution.py:329
  30.4 41.5 %collective-permute-start.2 = (bf16[2,1152,128]{2,1,0:T(8,128)(2,1)S(1)}, bf16[2,1152,128]{2,1,0:T(8,128)(2,1)S(1)}, u32[]{:S(2)}, u32[]{:S(2)}) collective-permute-start(bf16[2,1152,128]{2,1,0:T(8,128)(2,1)S(1)} %collective-permute-done.1.refs_0_.refs_2_), channel_id=1, source_target_pairs={{0,1},{1,0},{2,3},{3,2},{4,5},{5,4},{6,7},{7,6},{8,9},{9,8},{10,11... | collective-permute-start | bytes 1769480 | tf_op jit(solution)/shard_map/ppermute | solution.py:329
  32.0 39.8 %collective-permute-start.5 = (bf16[2,1152,128]{2,1,0:T(8,128)(2,1)S(1)}, bf16[2,1152,128]{2,1,0:T(8,128)(2,1)S(1)}, u32[]{:S(2)}, u32[]{:S(2)}) collective-permute-start(bf16[2,1152,128]{2,1,0:T(8,128)(2,1)S(1)} %collective-permute-done.4.refs_1_.refs_6_), channel_id=1, source_target_pairs={{0,1},{1,0},{2,3},{3,2},{4,5},{5,4},{6,7},{7,6},{8,9},{9,8},{10,11... | collective-permute-start | bytes 1769480 | tf_op jit(solution)/shard_map/ppermute | solution.py:329
  71.9 14.6 %collective-permute-start.6 = (bf16[2,1152,128]{2,1,0:T(8,128)(2,1)S(1)}, bf16[2,1152,128]{2,1,0:T(8,128)(2,1)S(1)}, u32[]{:S(2)}, u32[]{:S(2)}) collective-permute-start(bf16[2,1152,128]{2,1,0:T(8,128)(2,1)S(1)} %gate.4), channel_id=1, source_target_pairs={{0,1},{1,0},{2,3},{3,2},{4,5},{5,4},{6,7},{7,6},{8,9},{9,8},{10,11... | collective-permute-start | bytes 1769480 | tf_op jit(solution)/shard_map/ppermute | solution.py:329
  86.5 14.2 %collective-permute-start.19 = (bf16[336,1024]{1,0:T(8,128)(2,1)S(1)}, bf16[336,1024]{1,0:T(8,128)(2,1)S(1)}, u32[]{:S(2)}, u32[]{:S(2)}) collective-permute-start(bf16[336,1024]{1,0:T(8,128)(2,1)S(1)} %gate.6), channel_id=1, source_target_pairs={{0,2},{2,4},{4,6},{6,0},{1,3},{3,5},{5,7},{7,1},{8,10},{10,12},{12... | collective-permute-start | bytes 2064392 | tf_op jit(solution)/shard_map/ppermute | solution.py:329
  86.5 14.2 %collective-permute-start.20 = (bf16[336,1024]{1,0:T(8,128)(2,1)S(1)}, bf16[336,1024]{1,0:T(8,128)(2,1)S(1)}, u32[]{:S(2)}, u32[]{:S(2)}) collective-permute-start(bf16[336,1024]{1,0:T(8,128)(2,1)S(1)} %gate.7), channel_id=1, source_target_pairs={{0,6},{2,0},{4,2},{6,4},{1,7},{3,1},{5,3},{7,5},{8,14},{10,8},{12,... | collective-permute-start | bytes 2064392 | tf_op jit(solution)/shard_map/ppermute | solution.py:329
  94.2 11.2 %collective-permute-start.8 = (bf16[1152,1408]{1,0:T(8,128)(2,1)S(1)}, bf16[1152,1408]{1,0:T(8,128)(2,1)S(1)}, u32[]{:S(2)}, u32[]{:S(2)}) collective-permute-start(bf16[1152,1408]{1,0:T(8,128)(2,1)S(1)} %get-tuple-element.34.refs_10_), channel_id=1, source_target_pairs={{0,8},{8,0},{1,9},{9,1},{2,10},{10,2},{3,11},{11,3},{4,12},{12,4},... | collective-permute-start | bytes 9732104 | tf_op jit(solution)/shard_map/ppermute | solution.py:329
  105.3 7.8 %collective-permute-start.21 = (bf16[1152,1408]{1,0:T(8,128)(2,1)S(1)}, bf16[1152,1408]{1,0:T(8,128)(2,1)S(1)}, u32[]{:S(2)}, u32[]{:S(2)}) collective-permute-start(bf16[1152,1408]{1,0:T(8,128)(2,1)S(1)} %terms.6.refs_3_), channel_id=1, source_target_pairs={{0,8},{8,0},{1,9},{9,1},{2,10},{10,2},{3,11},{11,3},{4,12},{12,4},... | collective-permute-start | bytes 9732104 | tf_op jit(solution)/shard_map/ppermute | solution.py:329
  106.6 16.0 %collective-permute-start.9 = (bf16[144,1408]{1,0:T(8,128)(2,1)S(1)}, bf16[144,1408]{1,0:T(8,128)(2,1)S(1)}, u32[]{:S(2)}, u32[]{:S(2)}) collective-permute-start(bf16[144,1408]{1,0:T(8,128)(2,1)S(1)} %loads.8), channel_id=1, source_target_pairs={{0,16},{16,32},{32,48},{48,64},{64,80},{80,96},{96,112},{112,0},{1... | collective-permute-start | bytes 1216520 | tf_op jit(solution)/shard_map/ppermute | solution.py:329
  114.3 13.7 %collective-permute-start.22 = (bf16[144,1408]{1,0:T(8,128)(2,1)S(1)}, bf16[144,1408]{1,0:T(8,128)(2,1)S(1)}, u32[]{:S(2)}, u32[]{:S(2)}) collective-permute-start(bf16[144,1408]{1,0:T(8,128)(2,1)S(1)} %loads.12), channel_id=1, source_target_pairs={{0,112},{16,0},{32,16},{48,32},{64,48},{80,64},{96,80},{112,96},{1... | collective-permute-start | bytes 1216520 | tf_op jit(solution)/shard_map/ppermute | solution.py:329
  123.9 12.8 %collective-permute-start.10 = (bf16[144,1408]{1,0:T(8,128)(2,1)S(1)}, bf16[144,1408]{1,0:T(8,128)(2,1)S(1)}, u32[]{:S(2)}, u32[]{:S(2)}) collective-permute-start(bf16[144,1408]{1,0:T(8,128)(2,1)S(1)} %get-tuple-element.36), channel_id=1, source_target_pairs={{0,16},{16,32},{32,48},{48,64},{64,80},{80,96},{96,112},{112,0},{1... | collective-permute-start | bytes 1216520 | tf_op jit(solution)/shard_map/ppermute | solution.py:329
  124.0 13.1 %collective-permute-start.11 = (bf16[144,1408]{1,0:T(8,128)(2,1)S(1)}, bf16[144,1408]{1,0:T(8,128)(2,1)S(1)}, u32[]{:S(2)}, u32[]{:S(2)}) collective-permute-start(bf16[144,1408]{1,0:T(8,128)(2,1)S(1)} %get-tuple-element.37), channel_id=1, source_target_pairs={{0,112},{16,0},{32,16},{48,32},{64,48},{80,64},{96,80},{112,96},{1... | collective-permute-start | bytes 1216520 | tf_op jit(solution)/shard_map/ppermute | solution.py:329
  129.4 16.3 %collective-permute-start.23 = (bf16[144,1408]{1,0:T(8,128)(2,1)S(1)}, bf16[144,1408]{1,0:T(8,128)(2,1)S(1)}, u32[]{:S(2)}, u32[]{:S(2)}) collective-permute-start(bf16[144,1408]{1,0:T(8,128)(2,1)S(1)} %get-tuple-element.48), channel_id=1, source_target_pairs={{0,112},{16,0},{32,16},{48,32},{64,48},{80,64},{96,80},{112,96},{1... | collective-permute-start | bytes 1216520 | tf_op jit(solution)/shard_map/ppermute | solution.py:329
  133.2 13.5 %collective-permute-start.24 = (bf16[144,1408]{1,0:T(8,128)(2,1)S(1)}, bf16[144,1408]{1,0:T(8,128)(2,1)S(1)}, u32[]{:S(2)}, u32[]{:S(2)}) collective-permute-start(bf16[144,1408]{1,0:T(8,128)(2,1)S(1)} %get-tuple-element.49), channel_id=1, source_target_pairs={{0,16},{16,32},{32,48},{48,64},{64,80},{80,96},{96,112},{112,0},{1... | collective-permute-start | bytes 1216520 | tf_op jit(solution)/shard_map/ppermute | solution.py:329
  137.9 16.7 %collective-permute-start.12 = (bf16[144,1408]{1,0:T(8,128)(2,1)S(1)}, bf16[144,1408]{1,0:T(8,128)(2,1)S(1)}, u32[]{:S(2)}, u32[]{:S(2)}) collective-permute-start(bf16[144,1408]{1,0:T(8,128)(2,1)S(1)} %get-tuple-element.38), channel_id=1, source_target_pairs={{0,16},{16,32},{32,48},{48,64},{64,80},{80,96},{96,112},{112,0},{1... | collective-permute-start | bytes 1216520 | tf_op jit(solution)/shard_map/ppermute | solution.py:329
  138.1 16.4 %collective-permute-start.13 = (bf16[144,1408]{1,0:T(8,128)(2,1)S(1)}, bf16[144,1408]{1,0:T(8,128)(2,1)S(1)}, u32[]{:S(2)}, u32[]{:S(2)}) collective-permute-start(bf16[144,1408]{1,0:T(8,128)(2,1)S(1)} %get-tuple-element.39), channel_id=1, source_target_pairs={{0,112},{16,0},{32,16},{48,32},{64,48},{80,64},{96,80},{112,96},{1... | collective-permute-start | bytes 1216520 | tf_op jit(solution)/shard_map/ppermute | solution.py:329
  147.5 15.6 %collective-permute-start.25 = (bf16[144,1408]{1,0:T(8,128)(2,1)S(1)}, bf16[144,1408]{1,0:T(8,128)(2,1)S(1)}, u32[]{:S(2)}, u32[]{:S(2)}) collective-permute-start(bf16[144,1408]{1,0:T(8,128)(2,1)S(1)} %get-tuple-element.50), channel_id=1, source_target_pairs={{0,112},{16,0},{32,16},{48,32},{64,48},{80,64},{96,80},{112,96},{1... | collective-permute-start | bytes 1216520 | tf_op jit(solution)/shard_map/ppermute | solution.py:329
  150.6 13.5 %collective-permute-start.26 = (bf16[144,1408]{1,0:T(8,128)(2,1)S(1)}, bf16[144,1408]{1,0:T(8,128)(2,1)S(1)}, u32[]{:S(2)}, u32[]{:S(2)}) collective-permute-start(bf16[144,1408]{1,0:T(8,128)(2,1)S(1)} %get-tuple-element.51), channel_id=1, source_target_pairs={{0,16},{16,32},{32,48},{48,64},{64,80},{80,96},{96,112},{112,0},{1... | collective-permute-start | bytes 1216520 | tf_op jit(solution)/shard_map/ppermute | solution.py:329
  155.4 16.8 %collective-permute-start.14 = (bf16[144,1408]{1,0:T(8,128)(2,1)S(1)}, bf16[144,1408]{1,0:T(8,128)(2,1)S(1)}, u32[]{:S(2)}, u32[]{:S(2)}) collective-permute-start(bf16[144,1408]{1,0:T(8,128)(2,1)S(1)} %get-tuple-element.40), channel_id=1, source_target_pairs={{0,16},{16,32},{32,48},{48,64},{64,80},{80,96},{96,112},{112,0},{1... | collective-permute-start | bytes 1216520 | tf_op jit(solution)/shard_map/ppermute | solution.py:329
  155.6 16.5 %collective-permute-start.15 = (bf16[144,1408]{1,0:T(8,128)(2,1)S(1)}, bf16[144,1408]{1,0:T(8,128)(2,1)S(1)}, u32[]{:S(2)}, u32[]{:S(2)}) collective-permute-start(bf16[144,1408]{1,0:T(8,128)(2,1)S(1)} %get-tuple-element.41), channel_id=1, source_target_pairs={{0,112},{16,0},{32,16},{48,32},{64,48},{80,64},{96,80},{112,96},{1... | collective-permute-start | bytes 1216520 | tf_op jit(solution)/shard_map/ppermute | solution.py:329
  164.9 14.9 %collective-permute-start.27 = (bf16[144,1408]{1,0:T(8,128)(2,1)S(1)}, bf16[144,1408]{1,0:T(8,128)(2,1)S(1)}, u32[]{:S(2)}, u32[]{:S(2)}) collective-permute-start(bf16[144,1408]{1,0:T(8,128)(2,1)S(1)} %get-tuple-element.52), channel_id=1, source_target_pairs={{0,112},{16,0},{32,16},{48,32},{64,48},{80,64},{96,80},{112,96},{1... | collective-permute-start | bytes 1216520 | tf_op jit(solution)/shard_map/ppermute | solution.py:329
  167.7 12.1 %collective-permute-start.28 = (bf16[144,1408]{1,0:T(8,128)(2,1)S(1)}, bf16[144,1408]{1,0:T(8,128)(2,1)S(1)}, u32[]{:S(2)}, u32[]{:S(2)}) collective-permute-start(bf16[144,1408]{1,0:T(8,128)(2,1)S(1)} %get-tuple-element.53), channel_id=1, source_target_pairs={{0,16},{16,32},{32,48},{48,64},{64,80},{80,96},{96,112},{112,0},{1... | collective-permute-start | bytes 1216520 | tf_op jit(solution)/shard_map/ppermute | solution.py:329
  173.1 8.3 %collective-permute-start.16 = (bf16[72,1408]{1,0:T(8,128)(2,1)S(1)}, bf16[72,1408]{1,0:T(8,128)(2,1)S(1)}, u32[]{:S(2)}, u32[]{:S(2)}) collective-permute-start(bf16[72,1408]{1,0:T(8,128)(2,1)S(1)} %get-tuple-element.43), channel_id=1, source_target_pairs={{0,128},{128,0},{1,129},{129,1},{2,130},{130,2},{3,131},{131,3},{4... | collective-permute-start | bytes 608264 | tf_op jit(solution)/shard_map/ppermute | solution.py:329
  180.7 6.5 %collective-permute-start.29 = (bf16[72,1408]{1,0:T(8,128)(2,1)S(1)}, bf16[72,1408]{1,0:T(8,128)(2,1)S(1)}, u32[]{:S(2)}, u32[]{:S(2)}) collective-permute-start(bf16[72,1408]{1,0:T(8,128)(2,1)S(1)} %get-tuple-element.55), channel_id=1, source_target_pairs={{0,128},{128,0},{1,129},{129,1},{2,130},{130,2},{3,131},{131,3},{4... | collective-permute-start | bytes 608264 | tf_op jit(solution)/shard_map/ppermute | solution.py:329
  181.5 10.3 %collective-permute-start.17 = (bf16[72,672]{1,0:T(8,128)(2,1)S(1)}, bf16[72,672]{1,0:T(8,128)(2,1)S(1)}, u32[]{:S(2)}, u32[]{:S(2)}) collective-permute-start(bf16[72,672]{1,0:T(8,128)(2,1)S(1)} %get-tuple-element.45), channel_id=1, source_target_pairs={{0,6},{2,0},{4,2},{6,4},{1,7},{3,1},{5,3},{7,5},{8,14},{10,8},{12,... | collective-permute-start | bytes 290312 | tf_op jit(solution)/shard_map/ppermute | solution.py:329
  187.3 7.2 %collective-permute-start.30 = (bf16[72,672]{1,0:T(8,128)(2,1)S(1)}, bf16[72,672]{1,0:T(8,128)(2,1)S(1)}, u32[]{:S(2)}, u32[]{:S(2)}) collective-permute-start(bf16[72,672]{1,0:T(8,128)(2,1)S(1)} %get-tuple-element.56), channel_id=1, source_target_pairs={{0,4},{2,6},{4,0},{6,2},{1,5},{3,7},{5,1},{7,3},{8,12},{10,14},{12... | collective-permute-start | bytes 290312 | tf_op jit(solution)/shard_map/ppermute | solution.py:329
  191.8 4.7 %collective-permute-start.31 = (bf16[72,672]{1,0:T(8,128)(2,1)S(1)}, bf16[72,672]{1,0:T(8,128)(2,1)S(1)}, u32[]{:S(2)}, u32[]{:S(2)}) collective-permute-start(bf16[72,672]{1,0:T(8,128)(2,1)S(1)} %get-tuple-element.57), channel_id=1, source_target_pairs={{0,2},{2,4},{4,6},{6,0},{1,3},{3,5},{5,7},{7,1},{8,10},{10,12},{12... | collective-permute-start | bytes 290312 | tf_op jit(solution)/shard_map/ppermute | solution.py:329
  (9 other events, 77.6 us)

commit v3 on v2

--- a/solution.py
+++ b/solution.py
@@ -173,7 +173,7 @@
         compiler_params=pltpu.CompilerParams(vmem_limit_bytes=6 * MIB),
         cost_estimate=cost(3),
         name="turn",
-    )(place, activations, activations)
+    )(place, *[pltpu.with_memory_space_constraint(activations, pltpu.HBM)] * 2)
 
 
 def far_off(x):
@@ -274,13 +274,14 @@
 
 
 def finish_kernel(place_ref, mask_ref, key_mask_ref, *refs):
-    blocks = refs[:4]
-    out_ref, key_out_ref = refs[4:]
+    blocks = refs[:8]
+    out_ref, key_out_ref = refs[8:]
     query_width = out_ref.shape[1]
     for behind in range(4):
         owner = lax.rem(place_ref[0] + behind, 4)
         rows = pl.ds(pl.multiple_of(owner * ROWS, 8), ROWS)
-        total = blocks[behind][...].astype(jnp.float32) * (1.0 / LOSS_SCALE)
+        total = blocks[2 * behind][...].astype(jnp.float32) + blocks[2 * behind + 1][...].astype(jnp.float32)
+        total = total * (1.0 / LOSS_SCALE)
         out_ref[rows, :] = total[:, :query_width] * mask_ref[rows, :]
         key_out_ref[rows, :] = total[:, query_width:] * key_mask_ref[rows, :]
 
@@ -293,7 +294,7 @@
             jax.ShapeDtypeStruct(mask.shape, jnp.float32),
             jax.ShapeDtypeStruct(key_mask.shape, jnp.float32),
         ),
-        in_specs=[pl.BlockSpec(memory_space=pltpu.SMEM)] + [vmem] * 6,
+        in_specs=[pl.BlockSpec(memory_space=pltpu.SMEM)] + [vmem] * 10,
         out_specs=(vmem, vmem),
         compiler_params=pltpu.CompilerParams(vmem_limit_bytes=6 * MIB),
         cost_estimate=cost(2),
@@ -371,7 +372,8 @@
     )(place, *operands)
 
 
-def settle_kernel(spot_ref, keep_ref, got_ref, one_ref, two_ref, mine_ref, other_ref, total):
+def settle_kernel(spot_ref, keep_ref, got_ref, one_ref, two_ref, *refs):
+    total = refs[-1]
     total[...] = (
         keep_ref[...].astype(jnp.float32)
         + got_ref[...].astype(jnp.float32)
@@ -379,50 +381,32 @@
         + two_ref[...].astype(jnp.float32)
     )
     line = spot_ref[LINE_AT]
-    mine_ref[...] = total[pl.ds(pl.multiple_of(line * ROWS, 8), ROWS), :].astype(NARROW)
-    other_ref[...] = total[pl.ds(pl.multiple_of((1 - line) * ROWS, 8), ROWS), :].astype(NARROW)
+    for at, start in enumerate((line, 1 - line)):
+        rows = total[pl.ds(pl.multiple_of(start * ROWS, 8), ROWS), :]
+        for block in range(2):
+            refs[2 * at + block][...] = rows[:, block * WIDTH : (block + 1) * WIDTH].astype(NARROW)
 
 
 def settle(place, keep, got, one, two):
     width = keep.shape[1]
     local = pl.BlockSpec((PIECE, width), lambda i, spot: (spot[RING_AT], 0))
     whole = pl.BlockSpec((PIECE, width), lambda i, spot: (0, 0))
-    out = pl.BlockSpec((ROWS, width), lambda i, spot: (0, 0))
-    shape = jax.ShapeDtypeStruct((ROWS, width), NARROW)
+    out = pl.BlockSpec((ROWS, WIDTH), lambda i, spot: (0, 0))
+    shape = jax.ShapeDtypeStruct((ROWS, WIDTH), NARROW)
     return pl.pallas_call(
         settle_kernel,
-        out_shape=(shape, shape),
+        out_shape=(shape,) * 4,
         grid_spec=pltpu.PrefetchScalarGridSpec(
             num_scalar_prefetch=1,
             grid=(1,),
             in_specs=[local, local, whole, whole],
-            out_specs=(out, out),
+            out_specs=(out,) * 4,
             scratch_shapes=[pltpu.VMEM((PIECE, width), jnp.float32)],
         ),
         compiler_params=pltpu.CompilerParams(vmem_limit_bytes=6 * MIB),
         cost_estimate=cost(2),
         name="settle",
     )(place, keep, got, one, two)
-
-
-def merge_kernel(mine_ref, got_ref, *outs):
-    total = mine_ref[...].astype(jnp.float32) + got_ref[...].astype(jnp.float32)
-    for at, out_ref in enumerate(outs):
-        out_ref[...] = total[:, at * WIDTH : (at + 1) * WIDTH].astype(NARROW)
-
-
-def merge(mine, got):
-    vmem = pl.BlockSpec(memory_space=pltpu.VMEM)
-    count = mine.shape[1] // WIDTH
-    return pl.pallas_call(
-        merge_kernel,
-        out_shape=(jax.ShapeDtypeStruct((ROWS, WIDTH), NARROW),) * count,
-        in_specs=[vmem, vmem],
-        out_specs=(vmem,) * count,
-        compiler_params=pltpu.CompilerParams(vmem_limit_bytes=6 * MIB),
-        cost_estimate=cost(1),
-        name="merge",
-    )(mine, got)
 
 
 CHUNKS = ((0, 1), (3, 2))
@@ -446,23 +430,18 @@
     held = [cut[0]] + [shifted(cut[ahead], "y", 4, ahead) for ahead in (1, 2, 3)]
     swapped = [shifted(cut[0], "xh", 2, 1)]
     own = head_grads(queries, keys, teacher_attention_logits, document_length, [cut[0]])
-    own = gate(own, [held[1], held[3]] + swapped)
-    sides = [shifted(held[ahead], "xh", 2, 1) for ahead in (1, 3)]
-    swapped += [sides[0], shifted(gate(held[2], sides), "xh", 2, 1), sides[1]]
+    own = gate(own, held[1:] + swapped)
+    swapped += [shifted(piece, "xh", 2, 1) for piece in held[1:]]
     pieces = []
     for pair in zip(held, swapped):
         pieces += pair
     back = shifted(own, "y", 4, 1)
     fore = shifted(own, "y", 4, 3)
     half = WIDTH // 2
-    waited = [swapped[2]]
     factors = [
         [own],
         [back],
-        [
-            shifted(gate(back[:half], waited), "y", 4, 1),
-            shifted(gate(fore[half:], waited), "y", 4, 3),
-        ],
+        [shifted(back[:half], "y", 4, 1), shifted(fore[half:], "y", 4, 3)],
         [fore],
     ]
 
@@ -470,7 +449,7 @@
     key_mask = inside_mask(key_weight_latent, key_column_exponent[None, :])
 
     held_terms = []
-    after = place
+    after = fore
     wholes = []
     for at, chunk in enumerate(CHUNKS):
         parts = []
@@ -499,11 +478,12 @@
                 moving[at] = [shifted(pair[0], "z", RINGS, way), shifted(pair[1], "z", RINGS, -way)]
     blocks = {}
     for at, (keep, got) in enumerate(held_terms):
-        mine, other = settle(place, keep, got, *moving[at])
-        parts = merge(mine, shifted(other, "xl", 2, 1))
-        for behind, part in zip(CHUNKS[at], parts):
-            blocks[behind] = part if behind == 0 else shifted(part, "y", 4, 4 - behind)
-    return finish(place, mask, key_mask, [blocks[behind] for behind in range(4)])
+        made = settle(place, keep, got, *moving[at])
+        for behind, mine, other in zip(CHUNKS[at], made[:2], made[2:]):
+            across = [(x * 4 + y, (1 - x) * 4 + (y - behind) % 4) for x in range(2) for y in range(4)]
+            other = lax.ppermute(other, ("xl", "y"), across)
+            blocks[behind] = (mine if behind == 0 else shifted(mine, "y", 4, 4 - behind), other)
+    return finish(place, mask, key_mask, [block for behind in range(4) for block in blocks[behind]])
 
 
 def solution(mesh):

time: 199 us -> 189 us (0.950)
  waiting for transfers between devices: 93 us -> 76.4 us
  starting transfers between devices: 51.1 us -> 56.4 us
    ppermute x32 -> x30, waiting for transfers between devices: 93 us -> 73.8 us  [shifted(): return lax.ppermute(x, axis, [(at, (at + by) % size) for at in range(size)])]
    ppermute x0 -> x4, starting transfers between devices: none -> 6.89 us  [on_device(): other = lax.ppermute(other, ('xl', 'y'), across)]
    ppermute x0 -> x4, waiting for transfers between devices: none -> 2.57 us  [on_device(): other = lax.ppermute(other, ('xl', 'y'), across)]
    unnamed x19 -> x16, local copies, waits for them, and re-layouts: 4.51 us -> 2.82 us
    ppermute x32 -> x30, starting transfers between devices: 51.1 us -> 49.5 us  [shifted(): return lax.ppermute(x, axis, [(at, (at + by) % size) for at in range(size)])]
  transfers between devices with their start and end apart: 32 -> 34, of which waited for: 17 -> 19; matrix products, arithmetic and copies ran while one was open for 0% -> 0% of each run, Pallas kernels for 22% -> 24%
where the time goes in v3:
time: 189 us; the launch traced here: 186 us
  waiting for transfers between devices  76.4 us (40%)
  starting transfers between devices  56.4 us (30%)
  Pallas kernels  49.4 us (26%)
  local copies, waits for them, and re-layouts  2.99 us (2%)
    ppermute x30, waiting for transfers between devices, shifted(): return lax.ppermute(x, axis, [(at, (at + by) % size) for at in range(size)])  73.8 us
    ppermute x30, starting transfers between devices, shifted(): return lax.ppermute(x, axis, [(at, (at + by) % size) for at in range(size)])  49.5 us
    pallas_call x4, Pallas kernels, term_call(): pl.pallas_call(functools.partial(kernel, count), out_shape=out_shape, gri...  20.5 us
    pallas_call x1, Pallas kernels, head_grads(): pl.pallas_call(head_kernel, out_shape=jax.ShapeDtypeStruct(shape, NARROW)...  13.4 us
    pallas_call x8, Pallas kernels, loads(): pl.pallas_call(functools.partial(load_kernel, streams), out_shape=(shape,...  8.39 us
    ppermute x4, starting transfers between devices, on_device(): other = lax.ppermute(other, ('xl', 'y'), across)  6.89 us
  transfers between devices with their start and end apart: 34, of which 19 were waited for; matrix products, arithmetic and copies ran while one was open for 0% of the time, Pallas kernels for 24%

profile of v3, /device:TPU:8, one launch (start us, length us, event | category | flops | bytes accessed | tf_op | source)
XLA Modules:
  0.0 186.3 jit_solution(517424098763438710)
XLA Ops:
  0.8 3.4 %turn.1 = (bf16[2,1152,128]{2,1,0:T(8,128)(2,1)S(1)}, bf16[2,1152,128]{2,1,0:T(8,128)(2,1)S(1)}, bf16[2,1152,128]{2,1,0:T(8,128)(2,1)S(1)}, bf16[2,1152,128]{2,1,0:T(8,128)(2,1)S(1)}) custom-call(s32[12]{0:T(128)S(1)} %stack.51.place_ref.spot_ref.refs_2_.refs_5_, bf16[2,64,9216]{2,1,0:T(8,128)(2,1)} %far_ref.1, bf16[2,64,9216]{2,1,0:T(8,128)(2,1)} %far_ref.1), custom_call_target="tpu_custom_call" | custom-call | flops 1000 | bytes 10500000 | tf_op jit(solution)/shard_map/turn/pallas_call | solution.py:162
  4.2 3.1 %collective-permute-start = (bf16[2,1152,128]{2,1,0:T(8,128)(2,1)S(1)}, bf16[2,1152,128]{2,1,0:T(8,128)(2,1)S(1)}, u32[]{:S(2)}, u32[]{:S(2)}) collective-permute-start(bf16[2,1152,128]{2,1,0:T(8,128)(2,1)S(1)} %get-tuple-element.30.refs_0_), channel_id=1, source_target_pairs={{0,1},{1,0},{2,3},{3,2},{4,5},{5,4},{6,7},{7,6},{8,9},{9,8},{10,11... | collective-permute-start | bytes 1769480 | tf_op jit(solution)/shard_map/ppermute | solution.py:330
  9.8 2.4 %collective-permute-start.5 = (bf16[2,1152,128]{2,1,0:T(8,128)(2,1)S(1)}, bf16[2,1152,128]{2,1,0:T(8,128)(2,1)S(1)}, u32[]{:S(2)}, u32[]{:S(2)}) collective-permute-start(bf16[2,1152,128]{2,1,0:T(8,128)(2,1)S(1)} %get-tuple-element.33), channel_id=1, source_target_pairs={{0,6},{2,0},{4,2},{6,4},{1,7},{3,1},{5,3},{7,5},{8,14},{10,8},{12,... | collective-permute-start | bytes 1769480 | tf_op jit(solution)/shard_map/ppermute | solution.py:330
  12.2 2.8 %copy-done = bf16[2,6,512,512]{3,2,1,0:T(8,128)(2,1)S(1)} copy-done((bf16[2,6,512,512]{3,2,1,0:T(8,128)(2,1)S(1)}, bf16[2,6,512,512]{3,2,1,0:T(8,128)(2,1)}, u32[]{:S(2)}) %copy-start) | copy-done | bytes 6291480
  15.0 13.4 %head_grads.1 = bf16[7,96,1024]{2,1,0:T(8,128)(2,1)S(1)} custom-call(s32[2,4]{1,0:T(2,128)S(1)} %copy-done.3, bf16[2,576,512]{2,1,0:T(8,128)(2,1)S(1)} %bitcast.16, bf16[2,96,512]{2,1,0:T(8,128)(2,1)S(1)} %bitcast.17, bf16[2,6,512,512]{3,2,1,0:T(8,128)(2,1)S(1)} %copy-done, bf16[2,1152,128]{2,1,0:T(8,128)(2,1)S(1)} %get-tuple-element.30.refs_0_), custom_call_target="tpu_custom_call" | custom-call | flops 1000 | bytes 49000000 | tf_op jit(solution)/shard_map/head_grads/pallas_call | solution.py:114
  28.5 8.3 %collective-permute-done.5.refs_2_.refs_6_ = bf16[2,1152,128]{2,1,0:T(8,128)(2,1)S(1)} collective-permute-done((bf16[2,1152,128]{2,1,0:T(8,128)(2,1)S(1)}, bf16[2,1152,128]{2,1,0:T(8,128)(2,1)S(1)}, u32[]{:S(2)}, u32[]{:S(2)}) %collective-permute-start.5) | collective-permute-done | bytes 589856 | tf_op jit(solution)/shard_map/ppermute | solution.py:330
  39.3 3.0 %collective-permute-start.4 = (bf16[2,1152,128]{2,1,0:T(8,128)(2,1)S(1)}, bf16[2,1152,128]{2,1,0:T(8,128)(2,1)S(1)}, u32[]{:S(2)}, u32[]{:S(2)}) collective-permute-start(bf16[2,1152,128]{2,1,0:T(8,128)(2,1)S(1)} %collective-permute-done.3.refs_1_.refs_4_), channel_id=1, source_target_pairs={{0,1},{1,0},{2,3},{3,2},{4,5},{5,4},{6,7},{7,6},{8,9},{9,8},{10,11... | collective-permute-start | bytes 1769480 | tf_op jit(solution)/shard_map/ppermute | solution.py:330
  42.8 25.2 %collective-permute-done.7.refs_9_ = bf16[672,1024]{1,0:T(8,128)(2,1)S(1)} collective-permute-done((bf16[672,1024]{1,0:T(8,128)(2,1)S(1)}, bf16[672,1024]{1,0:T(8,128)(2,1)S(1)}, u32[]{:S(2)}, u32[]{:S(2)}) %collective-permute-start.7) | collective-permute-done | bytes 1376288 | tf_op jit(solution)/shard_map/ppermute | solution.py:330
  70.3 9.0 %collective-permute-done.6.refs_7_ = bf16[2,1152,128]{2,1,0:T(8,128)(2,1)S(1)} collective-permute-done((bf16[2,1152,128]{2,1,0:T(8,128)(2,1)S(1)}, bf16[2,1152,128]{2,1,0:T(8,128)(2,1)S(1)}, u32[]{:S(2)}, u32[]{:S(2)}) %collective-permute-start.6) | collective-permute-done | bytes 589856 | tf_op jit(solution)/shard_map/ppermute | solution.py:330
  79.4 5.7 %terms.4 = (bf16[1152,1408]{1,0:T(8,128)(2,1)S(1)}, bf16[1152,1024]{1,0:T(8,128)(2,1)S(1)}) custom-call(s32[12]{0:T(128)S(1)} %stack.51.place_ref.spot_ref.refs_2_.refs_5_, bf16[2,1152,128]{2,1,0:T(8,128)(2,1)S(1)} %get-tuple-element.30.refs_0_, bf16[2,1152,128]{2,1,0:T(8,128)(2,1)S(1)} %collective-permute-done.refs_3_.refs_1_, ...), custom_call_target="tpu_custom_call" | custom-call | flops 1000 | bytes 21000000 | tf_op jit(solution)/shard_map/terms/pallas_call | solution.py:222
  85.3 5.7 %terms.5 = (bf16[1152,1408]{1,0:T(8,128)(2,1)S(1)}, bf16[1152,1024]{1,0:T(8,128)(2,1)S(1)}) custom-call(s32[12]{0:T(128)S(1)} %stack.51.place_ref.spot_ref.refs_2_.refs_5_, bf16[2,1152,128]{2,1,0:T(8,128)(2,1)S(1)} %get-tuple-element.30.refs_0_, bf16[2,1152,128]{2,1,0:T(8,128)(2,1)S(1)} %collective-permute-done.refs_3_.refs_1_, ...), custom_call_target="tpu_custom_call" | custom-call | flops 1000 | bytes 21000000 | tf_op jit(solution)/shard_map/terms/pallas_call | solution.py:222
  91.1 4.6 %terms.6.refs_3_ = bf16[1152,1408]{1,0:T(8,128)(2,1)S(1)} custom-call(bf16[1152,1024]{1,0:T(8,128)(2,1)S(1)} %get-tuple-element.47.whole_ref, bf16[672,1024]{1,0:T(8,128)(2,1)S(1)} %collective-permute-done.8.refs_10_.refs_0_, bf16[336,1024]{1,0:T(8,128)(2,1)S(1)} %collective-permute-done.20.refs_1_, bf16[336,1024]{1,0:T(8,128)(2,1)S(1)} %collective-permute-done.21.refs_2_, ...), custom_call_target="tpu_custom_call" | custom-call | flops 1000 | bytes 21000000 | tf_op jit(solution)/shard_map/terms/pallas_call | solution.py:222
  99.4 4.5 %terms.7.refs_0_.refs_3_.keep_ref = bf16[1152,1408]{1,0:T(8,128)(2,1)S(1)} custom-call(bf16[1152,1024]{1,0:T(8,128)(2,1)S(1)} %get-tuple-element.46.whole_ref, bf16[672,1024]{1,0:T(8,128)(2,1)S(1)} %collective-permute-done.8.refs_10_.refs_0_, bf16[336,1024]{1,0:T(8,128)(2,1)S(1)} %collective-permute-done.20.refs_1_, ...), custom_call_target="tpu_custom_call" | custom-call | flops 1000 | bytes 21000000 | tf_op jit(solution)/shard_map/terms/pallas_call | solution.py:222
  105.1 4.0 %collective-permute-start.23 = (bf16[144,1408]{1,0:T(8,128)(2,1)S(1)}, bf16[144,1408]{1,0:T(8,128)(2,1)S(1)}, u32[]{:S(2)}, u32[]{:S(2)}) collective-permute-start(bf16[144,1408]{1,0:T(8,128)(2,1)S(1)} %loads.12), channel_id=1, source_target_pairs={{0,112},{16,0},{32,16},{48,32},{64,48},{80,64},{96,80},{112,96},{1... | collective-permute-start | bytes 1216520 | tf_op jit(solution)/shard_map/ppermute | solution.py:330
  109.2 3.7 %collective-permute-done.10.refs_2_ = bf16[144,1408]{1,0:T(8,128)(2,1)S(1)} collective-permute-done((bf16[144,1408]{1,0:T(8,128)(2,1)S(1)}, bf16[144,1408]{1,0:T(8,128)(2,1)S(1)}, u32[]{:S(2)}, u32[]{:S(2)}) %collective-permute-start.10) | collective-permute-done | bytes 405536 | tf_op jit(solution)/shard_map/ppermute | solution.py:330
  114.3 3.2 %collective-permute-start.12 = (bf16[144,1408]{1,0:T(8,128)(2,1)S(1)}, bf16[144,1408]{1,0:T(8,128)(2,1)S(1)}, u32[]{:S(2)}, u32[]{:S(2)}) collective-permute-start(bf16[144,1408]{1,0:T(8,128)(2,1)S(1)} %get-tuple-element.37), channel_id=1, source_target_pairs={{0,112},{16,0},{32,16},{48,32},{64,48},{80,64},{96,80},{112,96},{1... | collective-permute-start | bytes 1216520 | tf_op jit(solution)/shard_map/ppermute | solution.py:330
  120.3 3.8 %collective-permute-start.24 = (bf16[144,1408]{1,0:T(8,128)(2,1)S(1)}, bf16[144,1408]{1,0:T(8,128)(2,1)S(1)}, u32[]{:S(2)}, u32[]{:S(2)}) collective-permute-start(bf16[144,1408]{1,0:T(8,128)(2,1)S(1)} %get-tuple-element.48), channel_id=1, source_target_pairs={{0,112},{16,0},{32,16},{48,32},{64,48},{80,64},{96,80},{112,96},{1... | collective-permute-start | bytes 1216520 | tf_op jit(solution)/shard_map/ppermute | solution.py:330
  124.1 2.7 %collective-permute-done.11.refs_2_ = bf16[144,1408]{1,0:T(8,128)(2,1)S(1)} collective-permute-done((bf16[144,1408]{1,0:T(8,128)(2,1)S(1)}, bf16[144,1408]{1,0:T(8,128)(2,1)S(1)}, u32[]{:S(2)}, u32[]{:S(2)}) %collective-permute-start.11) | collective-permute-done | bytes 405536 | tf_op jit(solution)/shard_map/ppermute | solution.py:330
  129.0 3.3 %collective-permute-start.14 = (bf16[144,1408]{1,0:T(8,128)(2,1)S(1)}, bf16[144,1408]{1,0:T(8,128)(2,1)S(1)}, u32[]{:S(2)}, u32[]{:S(2)}) collective-permute-start(bf16[144,1408]{1,0:T(8,128)(2,1)S(1)} %get-tuple-element.39), channel_id=1, source_target_pairs={{0,112},{16,0},{32,16},{48,32},{64,48},{80,64},{96,80},{112,96},{1... | collective-permute-start | bytes 1216520 | tf_op jit(solution)/shard_map/ppermute | solution.py:330
  132.4 4.0 %collective-permute-done.24.refs_2_ = bf16[144,1408]{1,0:T(8,128)(2,1)S(1)} collective-permute-done((bf16[144,1408]{1,0:T(8,128)(2,1)S(1)}, bf16[144,1408]{1,0:T(8,128)(2,1)S(1)}, u32[]{:S(2)}, u32[]{:S(2)}) %collective-permute-start.24) | collective-permute-done | bytes 405536 | tf_op jit(solution)/shard_map/ppermute | solution.py:330
  138.4 2.8 %collective-permute-start.26 = (bf16[144,1408]{1,0:T(8,128)(2,1)S(1)}, bf16[144,1408]{1,0:T(8,128)(2,1)S(1)}, u32[]{:S(2)}, u32[]{:S(2)}) collective-permute-start(bf16[144,1408]{1,0:T(8,128)(2,1)S(1)} %get-tuple-element.50), channel_id=1, source_target_pairs={{0,112},{16,0},{32,16},{48,32},{64,48},{80,64},{96,80},{112,96},{1... | collective-permute-start | bytes 1216520 | tf_op jit(solution)/shard_map/ppermute | solution.py:330
  141.2 3.2 %collective-permute-done.13.refs_2_ = bf16[144,1408]{1,0:T(8,128)(2,1)S(1)} collective-permute-done((bf16[144,1408]{1,0:T(8,128)(2,1)S(1)}, bf16[144,1408]{1,0:T(8,128)(2,1)S(1)}, u32[]{:S(2)}, u32[]{:S(2)}) %collective-permute-start.13) | collective-permute-done | bytes 405536 | tf_op jit(solution)/shard_map/ppermute | solution.py:330
  146.5 3.2 %collective-permute-start.16 = (bf16[144,1408]{1,0:T(8,128)(2,1)S(1)}, bf16[144,1408]{1,0:T(8,128)(2,1)S(1)}, u32[]{:S(2)}, u32[]{:S(2)}) collective-permute-start(bf16[144,1408]{1,0:T(8,128)(2,1)S(1)} %get-tuple-element.41), channel_id=1, source_target_pairs={{0,112},{16,0},{32,16},{48,32},{64,48},{80,64},{96,80},{112,96},{1... | collective-permute-start | bytes 1216520 | tf_op jit(solution)/shard_map/ppermute | solution.py:330
  149.7 4.0 %collective-permute-done.26.refs_2_ = bf16[144,1408]{1,0:T(8,128)(2,1)S(1)} collective-permute-done((bf16[144,1408]{1,0:T(8,128)(2,1)S(1)}, bf16[144,1408]{1,0:T(8,128)(2,1)S(1)}, u32[]{:S(2)}, u32[]{:S(2)}) %collective-permute-start.26) | collective-permute-done | bytes 405536 | tf_op jit(solution)/shard_map/ppermute | solution.py:330
  155.6 2.8 %collective-permute-start.28 = (bf16[144,1408]{1,0:T(8,128)(2,1)S(1)}, bf16[144,1408]{1,0:T(8,128)(2,1)S(1)}, u32[]{:S(2)}, u32[]{:S(2)}) collective-permute-start(bf16[144,1408]{1,0:T(8,128)(2,1)S(1)} %get-tuple-element.52), channel_id=1, source_target_pairs={{0,112},{16,0},{32,16},{48,32},{64,48},{80,64},{96,80},{112,96},{1... | collective-permute-start | bytes 1216520 | tf_op jit(solution)/shard_map/ppermute | solution.py:330
  158.5 3.5 %collective-permute-done.15.one_ref = bf16[144,1408]{1,0:T(8,128)(2,1)S(1)} collective-permute-done((bf16[144,1408]{1,0:T(8,128)(2,1)S(1)}, bf16[144,1408]{1,0:T(8,128)(2,1)S(1)}, u32[]{:S(2)}, u32[]{:S(2)}) %collective-permute-start.15) | collective-permute-done | bytes 405536 | tf_op jit(solution)/shard_map/ppermute | solution.py:330
  164.1 2.1 %collective-permute-start.18 = (bf16[72,672]{1,0:T(8,128)(2,1)S(1)}, bf16[72,672]{1,0:T(8,128)(2,1)S(1)}, u32[]{:S(2)}, u32[]{:S(2)}) collective-permute-start(bf16[72,672]{1,0:T(8,128)(2,1)S(1)} %get-tuple-element.44), channel_id=1, source_target_pairs={{0,6},{2,0},{4,2},{6,4},{1,7},{3,1},{5,3},{7,5},{8,14},{10,8},{12,... | collective-permute-start | bytes 290312 | tf_op jit(solution)/shard_map/ppermute | solution.py:330
  166.2 2.7 %collective-permute-start.19 = (bf16[72,672]{1,0:T(8,128)(2,1)S(1)}, bf16[72,672]{1,0:T(8,128)(2,1)S(1)}, u32[]{:S(2)}, u32[]{:S(2)}) collective-permute-start(bf16[72,672]{1,0:T(8,128)(2,1)S(1)} %get-tuple-element.45), channel_id=1, source_target_pairs={{0,134},{2,128},{4,130},{6,132},{128,6},{130,0},{132,2},{134,4},{1... | collective-permute-start | bytes 290312 | tf_op jit(solution)/shard_map/ppermute | solution.py:484
  171.2 2.7 %collective-permute-start.30 = (bf16[72,672]{1,0:T(8,128)(2,1)S(1)}, bf16[72,672]{1,0:T(8,128)(2,1)S(1)}, u32[]{:S(2)}, u32[]{:S(2)}) collective-permute-start(bf16[72,672]{1,0:T(8,128)(2,1)S(1)} %get-tuple-element.54), channel_id=1, source_target_pairs={{0,4},{2,6},{4,0},{6,2},{1,5},{3,7},{5,1},{7,3},{8,12},{10,14},{12... | collective-permute-start | bytes 290312 | tf_op jit(solution)/shard_map/ppermute | solution.py:330
  176.3 2.6 %collective-permute-start.33 = (bf16[72,672]{1,0:T(8,128)(2,1)S(1)}, bf16[72,672]{1,0:T(8,128)(2,1)S(1)}, u32[]{:S(2)}, u32[]{:S(2)}) collective-permute-start(bf16[72,672]{1,0:T(8,128)(2,1)S(1)} %get-tuple-element.57), channel_id=1, source_target_pairs={{0,130},{2,132},{4,134},{6,128},{128,2},{130,4},{132,6},{134,0},{1... | collective-permute-start | bytes 290312 | tf_op jit(solution)/shard_map/ppermute | solution.py:484
  179.0 2.6 %collective-permute-done.31.refs_5_ = bf16[72,672]{1,0:T(8,128)(2,1)S(1)} collective-permute-done((bf16[72,672]{1,0:T(8,128)(2,1)S(1)}, bf16[72,672]{1,0:T(8,128)(2,1)S(1)}, u32[]{:S(2)}, u32[]{:S(2)}) %collective-permute-start.31) | collective-permute-done | bytes 96800 | tf_op jit(solution)/shard_map/ppermute | solution.py:484
  181.5 3.1 %collective-permute-done.32.refs_6_ = bf16[72,672]{1,0:T(8,128)(2,1)S(1)} collective-permute-done((bf16[72,672]{1,0:T(8,128)(2,1)S(1)}, bf16[72,672]{1,0:T(8,128)(2,1)S(1)}, u32[]{:S(2)}, u32[]{:S(2)}) %collective-permute-start.32) | collective-permute-done | bytes 96800 | tf_op jit(solution)/shard_map/ppermute | solution.py:330
  (77 shorter events, 34.4 us)
Async XLA Ops:
  4.2 24.3 %collective-permute-start = (bf16[2,1152,128]{2,1,0:T(8,128)(2,1)S(1)}, bf16[2,1152,128]{2,1,0:T(8,128)(2,1)S(1)}, u32[]{:S(2)}, u32[]{:S(2)}) collective-permute-start(bf16[2,1152,128]{2,1,0:T(8,128)(2,1)S(1)} %get-tuple-element.30.refs_0_), channel_id=1, source_target_pairs={{0,1},{1,0},{2,3},{3,2},{4,5},{5,4},{6,7},{7,6},{8,9},{9,8},{10,11... | collective-permute-start | bytes 1769480 | tf_op jit(solution)/shard_map/ppermute | solution.py:330
  7.3 21.2 %collective-permute-start.1 = (bf16[2,1152,128]{2,1,0:T(8,128)(2,1)S(1)}, bf16[2,1152,128]{2,1,0:T(8,128)(2,1)S(1)}, u32[]{:S(2)}, u32[]{:S(2)}) collective-permute-start(bf16[2,1152,128]{2,1,0:T(8,128)(2,1)S(1)} %get-tuple-element.31), channel_id=1, source_target_pairs={{0,2},{2,4},{4,6},{6,0},{1,3},{3,5},{5,7},{7,1},{8,10},{10,12},{12... | collective-permute-start | bytes 1769480 | tf_op jit(solution)/shard_map/ppermute | solution.py:330
  8.9 19.6 %collective-permute-start.3 = (bf16[2,1152,128]{2,1,0:T(8,128)(2,1)S(1)}, bf16[2,1152,128]{2,1,0:T(8,128)(2,1)S(1)}, u32[]{:S(2)}, u32[]{:S(2)}) collective-permute-start(bf16[2,1152,128]{2,1,0:T(8,128)(2,1)S(1)} %get-tuple-element.32), channel_id=1, source_target_pairs={{0,4},{2,6},{4,0},{6,2},{1,5},{3,7},{5,1},{7,3},{8,12},{10,14},{12... | collective-permute-start | bytes 1769480 | tf_op jit(solution)/shard_map/ppermute | solution.py:330
  9.8 26.9 %collective-permute-start.5 = (bf16[2,1152,128]{2,1,0:T(8,128)(2,1)S(1)}, bf16[2,1152,128]{2,1,0:T(8,128)(2,1)S(1)}, u32[]{:S(2)}, u32[]{:S(2)}) collective-permute-start(bf16[2,1152,128]{2,1,0:T(8,128)(2,1)S(1)} %get-tuple-element.33), channel_id=1, source_target_pairs={{0,6},{2,0},{4,2},{6,4},{1,7},{3,1},{5,3},{7,5},{8,14},{10,8},{12,... | collective-permute-start | bytes 1769480 | tf_op jit(solution)/shard_map/ppermute | solution.py:330
  36.7 31.2 %collective-permute-start.7 = (bf16[672,1024]{1,0:T(8,128)(2,1)S(1)}, bf16[672,1024]{1,0:T(8,128)(2,1)S(1)}, u32[]{:S(2)}, u32[]{:S(2)}) collective-permute-start(bf16[672,1024]{1,0:T(8,128)(2,1)S(1)} %gate.1.refs_8_), channel_id=1, source_target_pairs={{0,2},{2,4},{4,6},{6,0},{1,3},{3,5},{5,7},{7,1},{8,10},{10,12},{12... | collective-permute-start | bytes 4128776 | tf_op jit(solution)/shard_map/ppermute | solution.py:330
  38.1 31.0 %collective-permute-start.8 = (bf16[672,1024]{1,0:T(8,128)(2,1)S(1)}, bf16[672,1024]{1,0:T(8,128)(2,1)S(1)}, u32[]{:S(2)}, u32[]{:S(2)}) collective-permute-start(bf16[672,1024]{1,0:T(8,128)(2,1)S(1)} %gate.1.refs_8_), channel_id=1, source_target_pairs={{0,6},{2,0},{4,2},{6,4},{1,7},{3,1},{5,3},{7,5},{8,14},{10,8},{12,... | collective-permute-start | bytes 4128776 | tf_op jit(solution)/shard_map/ppermute | solution.py:330
  38.8 31.6 %collective-permute-start.2 = (bf16[2,1152,128]{2,1,0:T(8,128)(2,1)S(1)}, bf16[2,1152,128]{2,1,0:T(8,128)(2,1)S(1)}, u32[]{:S(2)}, u32[]{:S(2)}) collective-permute-start(bf16[2,1152,128]{2,1,0:T(8,128)(2,1)S(1)} %collective-permute-done.1.refs_0_.refs_2_), channel_id=1, source_target_pairs={{0,1},{1,0},{2,3},{3,2},{4,5},{5,4},{6,7},{7,6},{8,9},{9,8},{10,11... | collective-permute-start | bytes 1769480 | tf_op jit(solution)/shard_map/ppermute | solution.py:330
  39.3 31.1 %collective-permute-start.4 = (bf16[2,1152,128]{2,1,0:T(8,128)(2,1)S(1)}, bf16[2,1152,128]{2,1,0:T(8,128)(2,1)S(1)}, u32[]{:S(2)}, u32[]{:S(2)}) collective-permute-start(bf16[2,1152,128]{2,1,0:T(8,128)(2,1)S(1)} %collective-permute-done.3.refs_1_.refs_4_), channel_id=1, source_target_pairs={{0,1},{1,0},{2,3},{3,2},{4,5},{5,4},{6,7},{7,6},{8,9},{9,8},{10,11... | collective-permute-start | bytes 1769480 | tf_op jit(solution)/shard_map/ppermute | solution.py:330
  42.3 37.1 %collective-permute-start.6 = (bf16[2,1152,128]{2,1,0:T(8,128)(2,1)S(1)}, bf16[2,1152,128]{2,1,0:T(8,128)(2,1)S(1)}, u32[]{:S(2)}, u32[]{:S(2)}) collective-permute-start(bf16[2,1152,128]{2,1,0:T(8,128)(2,1)S(1)} %collective-permute-done.5.refs_2_.refs_6_), channel_id=1, source_target_pairs={{0,1},{1,0},{2,3},{3,2},{4,5},{5,4},{6,7},{7,6},{8,9},{9,8},{10,11... | collective-permute-start | bytes 1769480 | tf_op jit(solution)/shard_map/ppermute | solution.py:330
  68.0 23.0 %collective-permute-start.20 = (bf16[336,1024]{1,0:T(8,128)(2,1)S(1)}, bf16[336,1024]{1,0:T(8,128)(2,1)S(1)}, u32[]{:S(2)}, u32[]{:S(2)}) collective-permute-start(bf16[336,1024]{1,0:T(8,128)(2,1)S(1)} %slice.8), channel_id=1, source_target_pairs={{0,2},{2,4},{4,6},{6,0},{1,3},{3,5},{5,7},{7,1},{8,10},{10,12},{12... | collective-permute-start | bytes 2064392 | tf_op jit(solution)/shard_map/ppermute | solution.py:330
  69.2 21.9 %collective-permute-start.21 = (bf16[336,1024]{1,0:T(8,128)(2,1)S(1)}, bf16[336,1024]{1,0:T(8,128)(2,1)S(1)}, u32[]{:S(2)}, u32[]{:S(2)}) collective-permute-start(bf16[336,1024]{1,0:T(8,128)(2,1)S(1)} %slice.9), channel_id=1, source_target_pairs={{0,6},{2,0},{4,2},{6,4},{1,7},{3,1},{5,3},{7,5},{8,14},{10,8},{12,... | collective-permute-start | bytes 2064392 | tf_op jit(solution)/shard_map/ppermute | solution.py:330
  85.1 11.1 %collective-permute-start.9 = (bf16[1152,1408]{1,0:T(8,128)(2,1)S(1)}, bf16[1152,1408]{1,0:T(8,128)(2,1)S(1)}, u32[]{:S(2)}, u32[]{:S(2)}) collective-permute-start(bf16[1152,1408]{1,0:T(8,128)(2,1)S(1)} %get-tuple-element.34.refs_10_), channel_id=1, source_target_pairs={{0,8},{8,0},{1,9},{9,1},{2,10},{10,2},{3,11},{11,3},{4,12},{12,4},... | collective-permute-start | bytes 9732104 | tf_op jit(solution)/shard_map/ppermute | solution.py:330
  95.7 8.3 %collective-permute-start.22 = (bf16[1152,1408]{1,0:T(8,128)(2,1)S(1)}, bf16[1152,1408]{1,0:T(8,128)(2,1)S(1)}, u32[]{:S(2)}, u32[]{:S(2)}) collective-permute-start(bf16[1152,1408]{1,0:T(8,128)(2,1)S(1)} %terms.6.refs_3_), channel_id=1, source_target_pairs={{0,8},{8,0},{1,9},{9,1},{2,10},{10,2},{3,11},{11,3},{4,12},{12,4},... | collective-permute-start | bytes 9732104 | tf_op jit(solution)/shard_map/ppermute | solution.py:330
  97.4 15.5 %collective-permute-start.10 = (bf16[144,1408]{1,0:T(8,128)(2,1)S(1)}, bf16[144,1408]{1,0:T(8,128)(2,1)S(1)}, u32[]{:S(2)}, u32[]{:S(2)}) collective-permute-start(bf16[144,1408]{1,0:T(8,128)(2,1)S(1)} %loads.8), channel_id=1, source_target_pairs={{0,16},{16,32},{32,48},{48,64},{64,80},{80,96},{96,112},{112,0},{1... | collective-permute-start | bytes 1216520 | tf_op jit(solution)/shard_map/ppermute | solution.py:330
  105.1 13.8 %collective-permute-start.23 = (bf16[144,1408]{1,0:T(8,128)(2,1)S(1)}, bf16[144,1408]{1,0:T(8,128)(2,1)S(1)}, u32[]{:S(2)}, u32[]{:S(2)}) collective-permute-start(bf16[144,1408]{1,0:T(8,128)(2,1)S(1)} %loads.12), channel_id=1, source_target_pairs={{0,112},{16,0},{32,16},{48,32},{64,48},{80,64},{96,80},{112,96},{1... | collective-permute-start | bytes 1216520 | tf_op jit(solution)/shard_map/ppermute | solution.py:330
  114.2 12.5 %collective-permute-start.11 = (bf16[144,1408]{1,0:T(8,128)(2,1)S(1)}, bf16[144,1408]{1,0:T(8,128)(2,1)S(1)}, u32[]{:S(2)}, u32[]{:S(2)}) collective-permute-start(bf16[144,1408]{1,0:T(8,128)(2,1)S(1)} %get-tuple-element.36), channel_id=1, source_target_pairs={{0,16},{16,32},{32,48},{48,64},{64,80},{80,96},{96,112},{112,0},{1... | collective-permute-start | bytes 1216520 | tf_op jit(solution)/shard_map/ppermute | solution.py:330
  114.3 13.3 %collective-permute-start.12 = (bf16[144,1408]{1,0:T(8,128)(2,1)S(1)}, bf16[144,1408]{1,0:T(8,128)(2,1)S(1)}, u32[]{:S(2)}, u32[]{:S(2)}) collective-permute-start(bf16[144,1408]{1,0:T(8,128)(2,1)S(1)} %get-tuple-element.37), channel_id=1, source_target_pairs={{0,112},{16,0},{32,16},{48,32},{64,48},{80,64},{96,80},{112,96},{1... | collective-permute-start | bytes 1216520 | tf_op jit(solution)/shard_map/ppermute | solution.py:330
  120.3 16.0 %collective-permute-start.24 = (bf16[144,1408]{1,0:T(8,128)(2,1)S(1)}, bf16[144,1408]{1,0:T(8,128)(2,1)S(1)}, u32[]{:S(2)}, u32[]{:S(2)}) collective-permute-start(bf16[144,1408]{1,0:T(8,128)(2,1)S(1)} %get-tuple-element.48), channel_id=1, source_target_pairs={{0,112},{16,0},{32,16},{48,32},{64,48},{80,64},{96,80},{112,96},{1... | collective-permute-start | bytes 1216520 | tf_op jit(solution)/shard_map/ppermute | solution.py:330
  124.1 13.5 %collective-permute-start.25 = (bf16[144,1408]{1,0:T(8,128)(2,1)S(1)}, bf16[144,1408]{1,0:T(8,128)(2,1)S(1)}, u32[]{:S(2)}, u32[]{:S(2)}) collective-permute-start(bf16[144,1408]{1,0:T(8,128)(2,1)S(1)} %get-tuple-element.49), channel_id=1, source_target_pairs={{0,16},{16,32},{32,48},{48,64},{64,80},{80,96},{96,112},{112,0},{1... | collective-permute-start | bytes 1216520 | tf_op jit(solution)/shard_map/ppermute | solution.py:330
  128.5 15.9 %collective-permute-start.13 = (bf16[144,1408]{1,0:T(8,128)(2,1)S(1)}, bf16[144,1408]{1,0:T(8,128)(2,1)S(1)}, u32[]{:S(2)}, u32[]{:S(2)}) collective-permute-start(bf16[144,1408]{1,0:T(8,128)(2,1)S(1)} %get-tuple-element.38), channel_id=1, source_target_pairs={{0,16},{16,32},{32,48},{48,64},{64,80},{80,96},{96,112},{112,0},{1... | collective-permute-start | bytes 1216520 | tf_op jit(solution)/shard_map/ppermute | solution.py:330
  129.0 16.0 %collective-permute-start.14 = (bf16[144,1408]{1,0:T(8,128)(2,1)S(1)}, bf16[144,1408]{1,0:T(8,128)(2,1)S(1)}, u32[]{:S(2)}, u32[]{:S(2)}) collective-permute-start(bf16[144,1408]{1,0:T(8,128)(2,1)S(1)} %get-tuple-element.39), channel_id=1, source_target_pairs={{0,112},{16,0},{32,16},{48,32},{64,48},{80,64},{96,80},{112,96},{1... | collective-permute-start | bytes 1216520 | tf_op jit(solution)/shard_map/ppermute | solution.py:330
  138.4 15.3 %collective-permute-start.26 = (bf16[144,1408]{1,0:T(8,128)(2,1)S(1)}, bf16[144,1408]{1,0:T(8,128)(2,1)S(1)}, u32[]{:S(2)}, u32[]{:S(2)}) collective-permute-start(bf16[144,1408]{1,0:T(8,128)(2,1)S(1)} %get-tuple-element.50), channel_id=1, source_target_pairs={{0,112},{16,0},{32,16},{48,32},{64,48},{80,64},{96,80},{112,96},{1... | collective-permute-start | bytes 1216520 | tf_op jit(solution)/shard_map/ppermute | solution.py:330
  141.2 13.5 %collective-permute-start.27 = (bf16[144,1408]{1,0:T(8,128)(2,1)S(1)}, bf16[144,1408]{1,0:T(8,128)(2,1)S(1)}, u32[]{:S(2)}, u32[]{:S(2)}) collective-permute-start(bf16[144,1408]{1,0:T(8,128)(2,1)S(1)} %get-tuple-element.51), channel_id=1, source_target_pairs={{0,16},{16,32},{32,48},{48,64},{64,80},{80,96},{96,112},{112,0},{1... | collective-permute-start | bytes 1216520 | tf_op jit(solution)/shard_map/ppermute | solution.py:330
  145.9 16.1 %collective-permute-start.15 = (bf16[144,1408]{1,0:T(8,128)(2,1)S(1)}, bf16[144,1408]{1,0:T(8,128)(2,1)S(1)}, u32[]{:S(2)}, u32[]{:S(2)}) collective-permute-start(bf16[144,1408]{1,0:T(8,128)(2,1)S(1)} %get-tuple-element.40), channel_id=1, source_target_pairs={{0,16},{16,32},{32,48},{48,64},{64,80},{80,96},{96,112},{112,0},{1... | collective-permute-start | bytes 1216520 | tf_op jit(solution)/shard_map/ppermute | solution.py:330
  146.5 15.9 %collective-permute-start.16 = (bf16[144,1408]{1,0:T(8,128)(2,1)S(1)}, bf16[144,1408]{1,0:T(8,128)(2,1)S(1)}, u32[]{:S(2)}, u32[]{:S(2)}) collective-permute-start(bf16[144,1408]{1,0:T(8,128)(2,1)S(1)} %get-tuple-element.41), channel_id=1, source_target_pairs={{0,112},{16,0},{32,16},{48,32},{64,48},{80,64},{96,80},{112,96},{1... | collective-permute-start | bytes 1216520 | tf_op jit(solution)/shard_map/ppermute | solution.py:330
  155.6 14.6 %collective-permute-start.28 = (bf16[144,1408]{1,0:T(8,128)(2,1)S(1)}, bf16[144,1408]{1,0:T(8,128)(2,1)S(1)}, u32[]{:S(2)}, u32[]{:S(2)}) collective-permute-start(bf16[144,1408]{1,0:T(8,128)(2,1)S(1)} %get-tuple-element.52), channel_id=1, source_target_pairs={{0,112},{16,0},{32,16},{48,32},{64,48},{80,64},{96,80},{112,96},{1... | collective-permute-start | bytes 1216520 | tf_op jit(solution)/shard_map/ppermute | solution.py:330
  158.3 11.8 %collective-permute-start.29 = (bf16[144,1408]{1,0:T(8,128)(2,1)S(1)}, bf16[144,1408]{1,0:T(8,128)(2,1)S(1)}, u32[]{:S(2)}, u32[]{:S(2)}) collective-permute-start(bf16[144,1408]{1,0:T(8,128)(2,1)S(1)} %get-tuple-element.53), channel_id=1, source_target_pairs={{0,16},{16,32},{32,48},{48,64},{64,80},{80,96},{96,112},{112,0},{1... | collective-permute-start | bytes 1216520 | tf_op jit(solution)/shard_map/ppermute | solution.py:330
  163.4 11.4 %collective-permute-start.17 = (bf16[72,672]{1,0:T(8,128)(2,1)S(1)}, bf16[72,672]{1,0:T(8,128)(2,1)S(1)}, u32[]{:S(2)}, u32[]{:S(2)}) collective-permute-start(bf16[72,672]{1,0:T(8,128)(2,1)S(1)} %get-tuple-element.43), channel_id=1, source_target_pairs={{0,128},{2,130},{4,132},{6,134},{128,0},{130,2},{132,4},{134,6},{1... | collective-permute-start | bytes 290312 | tf_op jit(solution)/shard_map/ppermute | solution.py:484
  164.1 12.2 %collective-permute-start.18 = (bf16[72,672]{1,0:T(8,128)(2,1)S(1)}, bf16[72,672]{1,0:T(8,128)(2,1)S(1)}, u32[]{:S(2)}, u32[]{:S(2)}) collective-permute-start(bf16[72,672]{1,0:T(8,128)(2,1)S(1)} %get-tuple-element.44), channel_id=1, source_target_pairs={{0,6},{2,0},{4,2},{6,4},{1,7},{3,1},{5,3},{7,5},{8,14},{10,8},{12,... | collective-permute-start | bytes 290312 | tf_op jit(solution)/shard_map/ppermute | solution.py:330
  166.2 12.8 %collective-permute-start.19 = (bf16[72,672]{1,0:T(8,128)(2,1)S(1)}, bf16[72,672]{1,0:T(8,128)(2,1)S(1)}, u32[]{:S(2)}, u32[]{:S(2)}) collective-permute-start(bf16[72,672]{1,0:T(8,128)(2,1)S(1)} %get-tuple-element.45), channel_id=1, source_target_pairs={{0,134},{2,128},{4,130},{6,132},{128,6},{130,0},{132,2},{134,4},{1... | collective-permute-start | bytes 290312 | tf_op jit(solution)/shard_map/ppermute | solution.py:484
  174.8 9.8 %collective-permute-start.32 = (bf16[72,672]{1,0:T(8,128)(2,1)S(1)}, bf16[72,672]{1,0:T(8,128)(2,1)S(1)}, u32[]{:S(2)}, u32[]{:S(2)}) collective-permute-start(bf16[72,672]{1,0:T(8,128)(2,1)S(1)} %get-tuple-element.56), channel_id=1, source_target_pairs={{0,2},{2,4},{4,6},{6,0},{1,3},{3,5},{5,7},{7,1},{8,10},{10,12},{12... | collective-permute-start | bytes 290312 | tf_op jit(solution)/shard_map/ppermute | solution.py:330
  176.3 8.3 %collective-permute-start.33 = (bf16[72,672]{1,0:T(8,128)(2,1)S(1)}, bf16[72,672]{1,0:T(8,128)(2,1)S(1)}, u32[]{:S(2)}, u32[]{:S(2)}) collective-permute-start(bf16[72,672]{1,0:T(8,128)(2,1)S(1)} %get-tuple-element.57), channel_id=1, source_target_pairs={{0,130},{2,132},{4,134},{6,128},{128,2},{130,4},{132,6},{134,0},{1... | collective-permute-start | bytes 290312 | tf_op jit(solution)/shard_map/ppermute | solution.py:484
  (10 other events, 90.1 us)

commit v4 on v3

--- a/solution.py
+++ b/solution.py
@@ -24,6 +24,7 @@
 MIB = 1024 * 1024
 PIECE = 2 * ROWS
 LINE_AT = 3
+PIECE_ORDER = (0, 1, 3, 2)
 RING_AT = 4
 
 
@@ -201,11 +202,11 @@
     pieces = refs[:8]
     out_ref, whole_ref, joined = refs[9 + count :]
     join_factors(refs[8 : 8 + count], joined)
-    for behind in range(4):
+    for at, behind in enumerate(PIECE_ORDER):
         for across in range(2):
             source = lax.rem(place_ref[0] + 4 - behind, 4) * 2 + lax.rem(place_ref[1] + across, 2)
             lane = pl.multiple_of(source * 128, 128)
-            whole_ref[:, pl.ds(lane, 128)] = pieces[behind * 2 + across][0]
+            whole_ref[:, pl.ds(lane, 128)] = pieces[at * 2 + across][0]
     out_ref[...] = multiply(whole_ref[...], joined)
 
 
@@ -409,7 +410,7 @@
     )(place, keep, got, one, two)
 
 
-CHUNKS = ((0, 1), (3, 2))
+CHUNKS = ((1, 3), (2, 0))
 
 
 def on_device(
@@ -427,7 +428,7 @@
     place = [lax.axis_index(axis) for axis in ("y", "xh", "core", "xl")]
     place = jnp.stack(place + [lax.rem(ring + ahead, RINGS) for ahead in range(RINGS)]).astype(jnp.int32)
     cut = turn(place, activations)
-    held = [cut[0]] + [shifted(cut[ahead], "y", 4, ahead) for ahead in (1, 2, 3)]
+    held = [cut[0]] + [shifted(cut[ahead], "y", 4, ahead) for ahead in PIECE_ORDER[1:]]
     swapped = [shifted(cut[0], "xh", 2, 1)]
     own = head_grads(queries, keys, teacher_attention_logits, document_length, [cut[0]])
     own = gate(own, held[1:] + swapped)
@@ -469,13 +470,11 @@
     for slot in range(4):
         for at, (keep, got) in enumerate(held_terms):
             way = 1 - 2 * at
-            if slot == 0:
-                (first,) = loads(place, [4 * way], keep, got, [None])
-                moving[at][0] = shifted(first, "z", RINGS, way)
-            else:
-                left = 4 - slot
-                pair = loads(place, [left * way, -left * way], keep, got, moving[at])
-                moving[at] = [shifted(pair[0], "z", RINGS, way), shifted(pair[1], "z", RINGS, -way)]
+            aheads = [(4 - slot) * way, (slot - 3) * way]
+            count = 2 if slot < 3 else 1
+            sums = loads(place, aheads[:count], keep, got, moving[at][:count])
+            for stream, load in enumerate(sums):
+                moving[at][stream] = shifted(load, "z", RINGS, -way if stream else way)
     blocks = {}
     for at, (keep, got) in enumerate(held_terms):
         made = settle(place, keep, got, *moving[at])

time: 189 us -> 184 us (0.974); the launches traced: 186 us -> 183 us
  starting transfers between devices: 56.4 us -> 43.2 us
  waiting for transfers between devices: 76.4 us -> 87.8 us
    ppermute x30, starting transfers between devices: 49.5 us -> 37.9 us  [shifted(): return lax.ppermute(x, axis, [(at, (at + by) % size) for at in range(size)])]
    ppermute x30, waiting for transfers between devices: 73.8 us -> 84.1 us  [shifted(): return lax.ppermute(x, axis, [(at, (at + by) % size) for at in range(size)])]
  transfers between devices with their start and end apart: 34 -> 34, of which waited for: 19 -> 17; matrix products, arithmetic and copies ran while one was open for 0% -> 0% of each run, Pallas kernels for 24% -> 24%
where the time goes in v4:
time: 184 us; the launch traced here: 183 us
  waiting for transfers between devices  87.8 us (48%)
  Pallas kernels  48.3 us (26%)
  starting transfers between devices  43.2 us (23%)
  local copies, waits for them, and re-layouts  3 us (2%)
    ppermute x30, waiting for transfers between devices, shifted(): return lax.ppermute(x, axis, [(at, (at + by) % size) for at in range(size)])  84.1 us
    ppermute x30, starting transfers between devices, shifted(): return lax.ppermute(x, axis, [(at, (at + by) % size) for at in range(size)])  37.9 us
    pallas_call x4, Pallas kernels, term_call(): pl.pallas_call(functools.partial(kernel, count), out_shape=out_shape, gri...  20.5 us
    pallas_call x1, Pallas kernels, head_grads(): pl.pallas_call(head_kernel, out_shape=jax.ShapeDtypeStruct(shape, NARROW)...  13.4 us
    pallas_call x8, Pallas kernels, loads(): pl.pallas_call(functools.partial(load_kernel, streams), out_shape=(shape,...  7.35 us
    ppermute x4, starting transfers between devices, on_device(): other = lax.ppermute(other, ('xl', 'y'), across)  5.25 us
    ppermute x4, waiting for transfers between devices, on_device(): other = lax.ppermute(other, ('xl', 'y'), across)  3.71 us
  transfers between devices with their start and end apart: 34, of which 17 were waited for; matrix products, arithmetic and copies ran while one was open for 0% of the time, Pallas kernels for 24%

profile of v4, /device:TPU:8, one launch (start us, length us, event | category | flops | bytes accessed | tf_op | source)
XLA Modules:
  0.0 183.5 jit_solution(12930838986388739931)
XLA Ops:
  0.8 3.4 %turn.1 = (bf16[2,1152,128]{2,1,0:T(8,128)(2,1)S(1)}, bf16[2,1152,128]{2,1,0:T(8,128)(2,1)S(1)}, bf16[2,1152,128]{2,1,0:T(8,128)(2,1)S(1)}, bf16[2,1152,128]{2,1,0:T(8,128)(2,1)S(1)}) custom-call(s32[12]{0:T(128)S(1)} %stack.51.place_ref.spot_ref.refs_2_.refs_5_, bf16[2,64,9216]{2,1,0:T(8,128)(2,1)} %far_ref.1, bf16[2,64,9216]{2,1,0:T(8,128)(2,1)} %far_ref.1), custom_call_target="tpu_custom_call" | custom-call | flops 1000 | bytes 10500000 | tf_op jit(solution)/shard_map/turn/pallas_call | solution.py:163
  4.2 3.1 %collective-permute-start = (bf16[2,1152,128]{2,1,0:T(8,128)(2,1)S(1)}, bf16[2,1152,128]{2,1,0:T(8,128)(2,1)S(1)}, u32[]{:S(2)}, u32[]{:S(2)}) collective-permute-start(bf16[2,1152,128]{2,1,0:T(8,128)(2,1)S(1)} %get-tuple-element.30.refs_0_), channel_id=1, source_target_pairs={{0,1},{1,0},{2,3},{3,2},{4,5},{5,4},{6,7},{7,6},{8,9},{9,8},{10,11... | collective-permute-start | bytes 1769480 | tf_op jit(solution)/shard_map/ppermute | solution.py:331
  7.3 1.6 collective-permute-start.1
  9.3 2.3 %collective-permute-start.5 = (bf16[2,1152,128]{2,1,0:T(8,128)(2,1)S(1)}, bf16[2,1152,128]{2,1,0:T(8,128)(2,1)S(1)}, u32[]{:S(2)}, u32[]{:S(2)}) collective-permute-start(bf16[2,1152,128]{2,1,0:T(8,128)(2,1)S(1)} %get-tuple-element.33), channel_id=1, source_target_pairs={{0,4},{2,6},{4,0},{6,2},{1,5},{3,7},{5,1},{7,3},{8,12},{10,14},{12... | collective-permute-start | bytes 1769480 | tf_op jit(solution)/shard_map/ppermute | solution.py:331
  11.6 2.8 %copy-done = bf16[2,6,512,512]{3,2,1,0:T(8,128)(2,1)S(1)} copy-done((bf16[2,6,512,512]{3,2,1,0:T(8,128)(2,1)S(1)}, bf16[2,6,512,512]{3,2,1,0:T(8,128)(2,1)}, u32[]{:S(2)}) %copy-start) | copy-done | bytes 6291480
  14.4 13.4 %head_grads.1 = bf16[7,96,1024]{2,1,0:T(8,128)(2,1)S(1)} custom-call(s32[2,4]{1,0:T(2,128)S(1)} %copy-done.3, bf16[2,576,512]{2,1,0:T(8,128)(2,1)S(1)} %bitcast.16, bf16[2,96,512]{2,1,0:T(8,128)(2,1)S(1)} %bitcast.17, bf16[2,6,512,512]{3,2,1,0:T(8,128)(2,1)S(1)} %copy-done, bf16[2,1152,128]{2,1,0:T(8,128)(2,1)S(1)} %get-tuple-element.30.refs_0_), custom_call_target="tpu_custom_call" | custom-call | flops 1000 | bytes 49000000 | tf_op jit(solution)/shard_map/head_grads/pallas_call | solution.py:115
  27.8 8.9 %collective-permute-done.5.refs_2_.refs_6_ = bf16[2,1152,128]{2,1,0:T(8,128)(2,1)S(1)} collective-permute-done((bf16[2,1152,128]{2,1,0:T(8,128)(2,1)S(1)}, bf16[2,1152,128]{2,1,0:T(8,128)(2,1)S(1)}, u32[]{:S(2)}, u32[]{:S(2)}) %collective-permute-start.5) | collective-permute-done | bytes 589856 | tf_op jit(solution)/shard_map/ppermute | solution.py:331
  39.3 3.0 %collective-permute-start.4 = (bf16[2,1152,128]{2,1,0:T(8,128)(2,1)S(1)}, bf16[2,1152,128]{2,1,0:T(8,128)(2,1)S(1)}, u32[]{:S(2)}, u32[]{:S(2)}) collective-permute-start(bf16[2,1152,128]{2,1,0:T(8,128)(2,1)S(1)} %collective-permute-done.3.refs_1_.refs_4_), channel_id=1, source_target_pairs={{0,1},{1,0},{2,3},{3,2},{4,5},{5,4},{6,7},{7,6},{8,9},{9,8},{10,11... | collective-permute-start | bytes 1769480 | tf_op jit(solution)/shard_map/ppermute | solution.py:331
  42.8 24.4 %collective-permute-done.8.refs_9_.refs_10_ = bf16[672,1024]{1,0:T(8,128)(2,1)S(1)} collective-permute-done((bf16[672,1024]{1,0:T(8,128)(2,1)S(1)}, bf16[672,1024]{1,0:T(8,128)(2,1)S(1)}, u32[]{:S(2)}, u32[]{:S(2)}) %collective-permute-start.8) | collective-permute-done | bytes 1376288 | tf_op jit(solution)/shard_map/ppermute | solution.py:331
  69.4 9.1 %collective-permute-done.6.refs_7_ = bf16[2,1152,128]{2,1,0:T(8,128)(2,1)S(1)} collective-permute-done((bf16[2,1152,128]{2,1,0:T(8,128)(2,1)S(1)}, bf16[2,1152,128]{2,1,0:T(8,128)(2,1)S(1)}, u32[]{:S(2)}, u32[]{:S(2)}) %collective-permute-start.6) | collective-permute-done | bytes 589856 | tf_op jit(solution)/shard_map/ppermute | solution.py:331
  78.6 5.7 %terms.4 = (bf16[1152,1408]{1,0:T(8,128)(2,1)S(1)}, bf16[1152,1024]{1,0:T(8,128)(2,1)S(1)}) custom-call(s32[12]{0:T(128)S(1)} %stack.51.place_ref.spot_ref.refs_2_.refs_5_, bf16[2,1152,128]{2,1,0:T(8,128)(2,1)S(1)} %get-tuple-element.30.refs_0_, bf16[2,1152,128]{2,1,0:T(8,128)(2,1)S(1)} %collective-permute-done.refs_3_.refs_1_, ...), custom_call_target="tpu_custom_call" | custom-call | flops 1000 | bytes 21000000 | tf_op jit(solution)/shard_map/terms/pallas_call | solution.py:223
  84.5 5.7 %terms.5 = (bf16[1152,1408]{1,0:T(8,128)(2,1)S(1)}, bf16[1152,1024]{1,0:T(8,128)(2,1)S(1)}) custom-call(s32[12]{0:T(128)S(1)} %stack.51.place_ref.spot_ref.refs_2_.refs_5_, bf16[2,1152,128]{2,1,0:T(8,128)(2,1)S(1)} %get-tuple-element.30.refs_0_, bf16[2,1152,128]{2,1,0:T(8,128)(2,1)S(1)} %collective-permute-done.refs_3_.refs_1_, ...), custom_call_target="tpu_custom_call" | custom-call | flops 1000 | bytes 21000000 | tf_op jit(solution)/shard_map/terms/pallas_call | solution.py:223
  90.3 4.6 %terms.6.refs_3_ = bf16[1152,1408]{1,0:T(8,128)(2,1)S(1)} custom-call(bf16[1152,1024]{1,0:T(8,128)(2,1)S(1)} %get-tuple-element.36.whole_ref, bf16[336,1024]{1,0:T(8,128)(2,1)S(1)} %collective-permute-done.9.refs_0_, bf16[336,1024]{1,0:T(8,128)(2,1)S(1)} %collective-permute-done.10.refs_1_, bf16[672,1024]{1,0:T(8,128)(2,1)S(1)} %gate.1.refs_2_, ...), custom_call_target="tpu_custom_call" | custom-call | flops 1000 | bytes 21000000 | tf_op jit(solution)/shard_map/terms/pallas_call | solution.py:223
  96.7 2.0 %collective-permute-start.21 = (bf16[144,1408]{1,0:T(8,128)(2,1)S(1)}, bf16[144,1408]{1,0:T(8,128)(2,1)S(1)}, u32[]{:S(2)}, u32[]{:S(2)}) collective-permute-start(bf16[144,1408]{1,0:T(8,128)(2,1)S(1)} %get-tuple-element.46), channel_id=1, source_target_pairs={{0,16},{16,32},{32,48},{48,64},{64,80},{80,96},{96,112},{112,0},{1... | collective-permute-start | bytes 1216520 | tf_op jit(solution)/shard_map/ppermute | solution.py:331
  98.7 4.0 %collective-permute-start.22 = (bf16[144,1408]{1,0:T(8,128)(2,1)S(1)}, bf16[144,1408]{1,0:T(8,128)(2,1)S(1)}, u32[]{:S(2)}, u32[]{:S(2)}) collective-permute-start(bf16[144,1408]{1,0:T(8,128)(2,1)S(1)} %get-tuple-element.47), channel_id=1, source_target_pairs={{0,112},{16,0},{32,16},{48,32},{64,48},{80,64},{96,80},{112,96},{1... | collective-permute-start | bytes 1216520 | tf_op jit(solution)/shard_map/ppermute | solution.py:331
  102.7 4.5 %terms.7.refs_0_.refs_3_.keep_ref = bf16[1152,1408]{1,0:T(8,128)(2,1)S(1)} custom-call(bf16[1152,1024]{1,0:T(8,128)(2,1)S(1)} %get-tuple-element.35.whole_ref, bf16[336,1024]{1,0:T(8,128)(2,1)S(1)} %collective-permute-done.9.refs_0_, bf16[336,1024]{1,0:T(8,128)(2,1)S(1)} %collective-permute-done.10.refs_1_, bf16[672,1024]{1,0:T(8,128)(2,1)S(1)} %gate.1.refs_2_, ...), custom_call_target="tpu_custom_call" | custom-call | flops 1000 | bytes 21000000 | tf_op jit(solution)/shard_map/terms/pallas_call | solution.py:223
  108.6 2.0 %collective-permute-start.12 = (bf16[144,1408]{1,0:T(8,128)(2,1)S(1)}, bf16[144,1408]{1,0:T(8,128)(2,1)S(1)}, u32[]{:S(2)}, u32[]{:S(2)}) collective-permute-start(bf16[144,1408]{1,0:T(8,128)(2,1)S(1)} %get-tuple-element.38), channel_id=1, source_target_pairs={{0,112},{16,0},{32,16},{48,32},{64,48},{80,64},{96,80},{112,96},{1... | collective-permute-start | bytes 1216520 | tf_op jit(solution)/shard_map/ppermute | solution.py:331
  110.7 1.5 collective-permute-done.21.refs_2_
  113.8 3.4 %collective-permute-start.24 = (bf16[144,1408]{1,0:T(8,128)(2,1)S(1)}, bf16[144,1408]{1,0:T(8,128)(2,1)S(1)}, u32[]{:S(2)}, u32[]{:S(2)}) collective-permute-start(bf16[144,1408]{1,0:T(8,128)(2,1)S(1)} %get-tuple-element.49), channel_id=1, source_target_pairs={{0,112},{16,0},{32,16},{48,32},{64,48},{80,64},{96,80},{112,96},{1... | collective-permute-start | bytes 1216520 | tf_op jit(solution)/shard_map/ppermute | solution.py:331
  117.2 4.0 %collective-permute-done.12.refs_2_ = bf16[144,1408]{1,0:T(8,128)(2,1)S(1)} collective-permute-done((bf16[144,1408]{1,0:T(8,128)(2,1)S(1)}, bf16[144,1408]{1,0:T(8,128)(2,1)S(1)}, u32[]{:S(2)}, u32[]{:S(2)}) %collective-permute-start.12) | collective-permute-done | bytes 405536 | tf_op jit(solution)/shard_map/ppermute | solution.py:331
  121.2 2.9 %collective-permute-done.13.refs_5_ = bf16[144,1408]{1,0:T(8,128)(2,1)S(1)} collective-permute-done((bf16[144,1408]{1,0:T(8,128)(2,1)S(1)}, bf16[144,1408]{1,0:T(8,128)(2,1)S(1)}, u32[]{:S(2)}, u32[]{:S(2)}) %collective-permute-start.13) | collective-permute-done | bytes 405536 | tf_op jit(solution)/shard_map/ppermute | solution.py:331
  127.0 5.7 %collective-permute-done.23.refs_2_ = bf16[144,1408]{1,0:T(8,128)(2,1)S(1)} collective-permute-done((bf16[144,1408]{1,0:T(8,128)(2,1)S(1)}, bf16[144,1408]{1,0:T(8,128)(2,1)S(1)}, u32[]{:S(2)}, u32[]{:S(2)}) %collective-permute-start.23) | collective-permute-done | bytes 405536 | tf_op jit(solution)/shard_map/ppermute | solution.py:331
  134.0 3.7 %collective-permute-done.14.refs_2_ = bf16[144,1408]{1,0:T(8,128)(2,1)S(1)} collective-permute-done((bf16[144,1408]{1,0:T(8,128)(2,1)S(1)}, bf16[144,1408]{1,0:T(8,128)(2,1)S(1)}, u32[]{:S(2)}, u32[]{:S(2)}) %collective-permute-start.14) | collective-permute-done | bytes 405536 | tf_op jit(solution)/shard_map/ppermute | solution.py:331
  137.6 3.9 %collective-permute-done.15.refs_5_ = bf16[144,1408]{1,0:T(8,128)(2,1)S(1)} collective-permute-done((bf16[144,1408]{1,0:T(8,128)(2,1)S(1)}, bf16[144,1408]{1,0:T(8,128)(2,1)S(1)}, u32[]{:S(2)}, u32[]{:S(2)}) %collective-permute-start.15) | collective-permute-done | bytes 405536 | tf_op jit(solution)/shard_map/ppermute | solution.py:331
  143.4 4.9 %collective-permute-done.25.refs_2_ = bf16[144,1408]{1,0:T(8,128)(2,1)S(1)} collective-permute-done((bf16[144,1408]{1,0:T(8,128)(2,1)S(1)}, bf16[144,1408]{1,0:T(8,128)(2,1)S(1)}, u32[]{:S(2)}, u32[]{:S(2)}) %collective-permute-start.25) | collective-permute-done | bytes 405536 | tf_op jit(solution)/shard_map/ppermute | solution.py:331
  149.2 5.5 %collective-permute-done.16.refs_2_ = bf16[144,1408]{1,0:T(8,128)(2,1)S(1)} collective-permute-done((bf16[144,1408]{1,0:T(8,128)(2,1)S(1)}, bf16[144,1408]{1,0:T(8,128)(2,1)S(1)}, u32[]{:S(2)}, u32[]{:S(2)}) %collective-permute-start.16) | collective-permute-done | bytes 405536 | tf_op jit(solution)/shard_map/ppermute | solution.py:331
  156.9 6.3 %collective-permute-done.27.two_ref = bf16[144,1408]{1,0:T(8,128)(2,1)S(1)} collective-permute-done((bf16[144,1408]{1,0:T(8,128)(2,1)S(1)}, bf16[144,1408]{1,0:T(8,128)(2,1)S(1)}, u32[]{:S(2)}, u32[]{:S(2)}) %collective-permute-start.27) | collective-permute-done | bytes 405536 | tf_op jit(solution)/shard_map/ppermute | solution.py:331
  165.5 2.5 %collective-permute-start.29 = (bf16[72,672]{1,0:T(8,128)(2,1)S(1)}, bf16[72,672]{1,0:T(8,128)(2,1)S(1)}, u32[]{:S(2)}, u32[]{:S(2)}) collective-permute-start(bf16[72,672]{1,0:T(8,128)(2,1)S(1)} %get-tuple-element.53), channel_id=1, source_target_pairs={{0,134},{2,128},{4,130},{6,132},{128,6},{130,0},{132,2},{134,4},{1... | collective-permute-start | bytes 290312 | tf_op jit(solution)/shard_map/ppermute | solution.py:483
  171.4 3.2 %collective-permute-start.30 = (bf16[72,672]{1,0:T(8,128)(2,1)S(1)}, bf16[72,672]{1,0:T(8,128)(2,1)S(1)}, u32[]{:S(2)}, u32[]{:S(2)}) collective-permute-start(bf16[72,672]{1,0:T(8,128)(2,1)S(1)} %get-tuple-element.54), channel_id=1, source_target_pairs={{0,4},{2,6},{4,0},{6,2},{1,5},{3,7},{5,1},{7,3},{8,12},{10,14},{12... | collective-permute-start | bytes 290312 | tf_op jit(solution)/shard_map/ppermute | solution.py:331
  175.9 2.4 %collective-permute-done.30.refs_4_ = bf16[72,672]{1,0:T(8,128)(2,1)S(1)} collective-permute-done((bf16[72,672]{1,0:T(8,128)(2,1)S(1)}, bf16[72,672]{1,0:T(8,128)(2,1)S(1)}, u32[]{:S(2)}, u32[]{:S(2)}) %collective-permute-start.30) | collective-permute-done | bytes 96800 | tf_op jit(solution)/shard_map/ppermute | solution.py:331
  178.3 3.5 %collective-permute-done.31.refs_5_ = bf16[72,672]{1,0:T(8,128)(2,1)S(1)} collective-permute-done((bf16[72,672]{1,0:T(8,128)(2,1)S(1)}, bf16[72,672]{1,0:T(8,128)(2,1)S(1)}, u32[]{:S(2)}, u32[]{:S(2)}) %collective-permute-start.31) | collective-permute-done | bytes 96800 | tf_op jit(solution)/shard_map/ppermute | solution.py:483
  181.8 1.7 finish.1
  (77 shorter events, 27.0 us)
Async XLA Ops:
  4.2 23.7 %collective-permute-start = (bf16[2,1152,128]{2,1,0:T(8,128)(2,1)S(1)}, bf16[2,1152,128]{2,1,0:T(8,128)(2,1)S(1)}, u32[]{:S(2)}, u32[]{:S(2)}) collective-permute-start(bf16[2,1152,128]{2,1,0:T(8,128)(2,1)S(1)} %get-tuple-element.30.refs_0_), channel_id=1, source_target_pairs={{0,1},{1,0},{2,3},{3,2},{4,5},{5,4},{6,7},{7,6},{8,9},{9,8},{10,11... | collective-permute-start | bytes 1769480 | tf_op jit(solution)/shard_map/ppermute | solution.py:331
  7.3 20.6 %collective-permute-start.1 = (bf16[2,1152,128]{2,1,0:T(8,128)(2,1)S(1)}, bf16[2,1152,128]{2,1,0:T(8,128)(2,1)S(1)}, u32[]{:S(2)}, u32[]{:S(2)}) collective-permute-start(bf16[2,1152,128]{2,1,0:T(8,128)(2,1)S(1)} %get-tuple-element.31), channel_id=1, source_target_pairs={{0,2},{2,4},{4,6},{6,0},{1,3},{3,5},{5,7},{7,1},{8,10},{10,12},{12... | collective-permute-start | bytes 1769480 | tf_op jit(solution)/shard_map/ppermute | solution.py:331
  8.9 19.0 %collective-permute-start.3 = (bf16[2,1152,128]{2,1,0:T(8,128)(2,1)S(1)}, bf16[2,1152,128]{2,1,0:T(8,128)(2,1)S(1)}, u32[]{:S(2)}, u32[]{:S(2)}) collective-permute-start(bf16[2,1152,128]{2,1,0:T(8,128)(2,1)S(1)} %get-tuple-element.32), channel_id=1, source_target_pairs={{0,6},{2,0},{4,2},{6,4},{1,7},{3,1},{5,3},{7,5},{8,14},{10,8},{12,... | collective-permute-start | bytes 1769480 | tf_op jit(solution)/shard_map/ppermute | solution.py:331
  9.3 27.4 %collective-permute-start.5 = (bf16[2,1152,128]{2,1,0:T(8,128)(2,1)S(1)}, bf16[2,1152,128]{2,1,0:T(8,128)(2,1)S(1)}, u32[]{:S(2)}, u32[]{:S(2)}) collective-permute-start(bf16[2,1152,128]{2,1,0:T(8,128)(2,1)S(1)} %get-tuple-element.33), channel_id=1, source_target_pairs={{0,4},{2,6},{4,0},{6,2},{1,5},{3,7},{5,1},{7,3},{8,12},{10,14},{12... | collective-permute-start | bytes 1769480 | tf_op jit(solution)/shard_map/ppermute | solution.py:331
  36.7 30.4 %collective-permute-start.8 = (bf16[672,1024]{1,0:T(8,128)(2,1)S(1)}, bf16[672,1024]{1,0:T(8,128)(2,1)S(1)}, u32[]{:S(2)}, u32[]{:S(2)}) collective-permute-start(bf16[672,1024]{1,0:T(8,128)(2,1)S(1)} %gate.1.refs_2_), channel_id=1, source_target_pairs={{0,6},{2,0},{4,2},{6,4},{1,7},{3,1},{5,3},{7,5},{8,14},{10,8},{12,... | collective-permute-start | bytes 4128776 | tf_op jit(solution)/shard_map/ppermute | solution.py:331
  37.6 30.9 %collective-permute-start.7 = (bf16[672,1024]{1,0:T(8,128)(2,1)S(1)}, bf16[672,1024]{1,0:T(8,128)(2,1)S(1)}, u32[]{:S(2)}, u32[]{:S(2)}) collective-permute-start(bf16[672,1024]{1,0:T(8,128)(2,1)S(1)} %gate.1.refs_2_), channel_id=1, source_target_pairs={{0,2},{2,4},{4,6},{6,0},{1,3},{3,5},{5,7},{7,1},{8,10},{10,12},{12... | collective-permute-start | bytes 4128776 | tf_op jit(solution)/shard_map/ppermute | solution.py:331
  38.7 30.7 %collective-permute-start.2 = (bf16[2,1152,128]{2,1,0:T(8,128)(2,1)S(1)}, bf16[2,1152,128]{2,1,0:T(8,128)(2,1)S(1)}, u32[]{:S(2)}, u32[]{:S(2)}) collective-permute-start(bf16[2,1152,128]{2,1,0:T(8,128)(2,1)S(1)} %collective-permute-done.1.refs_0_.refs_2_), channel_id=1, source_target_pairs={{0,1},{1,0},{2,3},{3,2},{4,5},{5,4},{6,7},{7,6},{8,9},{9,8},{10,11... | collective-permute-start | bytes 1769480 | tf_op jit(solution)/shard_map/ppermute | solution.py:331
  39.3 30.2 %collective-permute-start.4 = (bf16[2,1152,128]{2,1,0:T(8,128)(2,1)S(1)}, bf16[2,1152,128]{2,1,0:T(8,128)(2,1)S(1)}, u32[]{:S(2)}, u32[]{:S(2)}) collective-permute-start(bf16[2,1152,128]{2,1,0:T(8,128)(2,1)S(1)} %collective-permute-done.3.refs_1_.refs_4_), channel_id=1, source_target_pairs={{0,1},{1,0},{2,3},{3,2},{4,5},{5,4},{6,7},{7,6},{8,9},{9,8},{10,11... | collective-permute-start | bytes 1769480 | tf_op jit(solution)/shard_map/ppermute | solution.py:331
  42.3 36.3 %collective-permute-start.6 = (bf16[2,1152,128]{2,1,0:T(8,128)(2,1)S(1)}, bf16[2,1152,128]{2,1,0:T(8,128)(2,1)S(1)}, u32[]{:S(2)}, u32[]{:S(2)}) collective-permute-start(bf16[2,1152,128]{2,1,0:T(8,128)(2,1)S(1)} %collective-permute-done.5.refs_2_.refs_6_), channel_id=1, source_target_pairs={{0,1},{1,0},{2,3},{3,2},{4,5},{5,4},{6,7},{7,6},{8,9},{9,8},{10,11... | collective-permute-start | bytes 1769480 | tf_op jit(solution)/shard_map/ppermute | solution.py:331
  67.2 23.0 %collective-permute-start.10 = (bf16[336,1024]{1,0:T(8,128)(2,1)S(1)}, bf16[336,1024]{1,0:T(8,128)(2,1)S(1)}, u32[]{:S(2)}, u32[]{:S(2)}) collective-permute-start(bf16[336,1024]{1,0:T(8,128)(2,1)S(1)} %slice.9), channel_id=1, source_target_pairs={{0,6},{2,0},{4,2},{6,4},{1,7},{3,1},{5,3},{7,5},{8,14},{10,8},{12,... | collective-permute-start | bytes 2064392 | tf_op jit(solution)/shard_map/ppermute | solution.py:331
  68.5 21.7 %collective-permute-start.9 = (bf16[336,1024]{1,0:T(8,128)(2,1)S(1)}, bf16[336,1024]{1,0:T(8,128)(2,1)S(1)}, u32[]{:S(2)}, u32[]{:S(2)}) collective-permute-start(bf16[336,1024]{1,0:T(8,128)(2,1)S(1)} %slice.8), channel_id=1, source_target_pairs={{0,2},{2,4},{4,6},{6,0},{1,3},{3,5},{5,7},{7,1},{8,10},{10,12},{12... | collective-permute-start | bytes 2064392 | tf_op jit(solution)/shard_map/ppermute | solution.py:331
  84.2 11.2 %collective-permute-start.20 = (bf16[1152,1408]{1,0:T(8,128)(2,1)S(1)}, bf16[1152,1408]{1,0:T(8,128)(2,1)S(1)}, u32[]{:S(2)}, u32[]{:S(2)}) collective-permute-start(bf16[1152,1408]{1,0:T(8,128)(2,1)S(1)} %get-tuple-element.34.refs_10_), channel_id=1, source_target_pairs={{0,8},{8,0},{1,9},{9,1},{2,10},{10,2},{3,11},{11,3},{4,12},{12,4},... | collective-permute-start | bytes 9732104 | tf_op jit(solution)/shard_map/ppermute | solution.py:331
  94.8 12.4 %collective-permute-start.11 = (bf16[1152,1408]{1,0:T(8,128)(2,1)S(1)}, bf16[1152,1408]{1,0:T(8,128)(2,1)S(1)}, u32[]{:S(2)}, u32[]{:S(2)}) collective-permute-start(bf16[1152,1408]{1,0:T(8,128)(2,1)S(1)} %terms.6.refs_3_), channel_id=1, source_target_pairs={{0,8},{8,0},{1,9},{9,1},{2,10},{10,2},{3,11},{11,3},{4,12},{12,4},... | collective-permute-start | bytes 9732104 | tf_op jit(solution)/shard_map/ppermute | solution.py:331
  96.7 15.5 %collective-permute-start.21 = (bf16[144,1408]{1,0:T(8,128)(2,1)S(1)}, bf16[144,1408]{1,0:T(8,128)(2,1)S(1)}, u32[]{:S(2)}, u32[]{:S(2)}) collective-permute-start(bf16[144,1408]{1,0:T(8,128)(2,1)S(1)} %get-tuple-element.46), channel_id=1, source_target_pairs={{0,16},{16,32},{32,48},{48,64},{64,80},{80,96},{96,112},{112,0},{1... | collective-permute-start | bytes 1216520 | tf_op jit(solution)/shard_map/ppermute | solution.py:331
  98.7 13.8 %collective-permute-start.22 = (bf16[144,1408]{1,0:T(8,128)(2,1)S(1)}, bf16[144,1408]{1,0:T(8,128)(2,1)S(1)}, u32[]{:S(2)}, u32[]{:S(2)}) collective-permute-start(bf16[144,1408]{1,0:T(8,128)(2,1)S(1)} %get-tuple-element.47), channel_id=1, source_target_pairs={{0,112},{16,0},{32,16},{48,32},{64,48},{80,64},{96,80},{112,96},{1... | collective-permute-start | bytes 1216520 | tf_op jit(solution)/shard_map/ppermute | solution.py:331
  108.6 12.6 %collective-permute-start.12 = (bf16[144,1408]{1,0:T(8,128)(2,1)S(1)}, bf16[144,1408]{1,0:T(8,128)(2,1)S(1)}, u32[]{:S(2)}, u32[]{:S(2)}) collective-permute-start(bf16[144,1408]{1,0:T(8,128)(2,1)S(1)} %get-tuple-element.38), channel_id=1, source_target_pairs={{0,112},{16,0},{32,16},{48,32},{64,48},{80,64},{96,80},{112,96},{1... | collective-permute-start | bytes 1216520 | tf_op jit(solution)/shard_map/ppermute | solution.py:331
  110.6 13.5 %collective-permute-start.13 = (bf16[144,1408]{1,0:T(8,128)(2,1)S(1)}, bf16[144,1408]{1,0:T(8,128)(2,1)S(1)}, u32[]{:S(2)}, u32[]{:S(2)}) collective-permute-start(bf16[144,1408]{1,0:T(8,128)(2,1)S(1)} %get-tuple-element.39), channel_id=1, source_target_pairs={{0,16},{16,32},{32,48},{48,64},{64,80},{80,96},{96,112},{112,0},{1... | collective-permute-start | bytes 1216520 | tf_op jit(solution)/shard_map/ppermute | solution.py:331
  113.3 19.5 %collective-permute-start.23 = (bf16[144,1408]{1,0:T(8,128)(2,1)S(1)}, bf16[144,1408]{1,0:T(8,128)(2,1)S(1)}, u32[]{:S(2)}, u32[]{:S(2)}) collective-permute-start(bf16[144,1408]{1,0:T(8,128)(2,1)S(1)} %get-tuple-element.48), channel_id=1, source_target_pairs={{0,16},{16,32},{32,48},{48,64},{64,80},{80,96},{96,112},{112,0},{1... | collective-permute-start | bytes 1216520 | tf_op jit(solution)/shard_map/ppermute | solution.py:331
  113.8 19.0 %collective-permute-start.24 = (bf16[144,1408]{1,0:T(8,128)(2,1)S(1)}, bf16[144,1408]{1,0:T(8,128)(2,1)S(1)}, u32[]{:S(2)}, u32[]{:S(2)}) collective-permute-start(bf16[144,1408]{1,0:T(8,128)(2,1)S(1)} %get-tuple-element.49), channel_id=1, source_target_pairs={{0,112},{16,0},{32,16},{48,32},{64,48},{80,64},{96,80},{112,96},{1... | collective-permute-start | bytes 1216520 | tf_op jit(solution)/shard_map/ppermute | solution.py:331
  124.9 12.7 %collective-permute-start.14 = (bf16[144,1408]{1,0:T(8,128)(2,1)S(1)}, bf16[144,1408]{1,0:T(8,128)(2,1)S(1)}, u32[]{:S(2)}, u32[]{:S(2)}) collective-permute-start(bf16[144,1408]{1,0:T(8,128)(2,1)S(1)} %get-tuple-element.40), channel_id=1, source_target_pairs={{0,112},{16,0},{32,16},{48,32},{64,48},{80,64},{96,80},{112,96},{1... | collective-permute-start | bytes 1216520 | tf_op jit(solution)/shard_map/ppermute | solution.py:331
  125.8 15.7 %collective-permute-start.15 = (bf16[144,1408]{1,0:T(8,128)(2,1)S(1)}, bf16[144,1408]{1,0:T(8,128)(2,1)S(1)}, u32[]{:S(2)}, u32[]{:S(2)}) collective-permute-start(bf16[144,1408]{1,0:T(8,128)(2,1)S(1)} %get-tuple-element.41), channel_id=1, source_target_pairs={{0,16},{16,32},{32,48},{48,64},{64,80},{80,96},{96,112},{112,0},{1... | collective-permute-start | bytes 1216520 | tf_op jit(solution)/shard_map/ppermute | solution.py:331
  133.6 14.7 %collective-permute-start.25 = (bf16[144,1408]{1,0:T(8,128)(2,1)S(1)}, bf16[144,1408]{1,0:T(8,128)(2,1)S(1)}, u32[]{:S(2)}, u32[]{:S(2)}) collective-permute-start(bf16[144,1408]{1,0:T(8,128)(2,1)S(1)} %get-tuple-element.50), channel_id=1, source_target_pairs={{0,16},{16,32},{32,48},{48,64},{64,80},{80,96},{96,112},{112,0},{1... | collective-permute-start | bytes 1216520 | tf_op jit(solution)/shard_map/ppermute | solution.py:331
  142.3 12.4 %collective-permute-start.16 = (bf16[144,1408]{1,0:T(8,128)(2,1)S(1)}, bf16[144,1408]{1,0:T(8,128)(2,1)S(1)}, u32[]{:S(2)}, u32[]{:S(2)}) collective-permute-start(bf16[144,1408]{1,0:T(8,128)(2,1)S(1)} %get-tuple-element.42), channel_id=1, source_target_pairs={{0,112},{16,0},{32,16},{48,32},{64,48},{80,64},{96,80},{112,96},{1... | collective-permute-start | bytes 1216520 | tf_op jit(solution)/shard_map/ppermute | solution.py:331
  142.4 20.7 %collective-permute-start.27 = (bf16[144,1408]{1,0:T(8,128)(2,1)S(1)}, bf16[144,1408]{1,0:T(8,128)(2,1)S(1)}, u32[]{:S(2)}, u32[]{:S(2)}) collective-permute-start(bf16[144,1408]{1,0:T(8,128)(2,1)S(1)} %get-tuple-element.51), channel_id=1, source_target_pairs={{0,112},{16,0},{32,16},{48,32},{64,48},{80,64},{96,80},{112,96},{1... | collective-permute-start | bytes 1216520 | tf_op jit(solution)/shard_map/ppermute | solution.py:331
  149.0 14.1 %collective-permute-start.26 = (bf16[144,1408]{1,0:T(8,128)(2,1)S(1)}, bf16[144,1408]{1,0:T(8,128)(2,1)S(1)}, u32[]{:S(2)}, u32[]{:S(2)}) collective-permute-start(bf16[144,1408]{1,0:T(8,128)(2,1)S(1)} %loads.15), channel_id=1, source_target_pairs={{0,16},{16,32},{32,48},{48,64},{64,80},{80,96},{96,112},{112,0},{1... | collective-permute-start | bytes 1216520 | tf_op jit(solution)/shard_map/ppermute | solution.py:331
  149.2 19.4 %collective-permute-start.18 = (bf16[144,1408]{1,0:T(8,128)(2,1)S(1)}, bf16[144,1408]{1,0:T(8,128)(2,1)S(1)}, u32[]{:S(2)}, u32[]{:S(2)}) collective-permute-start(bf16[144,1408]{1,0:T(8,128)(2,1)S(1)} %get-tuple-element.43), channel_id=1, source_target_pairs={{0,16},{16,32},{32,48},{48,64},{64,80},{80,96},{96,112},{112,0},{1... | collective-permute-start | bytes 1216520 | tf_op jit(solution)/shard_map/ppermute | solution.py:331
  155.4 13.8 %collective-permute-start.17 = (bf16[144,1408]{1,0:T(8,128)(2,1)S(1)}, bf16[144,1408]{1,0:T(8,128)(2,1)S(1)}, u32[]{:S(2)}, u32[]{:S(2)}) collective-permute-start(bf16[144,1408]{1,0:T(8,128)(2,1)S(1)} %loads.11), channel_id=1, source_target_pairs={{0,112},{16,0},{32,16},{48,32},{64,48},{80,64},{96,80},{112,96},{1... | collective-permute-start | bytes 1216520 | tf_op jit(solution)/shard_map/ppermute | solution.py:331
  164.2 7.2 %collective-permute-start.28 = (bf16[72,672]{1,0:T(8,128)(2,1)S(1)}, bf16[72,672]{1,0:T(8,128)(2,1)S(1)}, u32[]{:S(2)}, u32[]{:S(2)}) collective-permute-start(bf16[72,672]{1,0:T(8,128)(2,1)S(1)} %get-tuple-element.52), channel_id=1, source_target_pairs={{0,6},{2,0},{4,2},{6,4},{1,7},{3,1},{5,3},{7,5},{8,14},{10,8},{12,... | collective-permute-start | bytes 290312 | tf_op jit(solution)/shard_map/ppermute | solution.py:331
  165.5 9.2 %collective-permute-start.29 = (bf16[72,672]{1,0:T(8,128)(2,1)S(1)}, bf16[72,672]{1,0:T(8,128)(2,1)S(1)}, u32[]{:S(2)}, u32[]{:S(2)}) collective-permute-start(bf16[72,672]{1,0:T(8,128)(2,1)S(1)} %get-tuple-element.53), channel_id=1, source_target_pairs={{0,134},{2,128},{4,130},{6,132},{128,6},{130,0},{132,2},{134,4},{1... | collective-permute-start | bytes 290312 | tf_op jit(solution)/shard_map/ppermute | solution.py:483
  167.9 7.7 %collective-permute-start.32 = (bf16[72,672]{1,0:T(8,128)(2,1)S(1)}, bf16[72,672]{1,0:T(8,128)(2,1)S(1)}, u32[]{:S(2)}, u32[]{:S(2)}) collective-permute-start(bf16[72,672]{1,0:T(8,128)(2,1)S(1)} %get-tuple-element.56), channel_id=1, source_target_pairs={{0,2},{2,4},{4,6},{6,0},{1,3},{3,5},{5,7},{7,1},{8,10},{10,12},{12... | collective-permute-start | bytes 290312 | tf_op jit(solution)/shard_map/ppermute | solution.py:331
  168.6 7.0 %collective-permute-start.33 = (bf16[72,672]{1,0:T(8,128)(2,1)S(1)}, bf16[72,672]{1,0:T(8,128)(2,1)S(1)}, u32[]{:S(2)}, u32[]{:S(2)}) collective-permute-start(bf16[72,672]{1,0:T(8,128)(2,1)S(1)} %get-tuple-element.57), channel_id=1, source_target_pairs={{0,130},{2,132},{4,134},{6,128},{128,2},{130,4},{132,6},{134,0},{1... | collective-permute-start | bytes 290312 | tf_op jit(solution)/shard_map/ppermute | solution.py:483
  174.6 7.2 %collective-permute-start.31 = (bf16[72,672]{1,0:T(8,128)(2,1)S(1)}, bf16[72,672]{1,0:T(8,128)(2,1)S(1)}, u32[]{:S(2)}, u32[]{:S(2)}) collective-permute-start(bf16[72,672]{1,0:T(8,128)(2,1)S(1)} %get-tuple-element.55), channel_id=1, source_target_pairs={{0,132},{2,134},{4,128},{6,130},{128,4},{130,6},{132,0},{134,2},{1... | collective-permute-start | bytes 290312 | tf_op jit(solution)/shard_map/ppermute | solution.py:483
  (10 other events, 80.2 us)

commit v5 on v4

--- a/solution.py
+++ b/solution.py
@@ -206,7 +206,7 @@
         for across in range(2):
             source = lax.rem(place_ref[0] + 4 - behind, 4) * 2 + lax.rem(place_ref[1] + across, 2)
             lane = pl.multiple_of(source * 128, 128)
-            whole_ref[:, pl.ds(lane, 128)] = pieces[at * 2 + across][0]
+            whole_ref[:, pl.ds(lane, 128)] = pieces[at + 4 * across][0]
     out_ref[...] = multiply(whole_ref[...], joined)
 
 
@@ -373,14 +373,9 @@
     )(place, *operands)
 
 
-def settle_kernel(spot_ref, keep_ref, got_ref, one_ref, two_ref, *refs):
+def settle_kernel(spot_ref, one_ref, two_ref, *refs):
     total = refs[-1]
-    total[...] = (
-        keep_ref[...].astype(jnp.float32)
-        + got_ref[...].astype(jnp.float32)
-        + one_ref[...].astype(jnp.float32)
-        + two_ref[...].astype(jnp.float32)
-    )
+    total[...] = one_ref[...].astype(jnp.float32) + two_ref[...].astype(jnp.float32)
     line = spot_ref[LINE_AT]
     for at, start in enumerate((line, 1 - line)):
         rows = total[pl.ds(pl.multiple_of(start * ROWS, 8), ROWS), :]
@@ -388,9 +383,8 @@
             refs[2 * at + block][...] = rows[:, block * WIDTH : (block + 1) * WIDTH].astype(NARROW)
 
 
-def settle(place, keep, got, one, two):
-    width = keep.shape[1]
-    local = pl.BlockSpec((PIECE, width), lambda i, spot: (spot[RING_AT], 0))
+def settle(place, one, two):
+    width = one.shape[1]
     whole = pl.BlockSpec((PIECE, width), lambda i, spot: (0, 0))
     out = pl.BlockSpec((ROWS, WIDTH), lambda i, spot: (0, 0))
     shape = jax.ShapeDtypeStruct((ROWS, WIDTH), NARROW)
@@ -400,14 +394,14 @@
         grid_spec=pltpu.PrefetchScalarGridSpec(
             num_scalar_prefetch=1,
             grid=(1,),
-            in_specs=[local, local, whole, whole],
+            in_specs=[whole, whole],
             out_specs=(out,) * 4,
             scratch_shapes=[pltpu.VMEM((PIECE, width), jnp.float32)],
         ),
         compiler_params=pltpu.CompilerParams(vmem_limit_bytes=6 * MIB),
         cost_estimate=cost(2),
         name="settle",
-    )(place, keep, got, one, two)
+    )(place, one, two)
 
 
 CHUNKS = ((1, 3), (2, 0))
@@ -433,9 +427,7 @@
     own = head_grads(queries, keys, teacher_attention_logits, document_length, [cut[0]])
     own = gate(own, held[1:] + swapped)
     swapped += [shifted(piece, "xh", 2, 1) for piece in held[1:]]
-    pieces = []
-    for pair in zip(held, swapped):
-        pieces += pair
+    pieces = held + swapped
     back = shifted(own, "y", 4, 1)
     fore = shifted(own, "y", 4, 3)
     half = WIDTH // 2
@@ -471,13 +463,14 @@
         for at, (keep, got) in enumerate(held_terms):
             way = 1 - 2 * at
             aheads = [(4 - slot) * way, (slot - 3) * way]
-            count = 2 if slot < 3 else 1
-            sums = loads(place, aheads[:count], keep, got, moving[at][:count])
-            for stream, load in enumerate(sums):
-                moving[at][stream] = shifted(load, "z", RINGS, -way if stream else way)
+            long_load, short_load = loads(place, aheads, keep, got, moving[at])
+            moving[at] = [
+                shifted(long_load, "z", RINGS, way),
+                short_load if slot == 3 else shifted(short_load, "z", RINGS, -way),
+            ]
     blocks = {}
-    for at, (keep, got) in enumerate(held_terms):
-        made = settle(place, keep, got, *moving[at])
+    for at in range(2):
+        made = settle(place, *moving[at])
         for behind, mine, other in zip(CHUNKS[at], made[:2], made[2:]):
             across = [(x * 4 + y, (1 - x) * 4 + (y - behind) % 4) for x in range(2) for y in range(4)]
             other = lax.ppermute(other, ("xl", "y"), across)

time: 184 us -> 184 us (level)
  starting transfers between devices: 43.2 us -> 49.3 us
  waiting for transfers between devices: 87.8 us -> 82.3 us
    ppermute x30, starting transfers between devices: 37.9 us -> 43.9 us  [shifted(): return lax.ppermute(x, axis, [(at, (at + by) % size) for at in range(size)])]
    ppermute x30, waiting for transfers between devices: 84.1 us -> 78.6 us  [shifted(): return lax.ppermute(x, axis, [(at, (at + by) % size) for at in range(size)])]
  transfers between devices with their start and end apart: 34 -> 34, of which waited for: 17 -> 17; matrix products, arithmetic and copies ran while one was open for 0% -> 0% of each run, Pallas kernels for 24% -> 23%
where the time goes in v5:
time: 184 us
  waiting for transfers between devices  82.3 us (45%)
  starting transfers between devices  49.3 us (27%)
  Pallas kernels  48.3 us (26%)
  local copies, waits for them, and re-layouts  3 us (2%)
    ppermute x30, waiting for transfers between devices, shifted(): return lax.ppermute(x, axis, [(at, (at + by) % size) for at in range(size)])  78.6 us
    ppermute x30, starting transfers between devices, shifted(): return lax.ppermute(x, axis, [(at, (at + by) % size) for at in range(size)])  43.9 us
    pallas_call x4, Pallas kernels, term_call(): pl.pallas_call(functools.partial(kernel, count), out_shape=out_shape, gri...  20.5 us
    pallas_call x1, Pallas kernels, head_grads(): pl.pallas_call(head_kernel, out_shape=jax.ShapeDtypeStruct(shape, NARROW)...  13.4 us
    pallas_call x8, Pallas kernels, loads(): pl.pallas_call(functools.partial(load_kernel, streams), out_shape=(shape,...  7.67 us
    ppermute x4, starting transfers between devices, on_device(): other = lax.ppermute(other, ('xl', 'y'), across)  5.37 us
    ppermute x4, waiting for transfers between devices, on_device(): other = lax.ppermute(other, ('xl', 'y'), across)  3.69 us
  transfers between devices with their start and end apart: 34, of which 17 were waited for; matrix products, arithmetic and copies ran while one was open for 0% of the time, Pallas kernels for 23%

profile of v5, /device:TPU:8, one launch (start us, length us, event | category | flops | bytes accessed | tf_op | source)
XLA Modules:
  0.0 184.0 jit_solution(16294130041114667022)
XLA Ops:
  0.8 3.4 %turn.1 = (bf16[2,1152,128]{2,1,0:T(8,128)(2,1)S(1)}, bf16[2,1152,128]{2,1,0:T(8,128)(2,1)S(1)}, bf16[2,1152,128]{2,1,0:T(8,128)(2,1)S(1)}, bf16[2,1152,128]{2,1,0:T(8,128)(2,1)S(1)}) custom-call(s32[12]{0:T(128)S(1)} %stack.51.place_ref.spot_ref.refs_2_.refs_5_, bf16[2,64,9216]{2,1,0:T(8,128)(2,1)} %far_ref.1, bf16[2,64,9216]{2,1,0:T(8,128)(2,1)} %far_ref.1), custom_call_target="tpu_custom_call" | custom-call | flops 1000 | bytes 10500000 | tf_op jit(solution)/shard_map/turn/pallas_call | solution.py:163
  6.5 2.0 %collective-permute-start.2 = (bf16[2,1152,128]{2,1,0:T(8,128)(2,1)S(1)}, bf16[2,1152,128]{2,1,0:T(8,128)(2,1)S(1)}, u32[]{:S(2)}, u32[]{:S(2)}) collective-permute-start(bf16[2,1152,128]{2,1,0:T(8,128)(2,1)S(1)} %get-tuple-element.37), channel_id=1, source_target_pairs={{0,4},{2,6},{4,0},{6,2},{1,5},{3,7},{5,1},{7,3},{8,12},{10,14},{12... | collective-permute-start | bytes 1769480 | tf_op jit(solution)/shard_map/ppermute | solution.py:331
  8.6 3.0 %collective-permute-start.3 = (bf16[2,1152,128]{2,1,0:T(8,128)(2,1)S(1)}, bf16[2,1152,128]{2,1,0:T(8,128)(2,1)S(1)}, u32[]{:S(2)}, u32[]{:S(2)}) collective-permute-start(bf16[2,1152,128]{2,1,0:T(8,128)(2,1)S(1)} %get-tuple-element.34.refs_0_), channel_id=1, source_target_pairs={{0,1},{1,0},{2,3},{3,2},{4,5},{5,4},{6,7},{7,6},{8,9},{9,8},{10,11... | collective-permute-start | bytes 1769480 | tf_op jit(solution)/shard_map/ppermute | solution.py:331
  11.6 2.8 %copy-done = bf16[2,6,512,512]{3,2,1,0:T(8,128)(2,1)S(1)} copy-done((bf16[2,6,512,512]{3,2,1,0:T(8,128)(2,1)S(1)}, bf16[2,6,512,512]{3,2,1,0:T(8,128)(2,1)}, u32[]{:S(2)}) %copy-start) | copy-done | bytes 6291480
  14.4 13.4 %head_grads.1 = bf16[7,96,1024]{2,1,0:T(8,128)(2,1)S(1)} custom-call(s32[2,4]{1,0:T(2,128)S(1)} %copy-done.3, bf16[2,576,512]{2,1,0:T(8,128)(2,1)S(1)} %bitcast.16, bf16[2,96,512]{2,1,0:T(8,128)(2,1)S(1)} %bitcast.17, bf16[2,6,512,512]{3,2,1,0:T(8,128)(2,1)S(1)} %copy-done, bf16[2,1152,128]{2,1,0:T(8,128)(2,1)S(1)} %get-tuple-element.34.refs_0_), custom_call_target="tpu_custom_call" | custom-call | flops 1000 | bytes 49000000 | tf_op jit(solution)/shard_map/head_grads/pallas_call | solution.py:115
  27.8 6.1 %collective-permute-done.2.refs_2_.refs_3_ = bf16[2,1152,128]{2,1,0:T(8,128)(2,1)S(1)} collective-permute-done((bf16[2,1152,128]{2,1,0:T(8,128)(2,1)S(1)}, bf16[2,1152,128]{2,1,0:T(8,128)(2,1)S(1)}, u32[]{:S(2)}, u32[]{:S(2)}) %collective-permute-start.2) | collective-permute-done | bytes 589856 | tf_op jit(solution)/shard_map/ppermute | solution.py:331
  36.0 3.0 %collective-permute-start.4 = (bf16[2,1152,128]{2,1,0:T(8,128)(2,1)S(1)}, bf16[2,1152,128]{2,1,0:T(8,128)(2,1)S(1)}, u32[]{:S(2)}, u32[]{:S(2)}) collective-permute-start(bf16[2,1152,128]{2,1,0:T(8,128)(2,1)S(1)} %collective-permute-done.refs_0_.refs_1_), channel_id=1, source_target_pairs={{0,1},{1,0},{2,3},{3,2},{4,5},{5,4},{6,7},{7,6},{8,9},{9,8},{10,11... | collective-permute-start | bytes 1769480 | tf_op jit(solution)/shard_map/ppermute | solution.py:331
  39.5 3.0 %collective-permute-start.6 = (bf16[2,1152,128]{2,1,0:T(8,128)(2,1)S(1)}, bf16[2,1152,128]{2,1,0:T(8,128)(2,1)S(1)}, u32[]{:S(2)}, u32[]{:S(2)}) collective-permute-start(bf16[2,1152,128]{2,1,0:T(8,128)(2,1)S(1)} %collective-permute-done.2.refs_2_.refs_3_), channel_id=1, source_target_pairs={{0,1},{1,0},{2,3},{3,2},{4,5},{5,4},{6,7},{7,6},{8,9},{9,8},{10,11... | collective-permute-start | bytes 1769480 | tf_op jit(solution)/shard_map/ppermute | solution.py:331
  42.6 22.1 %collective-permute-done.8.refs_9_.refs_10_ = bf16[672,1024]{1,0:T(8,128)(2,1)S(1)} collective-permute-done((bf16[672,1024]{1,0:T(8,128)(2,1)S(1)}, bf16[672,1024]{1,0:T(8,128)(2,1)S(1)}, u32[]{:S(2)}, u32[]{:S(2)}) %collective-permute-start.8) | collective-permute-done | bytes 1376288 | tf_op jit(solution)/shard_map/ppermute | solution.py:331
  67.0 9.1 %collective-permute-done.6.refs_7_ = bf16[2,1152,128]{2,1,0:T(8,128)(2,1)S(1)} collective-permute-done((bf16[2,1152,128]{2,1,0:T(8,128)(2,1)S(1)}, bf16[2,1152,128]{2,1,0:T(8,128)(2,1)S(1)}, u32[]{:S(2)}, u32[]{:S(2)}) %collective-permute-start.6) | collective-permute-done | bytes 589856 | tf_op jit(solution)/shard_map/ppermute | solution.py:331
  76.1 5.7 %terms.4 = (bf16[1152,1408]{1,0:T(8,128)(2,1)S(1)}, bf16[1152,1024]{1,0:T(8,128)(2,1)S(1)}) custom-call(s32[12]{0:T(128)S(1)} %stack.51.place_ref.spot_ref.refs_2_.refs_5_, bf16[2,1152,128]{2,1,0:T(8,128)(2,1)S(1)} %get-tuple-element.34.refs_0_, bf16[2,1152,128]{2,1,0:T(8,128)(2,1)S(1)} %collective-permute-done.refs_0_.refs_1_, ...), custom_call_target="tpu_custom_call" | custom-call | flops 1000 | bytes 21000000 | tf_op jit(solution)/shard_map/terms/pallas_call | solution.py:223
  82.1 5.7 %terms.5 = (bf16[1152,1408]{1,0:T(8,128)(2,1)S(1)}, bf16[1152,1024]{1,0:T(8,128)(2,1)S(1)}) custom-call(s32[12]{0:T(128)S(1)} %stack.51.place_ref.spot_ref.refs_2_.refs_5_, bf16[2,1152,128]{2,1,0:T(8,128)(2,1)S(1)} %get-tuple-element.34.refs_0_, bf16[2,1152,128]{2,1,0:T(8,128)(2,1)S(1)} %collective-permute-done.refs_0_.refs_1_, ...), custom_call_target="tpu_custom_call" | custom-call | flops 1000 | bytes 21000000 | tf_op jit(solution)/shard_map/terms/pallas_call | solution.py:223
  87.8 4.6 %terms.6.refs_3_ = bf16[1152,1408]{1,0:T(8,128)(2,1)S(1)} custom-call(bf16[1152,1024]{1,0:T(8,128)(2,1)S(1)} %get-tuple-element.40.whole_ref, bf16[336,1024]{1,0:T(8,128)(2,1)S(1)} %collective-permute-done.9.refs_0_, bf16[336,1024]{1,0:T(8,128)(2,1)S(1)} %collective-permute-done.10.refs_1_, bf16[672,1024]{1,0:T(8,128)(2,1)S(1)} %gate.1.refs_2_, ...), custom_call_target="tpu_custom_call" | custom-call | flops 1000 | bytes 21000000 | tf_op jit(solution)/shard_map/terms/pallas_call | solution.py:223
  94.2 2.0 %collective-permute-start.21 = (bf16[144,1408]{1,0:T(8,128)(2,1)S(1)}, bf16[144,1408]{1,0:T(8,128)(2,1)S(1)}, u32[]{:S(2)}, u32[]{:S(2)}) collective-permute-start(bf16[144,1408]{1,0:T(8,128)(2,1)S(1)} %get-tuple-element.52), channel_id=1, source_target_pairs={{0,16},{16,32},{32,48},{48,64},{64,80},{80,96},{96,112},{112,0},{1... | collective-permute-start | bytes 1216520 | tf_op jit(solution)/shard_map/ppermute | solution.py:331
  96.2 4.0 %collective-permute-start.22 = (bf16[144,1408]{1,0:T(8,128)(2,1)S(1)}, bf16[144,1408]{1,0:T(8,128)(2,1)S(1)}, u32[]{:S(2)}, u32[]{:S(2)}) collective-permute-start(bf16[144,1408]{1,0:T(8,128)(2,1)S(1)} %get-tuple-element.53), channel_id=1, source_target_pairs={{0,112},{16,0},{32,16},{48,32},{64,48},{80,64},{96,80},{112,96},{1... | collective-permute-start | bytes 1216520 | tf_op jit(solution)/shard_map/ppermute | solution.py:331
  100.3 4.5 %terms.7.refs_0_.refs_3_ = bf16[1152,1408]{1,0:T(8,128)(2,1)S(1)} custom-call(bf16[1152,1024]{1,0:T(8,128)(2,1)S(1)} %get-tuple-element.39.whole_ref, bf16[336,1024]{1,0:T(8,128)(2,1)S(1)} %collective-permute-done.9.refs_0_, bf16[336,1024]{1,0:T(8,128)(2,1)S(1)} %collective-permute-done.10.refs_1_, bf16[672,1024]{1,0:T(8,128)(2,1)S(1)} %gate.1.refs_2_, ...), custom_call_target="tpu_custom_call" | custom-call | flops 1000 | bytes 21000000 | tf_op jit(solution)/shard_map/terms/pallas_call | solution.py:223
  106.1 2.0 %collective-permute-start.12 = (bf16[144,1408]{1,0:T(8,128)(2,1)S(1)}, bf16[144,1408]{1,0:T(8,128)(2,1)S(1)}, u32[]{:S(2)}, u32[]{:S(2)}) collective-permute-start(bf16[144,1408]{1,0:T(8,128)(2,1)S(1)} %get-tuple-element.42), channel_id=1, source_target_pairs={{0,112},{16,0},{32,16},{48,32},{64,48},{80,64},{96,80},{112,96},{1... | collective-permute-start | bytes 1216520 | tf_op jit(solution)/shard_map/ppermute | solution.py:331
  111.3 3.4 %collective-permute-start.24 = (bf16[144,1408]{1,0:T(8,128)(2,1)S(1)}, bf16[144,1408]{1,0:T(8,128)(2,1)S(1)}, u32[]{:S(2)}, u32[]{:S(2)}) collective-permute-start(bf16[144,1408]{1,0:T(8,128)(2,1)S(1)} %get-tuple-element.55), channel_id=1, source_target_pairs={{0,112},{16,0},{32,16},{48,32},{64,48},{80,64},{96,80},{112,96},{1... | collective-permute-start | bytes 1216520 | tf_op jit(solution)/shard_map/ppermute | solution.py:331
  114.7 4.0 %collective-permute-done.12.refs_2_ = bf16[144,1408]{1,0:T(8,128)(2,1)S(1)} collective-permute-done((bf16[144,1408]{1,0:T(8,128)(2,1)S(1)}, bf16[144,1408]{1,0:T(8,128)(2,1)S(1)}, u32[]{:S(2)}, u32[]{:S(2)}) %collective-permute-start.12) | collective-permute-done | bytes 405536 | tf_op jit(solution)/shard_map/ppermute | solution.py:331
  118.7 2.9 %collective-permute-done.13.refs_5_ = bf16[144,1408]{1,0:T(8,128)(2,1)S(1)} collective-permute-done((bf16[144,1408]{1,0:T(8,128)(2,1)S(1)}, bf16[144,1408]{1,0:T(8,128)(2,1)S(1)}, u32[]{:S(2)}, u32[]{:S(2)}) %collective-permute-start.13) | collective-permute-done | bytes 405536 | tf_op jit(solution)/shard_map/ppermute | solution.py:331
  124.6 5.7 %collective-permute-done.23.refs_2_ = bf16[144,1408]{1,0:T(8,128)(2,1)S(1)} collective-permute-done((bf16[144,1408]{1,0:T(8,128)(2,1)S(1)}, bf16[144,1408]{1,0:T(8,128)(2,1)S(1)}, u32[]{:S(2)}, u32[]{:S(2)}) %collective-permute-start.23) | collective-permute-done | bytes 405536 | tf_op jit(solution)/shard_map/ppermute | solution.py:331
  131.5 3.2 %collective-permute-start.26 = (bf16[144,1408]{1,0:T(8,128)(2,1)S(1)}, bf16[144,1408]{1,0:T(8,128)(2,1)S(1)}, u32[]{:S(2)}, u32[]{:S(2)}) collective-permute-start(bf16[144,1408]{1,0:T(8,128)(2,1)S(1)} %get-tuple-element.57), channel_id=1, source_target_pairs={{0,112},{16,0},{32,16},{48,32},{64,48},{80,64},{96,80},{112,96},{1... | collective-permute-start | bytes 1216520 | tf_op jit(solution)/shard_map/ppermute | solution.py:331
  136.1 2.9 %collective-permute-done.15.refs_5_ = bf16[144,1408]{1,0:T(8,128)(2,1)S(1)} collective-permute-done((bf16[144,1408]{1,0:T(8,128)(2,1)S(1)}, bf16[144,1408]{1,0:T(8,128)(2,1)S(1)}, u32[]{:S(2)}, u32[]{:S(2)}) %collective-permute-start.15) | collective-permute-done | bytes 405536 | tf_op jit(solution)/shard_map/ppermute | solution.py:331
  142.0 5.7 %collective-permute-done.25.refs_2_ = bf16[144,1408]{1,0:T(8,128)(2,1)S(1)} collective-permute-done((bf16[144,1408]{1,0:T(8,128)(2,1)S(1)}, bf16[144,1408]{1,0:T(8,128)(2,1)S(1)}, u32[]{:S(2)}, u32[]{:S(2)}) %collective-permute-start.25) | collective-permute-done | bytes 405536 | tf_op jit(solution)/shard_map/ppermute | solution.py:331
  148.7 3.8 %collective-permute-done.16.refs_2_ = bf16[144,1408]{1,0:T(8,128)(2,1)S(1)} collective-permute-done((bf16[144,1408]{1,0:T(8,128)(2,1)S(1)}, bf16[144,1408]{1,0:T(8,128)(2,1)S(1)}, u32[]{:S(2)}, u32[]{:S(2)}) %collective-permute-start.16) | collective-permute-done | bytes 405536 | tf_op jit(solution)/shard_map/ppermute | solution.py:331
  152.5 3.8 %collective-permute-done.17.refs_5_ = bf16[144,1408]{1,0:T(8,128)(2,1)S(1)} collective-permute-done((bf16[144,1408]{1,0:T(8,128)(2,1)S(1)}, bf16[144,1408]{1,0:T(8,128)(2,1)S(1)}, u32[]{:S(2)}, u32[]{:S(2)}) %collective-permute-start.17) | collective-permute-done | bytes 405536 | tf_op jit(solution)/shard_map/ppermute | solution.py:331
  157.6 5.7 %collective-permute-done.27.one_ref = bf16[144,1408]{1,0:T(8,128)(2,1)S(1)} collective-permute-done((bf16[144,1408]{1,0:T(8,128)(2,1)S(1)}, bf16[144,1408]{1,0:T(8,128)(2,1)S(1)}, u32[]{:S(2)}, u32[]{:S(2)}) %collective-permute-start.27) | collective-permute-done | bytes 405536 | tf_op jit(solution)/shard_map/ppermute | solution.py:331
  165.4 3.4 %collective-permute-start.29 = (bf16[72,672]{1,0:T(8,128)(2,1)S(1)}, bf16[72,672]{1,0:T(8,128)(2,1)S(1)}, u32[]{:S(2)}, u32[]{:S(2)}) collective-permute-start(bf16[72,672]{1,0:T(8,128)(2,1)S(1)} %get-tuple-element.61), channel_id=1, source_target_pairs={{0,134},{2,128},{4,130},{6,132},{128,6},{130,0},{132,2},{134,4},{1... | collective-permute-start | bytes 290312 | tf_op jit(solution)/shard_map/ppermute | solution.py:476
  171.5 3.7 %collective-permute-start.30 = (bf16[72,672]{1,0:T(8,128)(2,1)S(1)}, bf16[72,672]{1,0:T(8,128)(2,1)S(1)}, u32[]{:S(2)}, u32[]{:S(2)}) collective-permute-start(bf16[72,672]{1,0:T(8,128)(2,1)S(1)} %get-tuple-element.62), channel_id=1, source_target_pairs={{0,4},{2,6},{4,0},{6,2},{1,5},{3,7},{5,1},{7,3},{8,12},{10,14},{12... | collective-permute-start | bytes 290312 | tf_op jit(solution)/shard_map/ppermute | solution.py:331
  175.7 3.3 %collective-permute-done.30.refs_4_ = bf16[72,672]{1,0:T(8,128)(2,1)S(1)} collective-permute-done((bf16[72,672]{1,0:T(8,128)(2,1)S(1)}, bf16[72,672]{1,0:T(8,128)(2,1)S(1)}, u32[]{:S(2)}, u32[]{:S(2)}) %collective-permute-start.30) | collective-permute-done | bytes 96800 | tf_op jit(solution)/shard_map/ppermute | solution.py:331
  179.0 3.3 %collective-permute-done.31.refs_5_ = bf16[72,672]{1,0:T(8,128)(2,1)S(1)} collective-permute-done((bf16[72,672]{1,0:T(8,128)(2,1)S(1)}, bf16[72,672]{1,0:T(8,128)(2,1)S(1)}, u32[]{:S(2)}, u32[]{:S(2)}) %collective-permute-start.31) | collective-permute-done | bytes 96800 | tf_op jit(solution)/shard_map/ppermute | solution.py:476
  182.3 1.7 finish.1
  (77 shorter events, 29.7 us)
Async XLA Ops:
  4.2 23.6 %collective-permute-start = (bf16[2,1152,128]{2,1,0:T(8,128)(2,1)S(1)}, bf16[2,1152,128]{2,1,0:T(8,128)(2,1)S(1)}, u32[]{:S(2)}, u32[]{:S(2)}) collective-permute-start(bf16[2,1152,128]{2,1,0:T(8,128)(2,1)S(1)} %get-tuple-element.35), channel_id=1, source_target_pairs={{0,2},{2,4},{4,6},{6,0},{1,3},{3,5},{5,7},{7,1},{8,10},{10,12},{12... | collective-permute-start | bytes 1769480 | tf_op jit(solution)/shard_map/ppermute | solution.py:331
  5.8 22.0 %collective-permute-start.1 = (bf16[2,1152,128]{2,1,0:T(8,128)(2,1)S(1)}, bf16[2,1152,128]{2,1,0:T(8,128)(2,1)S(1)}, u32[]{:S(2)}, u32[]{:S(2)}) collective-permute-start(bf16[2,1152,128]{2,1,0:T(8,128)(2,1)S(1)} %get-tuple-element.36), channel_id=1, source_target_pairs={{0,6},{2,0},{4,2},{6,4},{1,7},{3,1},{5,3},{7,5},{8,14},{10,8},{12,... | collective-permute-start | bytes 1769480 | tf_op jit(solution)/shard_map/ppermute | solution.py:331
  6.5 27.4 %collective-permute-start.2 = (bf16[2,1152,128]{2,1,0:T(8,128)(2,1)S(1)}, bf16[2,1152,128]{2,1,0:T(8,128)(2,1)S(1)}, u32[]{:S(2)}, u32[]{:S(2)}) collective-permute-start(bf16[2,1152,128]{2,1,0:T(8,128)(2,1)S(1)} %get-tuple-element.37), channel_id=1, source_target_pairs={{0,4},{2,6},{4,0},{6,2},{1,5},{3,7},{5,1},{7,3},{8,12},{10,14},{12... | collective-permute-start | bytes 1769480 | tf_op jit(solution)/shard_map/ppermute | solution.py:331
  8.6 25.4 %collective-permute-start.3 = (bf16[2,1152,128]{2,1,0:T(8,128)(2,1)S(1)}, bf16[2,1152,128]{2,1,0:T(8,128)(2,1)S(1)}, u32[]{:S(2)}, u32[]{:S(2)}) collective-permute-start(bf16[2,1152,128]{2,1,0:T(8,128)(2,1)S(1)} %get-tuple-element.34.refs_0_), channel_id=1, source_target_pairs={{0,1},{1,0},{2,3},{3,2},{4,5},{5,4},{6,7},{7,6},{8,9},{9,8},{10,11... | collective-permute-start | bytes 1769480 | tf_op jit(solution)/shard_map/ppermute | solution.py:331
  34.0 30.7 %collective-permute-start.8 = (bf16[672,1024]{1,0:T(8,128)(2,1)S(1)}, bf16[672,1024]{1,0:T(8,128)(2,1)S(1)}, u32[]{:S(2)}, u32[]{:S(2)}) collective-permute-start(bf16[672,1024]{1,0:T(8,128)(2,1)S(1)} %gate.1.refs_2_), channel_id=1, source_target_pairs={{0,6},{2,0},{4,2},{6,4},{1,7},{3,1},{5,3},{7,5},{8,14},{10,8},{12,... | collective-permute-start | bytes 4128776 | tf_op jit(solution)/shard_map/ppermute | solution.py:331
  34.9 31.2 %collective-permute-start.7 = (bf16[672,1024]{1,0:T(8,128)(2,1)S(1)}, bf16[672,1024]{1,0:T(8,128)(2,1)S(1)}, u32[]{:S(2)}, u32[]{:S(2)}) collective-permute-start(bf16[672,1024]{1,0:T(8,128)(2,1)S(1)} %gate.1.refs_2_), channel_id=1, source_target_pairs={{0,2},{2,4},{4,6},{6,0},{1,3},{3,5},{5,7},{7,1},{8,10},{10,12},{12... | collective-permute-start | bytes 4128776 | tf_op jit(solution)/shard_map/ppermute | solution.py:331
  36.0 31.0 %collective-permute-start.4 = (bf16[2,1152,128]{2,1,0:T(8,128)(2,1)S(1)}, bf16[2,1152,128]{2,1,0:T(8,128)(2,1)S(1)}, u32[]{:S(2)}, u32[]{:S(2)}) collective-permute-start(bf16[2,1152,128]{2,1,0:T(8,128)(2,1)S(1)} %collective-permute-done.refs_0_.refs_1_), channel_id=1, source_target_pairs={{0,1},{1,0},{2,3},{3,2},{4,5},{5,4},{6,7},{7,6},{8,9},{9,8},{10,11... | collective-permute-start | bytes 1769480 | tf_op jit(solution)/shard_map/ppermute | solution.py:331
  39.0 28.0 %collective-permute-start.5 = (bf16[2,1152,128]{2,1,0:T(8,128)(2,1)S(1)}, bf16[2,1152,128]{2,1,0:T(8,128)(2,1)S(1)}, u32[]{:S(2)}, u32[]{:S(2)}) collective-permute-start(bf16[2,1152,128]{2,1,0:T(8,128)(2,1)S(1)} %collective-permute-done.1.refs_1_.refs_2_), channel_id=1, source_target_pairs={{0,1},{1,0},{2,3},{3,2},{4,5},{5,4},{6,7},{7,6},{8,9},{9,8},{10,11... | collective-permute-start | bytes 1769480 | tf_op jit(solution)/shard_map/ppermute | solution.py:331
  39.5 36.6 %collective-permute-start.6 = (bf16[2,1152,128]{2,1,0:T(8,128)(2,1)S(1)}, bf16[2,1152,128]{2,1,0:T(8,128)(2,1)S(1)}, u32[]{:S(2)}, u32[]{:S(2)}) collective-permute-start(bf16[2,1152,128]{2,1,0:T(8,128)(2,1)S(1)} %collective-permute-done.2.refs_2_.refs_3_), channel_id=1, source_target_pairs={{0,1},{1,0},{2,3},{3,2},{4,5},{5,4},{6,7},{7,6},{8,9},{9,8},{10,11... | collective-permute-start | bytes 1769480 | tf_op jit(solution)/shard_map/ppermute | solution.py:331
  64.8 23.1 %collective-permute-start.10 = (bf16[336,1024]{1,0:T(8,128)(2,1)S(1)}, bf16[336,1024]{1,0:T(8,128)(2,1)S(1)}, u32[]{:S(2)}, u32[]{:S(2)}) collective-permute-start(bf16[336,1024]{1,0:T(8,128)(2,1)S(1)} %slice.9), channel_id=1, source_target_pairs={{0,6},{2,0},{4,2},{6,4},{1,7},{3,1},{5,3},{7,5},{8,14},{10,8},{12,... | collective-permute-start | bytes 2064392 | tf_op jit(solution)/shard_map/ppermute | solution.py:331
  66.1 21.7 %collective-permute-start.9 = (bf16[336,1024]{1,0:T(8,128)(2,1)S(1)}, bf16[336,1024]{1,0:T(8,128)(2,1)S(1)}, u32[]{:S(2)}, u32[]{:S(2)}) collective-permute-start(bf16[336,1024]{1,0:T(8,128)(2,1)S(1)} %slice.8), channel_id=1, source_target_pairs={{0,2},{2,4},{4,6},{6,0},{1,3},{3,5},{5,7},{7,1},{8,10},{10,12},{12... | collective-permute-start | bytes 2064392 | tf_op jit(solution)/shard_map/ppermute | solution.py:331
  81.8 11.2 %collective-permute-start.20 = (bf16[1152,1408]{1,0:T(8,128)(2,1)S(1)}, bf16[1152,1408]{1,0:T(8,128)(2,1)S(1)}, u32[]{:S(2)}, u32[]{:S(2)}) collective-permute-start(bf16[1152,1408]{1,0:T(8,128)(2,1)S(1)} %get-tuple-element.38.refs_10_), channel_id=1, source_target_pairs={{0,8},{8,0},{1,9},{9,1},{2,10},{10,2},{3,11},{11,3},{4,12},{12,4},... | collective-permute-start | bytes 9732104 | tf_op jit(solution)/shard_map/ppermute | solution.py:331
  92.4 12.4 %collective-permute-start.11 = (bf16[1152,1408]{1,0:T(8,128)(2,1)S(1)}, bf16[1152,1408]{1,0:T(8,128)(2,1)S(1)}, u32[]{:S(2)}, u32[]{:S(2)}) collective-permute-start(bf16[1152,1408]{1,0:T(8,128)(2,1)S(1)} %terms.6.refs_3_), channel_id=1, source_target_pairs={{0,8},{8,0},{1,9},{9,1},{2,10},{10,2},{3,11},{11,3},{4,12},{12,4},... | collective-permute-start | bytes 9732104 | tf_op jit(solution)/shard_map/ppermute | solution.py:331
  94.2 15.5 %collective-permute-start.21 = (bf16[144,1408]{1,0:T(8,128)(2,1)S(1)}, bf16[144,1408]{1,0:T(8,128)(2,1)S(1)}, u32[]{:S(2)}, u32[]{:S(2)}) collective-permute-start(bf16[144,1408]{1,0:T(8,128)(2,1)S(1)} %get-tuple-element.52), channel_id=1, source_target_pairs={{0,16},{16,32},{32,48},{48,64},{64,80},{80,96},{96,112},{112,0},{1... | collective-permute-start | bytes 1216520 | tf_op jit(solution)/shard_map/ppermute | solution.py:331
  96.2 13.8 %collective-permute-start.22 = (bf16[144,1408]{1,0:T(8,128)(2,1)S(1)}, bf16[144,1408]{1,0:T(8,128)(2,1)S(1)}, u32[]{:S(2)}, u32[]{:S(2)}) collective-permute-start(bf16[144,1408]{1,0:T(8,128)(2,1)S(1)} %get-tuple-element.53), channel_id=1, source_target_pairs={{0,112},{16,0},{32,16},{48,32},{64,48},{80,64},{96,80},{112,96},{1... | collective-permute-start | bytes 1216520 | tf_op jit(solution)/shard_map/ppermute | solution.py:331
  106.1 12.6 %collective-permute-start.12 = (bf16[144,1408]{1,0:T(8,128)(2,1)S(1)}, bf16[144,1408]{1,0:T(8,128)(2,1)S(1)}, u32[]{:S(2)}, u32[]{:S(2)}) collective-permute-start(bf16[144,1408]{1,0:T(8,128)(2,1)S(1)} %get-tuple-element.42), channel_id=1, source_target_pairs={{0,112},{16,0},{32,16},{48,32},{64,48},{80,64},{96,80},{112,96},{1... | collective-permute-start | bytes 1216520 | tf_op jit(solution)/shard_map/ppermute | solution.py:331
  108.1 13.5 %collective-permute-start.13 = (bf16[144,1408]{1,0:T(8,128)(2,1)S(1)}, bf16[144,1408]{1,0:T(8,128)(2,1)S(1)}, u32[]{:S(2)}, u32[]{:S(2)}) collective-permute-start(bf16[144,1408]{1,0:T(8,128)(2,1)S(1)} %get-tuple-element.43), channel_id=1, source_target_pairs={{0,16},{16,32},{32,48},{48,64},{64,80},{80,96},{96,112},{112,0},{1... | collective-permute-start | bytes 1216520 | tf_op jit(solution)/shard_map/ppermute | solution.py:331
  110.9 19.5 %collective-permute-start.23 = (bf16[144,1408]{1,0:T(8,128)(2,1)S(1)}, bf16[144,1408]{1,0:T(8,128)(2,1)S(1)}, u32[]{:S(2)}, u32[]{:S(2)}) collective-permute-start(bf16[144,1408]{1,0:T(8,128)(2,1)S(1)} %get-tuple-element.54), channel_id=1, source_target_pairs={{0,16},{16,32},{32,48},{48,64},{64,80},{80,96},{96,112},{112,0},{1... | collective-permute-start | bytes 1216520 | tf_op jit(solution)/shard_map/ppermute | solution.py:331
  111.3 19.0 %collective-permute-start.24 = (bf16[144,1408]{1,0:T(8,128)(2,1)S(1)}, bf16[144,1408]{1,0:T(8,128)(2,1)S(1)}, u32[]{:S(2)}, u32[]{:S(2)}) collective-permute-start(bf16[144,1408]{1,0:T(8,128)(2,1)S(1)} %get-tuple-element.55), channel_id=1, source_target_pairs={{0,112},{16,0},{32,16},{48,32},{64,48},{80,64},{96,80},{112,96},{1... | collective-permute-start | bytes 1216520 | tf_op jit(solution)/shard_map/ppermute | solution.py:331
  122.5 13.6 %collective-permute-start.14 = (bf16[144,1408]{1,0:T(8,128)(2,1)S(1)}, bf16[144,1408]{1,0:T(8,128)(2,1)S(1)}, u32[]{:S(2)}, u32[]{:S(2)}) collective-permute-start(bf16[144,1408]{1,0:T(8,128)(2,1)S(1)} %get-tuple-element.44), channel_id=1, source_target_pairs={{0,112},{16,0},{32,16},{48,32},{64,48},{80,64},{96,80},{112,96},{1... | collective-permute-start | bytes 1216520 | tf_op jit(solution)/shard_map/ppermute | solution.py:331
  123.3 15.7 %collective-permute-start.15 = (bf16[144,1408]{1,0:T(8,128)(2,1)S(1)}, bf16[144,1408]{1,0:T(8,128)(2,1)S(1)}, u32[]{:S(2)}, u32[]{:S(2)}) collective-permute-start(bf16[144,1408]{1,0:T(8,128)(2,1)S(1)} %get-tuple-element.45), channel_id=1, source_target_pairs={{0,16},{16,32},{32,48},{48,64},{64,80},{80,96},{96,112},{112,0},{1... | collective-permute-start | bytes 1216520 | tf_op jit(solution)/shard_map/ppermute | solution.py:331
  131.2 16.5 %collective-permute-start.25 = (bf16[144,1408]{1,0:T(8,128)(2,1)S(1)}, bf16[144,1408]{1,0:T(8,128)(2,1)S(1)}, u32[]{:S(2)}, u32[]{:S(2)}) collective-permute-start(bf16[144,1408]{1,0:T(8,128)(2,1)S(1)} %get-tuple-element.56), channel_id=1, source_target_pairs={{0,16},{16,32},{32,48},{48,64},{64,80},{80,96},{96,112},{112,0},{1... | collective-permute-start | bytes 1216520 | tf_op jit(solution)/shard_map/ppermute | solution.py:331
  131.5 16.2 %collective-permute-start.26 = (bf16[144,1408]{1,0:T(8,128)(2,1)S(1)}, bf16[144,1408]{1,0:T(8,128)(2,1)S(1)}, u32[]{:S(2)}, u32[]{:S(2)}) collective-permute-start(bf16[144,1408]{1,0:T(8,128)(2,1)S(1)} %get-tuple-element.57), channel_id=1, source_target_pairs={{0,112},{16,0},{32,16},{48,32},{64,48},{80,64},{96,80},{112,96},{1... | collective-permute-start | bytes 1216520 | tf_op jit(solution)/shard_map/ppermute | solution.py:331
  139.9 12.7 %collective-permute-start.16 = (bf16[144,1408]{1,0:T(8,128)(2,1)S(1)}, bf16[144,1408]{1,0:T(8,128)(2,1)S(1)}, u32[]{:S(2)}, u32[]{:S(2)}) collective-permute-start(bf16[144,1408]{1,0:T(8,128)(2,1)S(1)} %get-tuple-element.46), channel_id=1, source_target_pairs={{0,112},{16,0},{32,16},{48,32},{64,48},{80,64},{96,80},{112,96},{1... | collective-permute-start | bytes 1216520 | tf_op jit(solution)/shard_map/ppermute | solution.py:331
  140.7 15.7 %collective-permute-start.17 = (bf16[144,1408]{1,0:T(8,128)(2,1)S(1)}, bf16[144,1408]{1,0:T(8,128)(2,1)S(1)}, u32[]{:S(2)}, u32[]{:S(2)}) collective-permute-start(bf16[144,1408]{1,0:T(8,128)(2,1)S(1)} %get-tuple-element.47), channel_id=1, source_target_pairs={{0,16},{16,32},{32,48},{48,64},{64,80},{80,96},{96,112},{112,0},{1... | collective-permute-start | bytes 1216520 | tf_op jit(solution)/shard_map/ppermute | solution.py:331
  148.6 14.7 %collective-permute-start.27 = (bf16[144,1408]{1,0:T(8,128)(2,1)S(1)}, bf16[144,1408]{1,0:T(8,128)(2,1)S(1)}, u32[]{:S(2)}, u32[]{:S(2)}) collective-permute-start(bf16[144,1408]{1,0:T(8,128)(2,1)S(1)} %get-tuple-element.58), channel_id=1, source_target_pairs={{0,16},{16,32},{32,48},{48,64},{64,80},{80,96},{96,112},{112,0},{1... | collective-permute-start | bytes 1216520 | tf_op jit(solution)/shard_map/ppermute | solution.py:331
  157.3 11.8 %collective-permute-start.18 = (bf16[144,1408]{1,0:T(8,128)(2,1)S(1)}, bf16[144,1408]{1,0:T(8,128)(2,1)S(1)}, u32[]{:S(2)}, u32[]{:S(2)}) collective-permute-start(bf16[144,1408]{1,0:T(8,128)(2,1)S(1)} %get-tuple-element.48), channel_id=1, source_target_pairs={{0,112},{16,0},{32,16},{48,32},{64,48},{80,64},{96,80},{112,96},{1... | collective-permute-start | bytes 1216520 | tf_op jit(solution)/shard_map/ppermute | solution.py:331
  164.1 7.4 %collective-permute-start.28 = (bf16[72,672]{1,0:T(8,128)(2,1)S(1)}, bf16[72,672]{1,0:T(8,128)(2,1)S(1)}, u32[]{:S(2)}, u32[]{:S(2)}) collective-permute-start(bf16[72,672]{1,0:T(8,128)(2,1)S(1)} %get-tuple-element.60), channel_id=1, source_target_pairs={{0,6},{2,0},{4,2},{6,4},{1,7},{3,1},{5,3},{7,5},{8,14},{10,8},{12,... | collective-permute-start | bytes 290312 | tf_op jit(solution)/shard_map/ppermute | solution.py:331
  165.4 9.8 %collective-permute-start.29 = (bf16[72,672]{1,0:T(8,128)(2,1)S(1)}, bf16[72,672]{1,0:T(8,128)(2,1)S(1)}, u32[]{:S(2)}, u32[]{:S(2)}) collective-permute-start(bf16[72,672]{1,0:T(8,128)(2,1)S(1)} %get-tuple-element.61), channel_id=1, source_target_pairs={{0,134},{2,128},{4,130},{6,132},{128,6},{130,0},{132,2},{134,4},{1... | collective-permute-start | bytes 290312 | tf_op jit(solution)/shard_map/ppermute | solution.py:476
  168.7 6.6 %collective-permute-start.33 = (bf16[72,672]{1,0:T(8,128)(2,1)S(1)}, bf16[72,672]{1,0:T(8,128)(2,1)S(1)}, u32[]{:S(2)}, u32[]{:S(2)}) collective-permute-start(bf16[72,672]{1,0:T(8,128)(2,1)S(1)} %get-tuple-element.65), channel_id=1, source_target_pairs={{0,130},{2,132},{4,134},{6,128},{128,2},{130,4},{132,6},{134,0},{1... | collective-permute-start | bytes 290312 | tf_op jit(solution)/shard_map/ppermute | solution.py:476
  171.5 7.5 %collective-permute-start.30 = (bf16[72,672]{1,0:T(8,128)(2,1)S(1)}, bf16[72,672]{1,0:T(8,128)(2,1)S(1)}, u32[]{:S(2)}, u32[]{:S(2)}) collective-permute-start(bf16[72,672]{1,0:T(8,128)(2,1)S(1)} %get-tuple-element.62), channel_id=1, source_target_pairs={{0,4},{2,6},{4,0},{6,2},{1,5},{3,7},{5,1},{7,3},{8,12},{10,14},{12... | collective-permute-start | bytes 290312 | tf_op jit(solution)/shard_map/ppermute | solution.py:331
  175.2 7.2 %collective-permute-start.31 = (bf16[72,672]{1,0:T(8,128)(2,1)S(1)}, bf16[72,672]{1,0:T(8,128)(2,1)S(1)}, u32[]{:S(2)}, u32[]{:S(2)}) collective-permute-start(bf16[72,672]{1,0:T(8,128)(2,1)S(1)} %get-tuple-element.63), channel_id=1, source_target_pairs={{0,132},{2,134},{4,128},{6,130},{128,4},{130,6},{132,0},{134,2},{1... | collective-permute-start | bytes 290312 | tf_op jit(solution)/shard_map/ppermute | solution.py:476
  (10 other events, 102.3 us)

commit v6 on v4

--- a/solution.py
+++ b/solution.py
@@ -206,7 +206,7 @@
         for across in range(2):
             source = lax.rem(place_ref[0] + 4 - behind, 4) * 2 + lax.rem(place_ref[1] + across, 2)
             lane = pl.multiple_of(source * 128, 128)
-            whole_ref[:, pl.ds(lane, 128)] = pieces[at * 2 + across][0]
+            whole_ref[:, pl.ds(lane, 128)] = pieces[at + 4 * across][0]
     out_ref[...] = multiply(whole_ref[...], joined)
 
 
@@ -433,9 +433,7 @@
     own = head_grads(queries, keys, teacher_attention_logits, document_length, [cut[0]])
     own = gate(own, held[1:] + swapped)
     swapped += [shifted(piece, "xh", 2, 1) for piece in held[1:]]
-    pieces = []
-    for pair in zip(held, swapped):
-        pieces += pair
+    pieces = held + swapped
     back = shifted(own, "y", 4, 1)
     fore = shifted(own, "y", 4, 3)
     half = WIDTH // 2

time: 184 us -> 182 us (0.989)
  waiting for transfers between devices: 87.8 us -> 82.8 us
  starting transfers between devices: 43.2 us -> 46.6 us
    ppermute x30, waiting for transfers between devices: 84.1 us -> 78.4 us  [shifted(): return lax.ppermute(x, axis, [(at, (at + by) % size) for at in range(size)])]
    ppermute x30, starting transfers between devices: 37.9 us -> 40.9 us  [shifted(): return lax.ppermute(x, axis, [(at, (at + by) % size) for at in range(size)])]
  transfers between devices with their start and end apart: 34 -> 34, of which waited for: 17 -> 16; matrix products, arithmetic and copies ran while one was open for 0% -> 0% of each run, Pallas kernels for 24% -> 24%
where the time goes in v6:
time: 182 us
  waiting for transfers between devices  82.8 us (45%)
  Pallas kernels  48.3 us (27%)
  starting transfers between devices  46.6 us (26%)
  local copies, waits for them, and re-layouts  3 us (2%)
    ppermute x30, waiting for transfers between devices, shifted(): return lax.ppermute(x, axis, [(at, (at + by) % size) for at in range(size)])  78.4 us
    ppermute x30, starting transfers between devices, shifted(): return lax.ppermute(x, axis, [(at, (at + by) % size) for at in range(size)])  40.9 us
    pallas_call x4, Pallas kernels, term_call(): pl.pallas_call(functools.partial(kernel, count), out_shape=out_shape, gri...  20.5 us
    pallas_call x1, Pallas kernels, head_grads(): pl.pallas_call(head_kernel, out_shape=jax.ShapeDtypeStruct(shape, NARROW)...  13.4 us
    pallas_call x8, Pallas kernels, loads(): pl.pallas_call(functools.partial(load_kernel, streams), out_shape=(shape,...  7.35 us
    ppermute x4, starting transfers between devices, on_device(): other = lax.ppermute(other, ('xl', 'y'), across)  5.65 us
    ppermute x4, waiting for transfers between devices, on_device(): other = lax.ppermute(other, ('xl', 'y'), across)  4.36 us
  transfers between devices with their start and end apart: 34, of which 16 were waited for; matrix products, arithmetic and copies ran while one was open for 0% of the time, Pallas kernels for 24%

profile of v6, /device:TPU:8, one launch (start us, length us, event | category | flops | bytes accessed | tf_op | source)
XLA Modules:
  0.0 181.9 jit_solution(13270419724096319299)
XLA Ops:
  0.8 3.4 %turn.1 = (bf16[2,1152,128]{2,1,0:T(8,128)(2,1)S(1)}, bf16[2,1152,128]{2,1,0:T(8,128)(2,1)S(1)}, bf16[2,1152,128]{2,1,0:T(8,128)(2,1)S(1)}, bf16[2,1152,128]{2,1,0:T(8,128)(2,1)S(1)}) custom-call(s32[12]{0:T(128)S(1)} %stack.51.place_ref.spot_ref.refs_2_.refs_5_, bf16[2,64,9216]{2,1,0:T(8,128)(2,1)} %far_ref.1, bf16[2,64,9216]{2,1,0:T(8,128)(2,1)} %far_ref.1), custom_call_target="tpu_custom_call" | custom-call | flops 1000 | bytes 10500000 | tf_op jit(solution)/shard_map/turn/pallas_call | solution.py:163
  4.2 1.7 collective-permute-start
  6.5 2.0 %collective-permute-start.2 = (bf16[2,1152,128]{2,1,0:T(8,128)(2,1)S(1)}, bf16[2,1152,128]{2,1,0:T(8,128)(2,1)S(1)}, u32[]{:S(2)}, u32[]{:S(2)}) collective-permute-start(bf16[2,1152,128]{2,1,0:T(8,128)(2,1)S(1)} %get-tuple-element.33), channel_id=1, source_target_pairs={{0,4},{2,6},{4,0},{6,2},{1,5},{3,7},{5,1},{7,3},{8,12},{10,14},{12... | collective-permute-start | bytes 1769480 | tf_op jit(solution)/shard_map/ppermute | solution.py:331
  8.6 3.0 %collective-permute-start.3 = (bf16[2,1152,128]{2,1,0:T(8,128)(2,1)S(1)}, bf16[2,1152,128]{2,1,0:T(8,128)(2,1)S(1)}, u32[]{:S(2)}, u32[]{:S(2)}) collective-permute-start(bf16[2,1152,128]{2,1,0:T(8,128)(2,1)S(1)} %get-tuple-element.30.refs_0_), channel_id=1, source_target_pairs={{0,1},{1,0},{2,3},{3,2},{4,5},{5,4},{6,7},{7,6},{8,9},{9,8},{10,11... | collective-permute-start | bytes 1769480 | tf_op jit(solution)/shard_map/ppermute | solution.py:331
  11.6 2.8 %copy-done = bf16[2,6,512,512]{3,2,1,0:T(8,128)(2,1)S(1)} copy-done((bf16[2,6,512,512]{3,2,1,0:T(8,128)(2,1)S(1)}, bf16[2,6,512,512]{3,2,1,0:T(8,128)(2,1)}, u32[]{:S(2)}) %copy-start) | copy-done | bytes 6291480
  14.4 13.4 %head_grads.1 = bf16[7,96,1024]{2,1,0:T(8,128)(2,1)S(1)} custom-call(s32[2,4]{1,0:T(2,128)S(1)} %copy-done.3, bf16[2,576,512]{2,1,0:T(8,128)(2,1)S(1)} %bitcast.16, bf16[2,96,512]{2,1,0:T(8,128)(2,1)S(1)} %bitcast.17, bf16[2,6,512,512]{3,2,1,0:T(8,128)(2,1)S(1)} %copy-done, bf16[2,1152,128]{2,1,0:T(8,128)(2,1)S(1)} %get-tuple-element.30.refs_0_), custom_call_target="tpu_custom_call" | custom-call | flops 1000 | bytes 49000000 | tf_op jit(solution)/shard_map/head_grads/pallas_call | solution.py:115
  27.8 6.1 %collective-permute-done.2.refs_2_.refs_3_ = bf16[2,1152,128]{2,1,0:T(8,128)(2,1)S(1)} collective-permute-done((bf16[2,1152,128]{2,1,0:T(8,128)(2,1)S(1)}, bf16[2,1152,128]{2,1,0:T(8,128)(2,1)S(1)}, u32[]{:S(2)}, u32[]{:S(2)}) %collective-permute-start.2) | collective-permute-done | bytes 589856 | tf_op jit(solution)/shard_map/ppermute | solution.py:331
  36.0 3.0 %collective-permute-start.4 = (bf16[2,1152,128]{2,1,0:T(8,128)(2,1)S(1)}, bf16[2,1152,128]{2,1,0:T(8,128)(2,1)S(1)}, u32[]{:S(2)}, u32[]{:S(2)}) collective-permute-start(bf16[2,1152,128]{2,1,0:T(8,128)(2,1)S(1)} %collective-permute-done.refs_0_.refs_1_), channel_id=1, source_target_pairs={{0,1},{1,0},{2,3},{3,2},{4,5},{5,4},{6,7},{7,6},{8,9},{9,8},{10,11... | collective-permute-start | bytes 1769480 | tf_op jit(solution)/shard_map/ppermute | solution.py:331
  39.5 3.0 %collective-permute-start.6 = (bf16[2,1152,128]{2,1,0:T(8,128)(2,1)S(1)}, bf16[2,1152,128]{2,1,0:T(8,128)(2,1)S(1)}, u32[]{:S(2)}, u32[]{:S(2)}) collective-permute-start(bf16[2,1152,128]{2,1,0:T(8,128)(2,1)S(1)} %collective-permute-done.2.refs_2_.refs_3_), channel_id=1, source_target_pairs={{0,1},{1,0},{2,3},{3,2},{4,5},{5,4},{6,7},{7,6},{8,9},{9,8},{10,11... | collective-permute-start | bytes 1769480 | tf_op jit(solution)/shard_map/ppermute | solution.py:331
  42.6 22.1 %collective-permute-done.8.refs_9_.refs_10_ = bf16[672,1024]{1,0:T(8,128)(2,1)S(1)} collective-permute-done((bf16[672,1024]{1,0:T(8,128)(2,1)S(1)}, bf16[672,1024]{1,0:T(8,128)(2,1)S(1)}, u32[]{:S(2)}, u32[]{:S(2)}) %collective-permute-start.8) | collective-permute-done | bytes 1376288 | tf_op jit(solution)/shard_map/ppermute | solution.py:331
  67.0 9.1 %collective-permute-done.6.refs_7_ = bf16[2,1152,128]{2,1,0:T(8,128)(2,1)S(1)} collective-permute-done((bf16[2,1152,128]{2,1,0:T(8,128)(2,1)S(1)}, bf16[2,1152,128]{2,1,0:T(8,128)(2,1)S(1)}, u32[]{:S(2)}, u32[]{:S(2)}) %collective-permute-start.6) | collective-permute-done | bytes 589856 | tf_op jit(solution)/shard_map/ppermute | solution.py:331
  76.1 5.7 %terms.4 = (bf16[1152,1408]{1,0:T(8,128)(2,1)S(1)}, bf16[1152,1024]{1,0:T(8,128)(2,1)S(1)}) custom-call(s32[12]{0:T(128)S(1)} %stack.51.place_ref.spot_ref.refs_2_.refs_5_, bf16[2,1152,128]{2,1,0:T(8,128)(2,1)S(1)} %get-tuple-element.30.refs_0_, bf16[2,1152,128]{2,1,0:T(8,128)(2,1)S(1)} %collective-permute-done.refs_0_.refs_1_, ...), custom_call_target="tpu_custom_call" | custom-call | flops 1000 | bytes 21000000 | tf_op jit(solution)/shard_map/terms/pallas_call | solution.py:223
  82.1 5.7 %terms.5 = (bf16[1152,1408]{1,0:T(8,128)(2,1)S(1)}, bf16[1152,1024]{1,0:T(8,128)(2,1)S(1)}) custom-call(s32[12]{0:T(128)S(1)} %stack.51.place_ref.spot_ref.refs_2_.refs_5_, bf16[2,1152,128]{2,1,0:T(8,128)(2,1)S(1)} %get-tuple-element.30.refs_0_, bf16[2,1152,128]{2,1,0:T(8,128)(2,1)S(1)} %collective-permute-done.refs_0_.refs_1_, ...), custom_call_target="tpu_custom_call" | custom-call | flops 1000 | bytes 21000000 | tf_op jit(solution)/shard_map/terms/pallas_call | solution.py:223
  87.8 4.6 %terms.6.refs_3_ = bf16[1152,1408]{1,0:T(8,128)(2,1)S(1)} custom-call(bf16[1152,1024]{1,0:T(8,128)(2,1)S(1)} %get-tuple-element.36.whole_ref, bf16[336,1024]{1,0:T(8,128)(2,1)S(1)} %collective-permute-done.9.refs_0_, bf16[336,1024]{1,0:T(8,128)(2,1)S(1)} %collective-permute-done.10.refs_1_, bf16[672,1024]{1,0:T(8,128)(2,1)S(1)} %gate.1.refs_2_, ...), custom_call_target="tpu_custom_call" | custom-call | flops 1000 | bytes 21000000 | tf_op jit(solution)/shard_map/terms/pallas_call | solution.py:223
  94.2 2.0 %collective-permute-start.21 = (bf16[144,1408]{1,0:T(8,128)(2,1)S(1)}, bf16[144,1408]{1,0:T(8,128)(2,1)S(1)}, u32[]{:S(2)}, u32[]{:S(2)}) collective-permute-start(bf16[144,1408]{1,0:T(8,128)(2,1)S(1)} %get-tuple-element.46), channel_id=1, source_target_pairs={{0,16},{16,32},{32,48},{48,64},{64,80},{80,96},{96,112},{112,0},{1... | collective-permute-start | bytes 1216520 | tf_op jit(solution)/shard_map/ppermute | solution.py:331
  96.2 4.0 %collective-permute-start.22 = (bf16[144,1408]{1,0:T(8,128)(2,1)S(1)}, bf16[144,1408]{1,0:T(8,128)(2,1)S(1)}, u32[]{:S(2)}, u32[]{:S(2)}) collective-permute-start(bf16[144,1408]{1,0:T(8,128)(2,1)S(1)} %get-tuple-element.47), channel_id=1, source_target_pairs={{0,112},{16,0},{32,16},{48,32},{64,48},{80,64},{96,80},{112,96},{1... | collective-permute-start | bytes 1216520 | tf_op jit(solution)/shard_map/ppermute | solution.py:331
  100.3 4.5 %terms.7.refs_0_.refs_3_.keep_ref = bf16[1152,1408]{1,0:T(8,128)(2,1)S(1)} custom-call(bf16[1152,1024]{1,0:T(8,128)(2,1)S(1)} %get-tuple-element.35.whole_ref, bf16[336,1024]{1,0:T(8,128)(2,1)S(1)} %collective-permute-done.9.refs_0_, bf16[336,1024]{1,0:T(8,128)(2,1)S(1)} %collective-permute-done.10.refs_1_, bf16[672,1024]{1,0:T(8,128)(2,1)S(1)} %gate.1.refs_2_, ...), custom_call_target="tpu_custom_call" | custom-call | flops 1000 | bytes 21000000 | tf_op jit(solution)/shard_map/terms/pallas_call | solution.py:223
  106.1 2.0 %collective-permute-start.12 = (bf16[144,1408]{1,0:T(8,128)(2,1)S(1)}, bf16[144,1408]{1,0:T(8,128)(2,1)S(1)}, u32[]{:S(2)}, u32[]{:S(2)}) collective-permute-start(bf16[144,1408]{1,0:T(8,128)(2,1)S(1)} %get-tuple-element.38), channel_id=1, source_target_pairs={{0,112},{16,0},{32,16},{48,32},{64,48},{80,64},{96,80},{112,96},{1... | collective-permute-start | bytes 1216520 | tf_op jit(solution)/shard_map/ppermute | solution.py:331
  111.3 3.4 %collective-permute-start.24 = (bf16[144,1408]{1,0:T(8,128)(2,1)S(1)}, bf16[144,1408]{1,0:T(8,128)(2,1)S(1)}, u32[]{:S(2)}, u32[]{:S(2)}) collective-permute-start(bf16[144,1408]{1,0:T(8,128)(2,1)S(1)} %get-tuple-element.49), channel_id=1, source_target_pairs={{0,112},{16,0},{32,16},{48,32},{64,48},{80,64},{96,80},{112,96},{1... | collective-permute-start | bytes 1216520 | tf_op jit(solution)/shard_map/ppermute | solution.py:331
  114.7 4.0 %collective-permute-done.12.refs_2_ = bf16[144,1408]{1,0:T(8,128)(2,1)S(1)} collective-permute-done((bf16[144,1408]{1,0:T(8,128)(2,1)S(1)}, bf16[144,1408]{1,0:T(8,128)(2,1)S(1)}, u32[]{:S(2)}, u32[]{:S(2)}) %collective-permute-start.12) | collective-permute-done | bytes 405536 | tf_op jit(solution)/shard_map/ppermute | solution.py:331
  118.7 2.9 %collective-permute-done.13.refs_5_ = bf16[144,1408]{1,0:T(8,128)(2,1)S(1)} collective-permute-done((bf16[144,1408]{1,0:T(8,128)(2,1)S(1)}, bf16[144,1408]{1,0:T(8,128)(2,1)S(1)}, u32[]{:S(2)}, u32[]{:S(2)}) %collective-permute-start.13) | collective-permute-done | bytes 405536 | tf_op jit(solution)/shard_map/ppermute | solution.py:331
  124.6 5.7 %collective-permute-done.23.refs_2_ = bf16[144,1408]{1,0:T(8,128)(2,1)S(1)} collective-permute-done((bf16[144,1408]{1,0:T(8,128)(2,1)S(1)}, bf16[144,1408]{1,0:T(8,128)(2,1)S(1)}, u32[]{:S(2)}, u32[]{:S(2)}) %collective-permute-start.23) | collective-permute-done | bytes 405536 | tf_op jit(solution)/shard_map/ppermute | solution.py:331
  131.5 3.7 %collective-permute-done.14.refs_2_ = bf16[144,1408]{1,0:T(8,128)(2,1)S(1)} collective-permute-done((bf16[144,1408]{1,0:T(8,128)(2,1)S(1)}, bf16[144,1408]{1,0:T(8,128)(2,1)S(1)}, u32[]{:S(2)}, u32[]{:S(2)}) %collective-permute-start.14) | collective-permute-done | bytes 405536 | tf_op jit(solution)/shard_map/ppermute | solution.py:331
  135.2 3.8 %collective-permute-done.15.refs_5_ = bf16[144,1408]{1,0:T(8,128)(2,1)S(1)} collective-permute-done((bf16[144,1408]{1,0:T(8,128)(2,1)S(1)}, bf16[144,1408]{1,0:T(8,128)(2,1)S(1)}, u32[]{:S(2)}, u32[]{:S(2)}) %collective-permute-start.15) | collective-permute-done | bytes 405536 | tf_op jit(solution)/shard_map/ppermute | solution.py:331
  141.0 4.9 %collective-permute-done.25.refs_2_ = bf16[144,1408]{1,0:T(8,128)(2,1)S(1)} collective-permute-done((bf16[144,1408]{1,0:T(8,128)(2,1)S(1)}, bf16[144,1408]{1,0:T(8,128)(2,1)S(1)}, u32[]{:S(2)}, u32[]{:S(2)}) %collective-permute-start.25) | collective-permute-done | bytes 405536 | tf_op jit(solution)/shard_map/ppermute | solution.py:331
  146.8 5.5 %collective-permute-done.16.refs_2_ = bf16[144,1408]{1,0:T(8,128)(2,1)S(1)} collective-permute-done((bf16[144,1408]{1,0:T(8,128)(2,1)S(1)}, bf16[144,1408]{1,0:T(8,128)(2,1)S(1)}, u32[]{:S(2)}, u32[]{:S(2)}) %collective-permute-start.16) | collective-permute-done | bytes 405536 | tf_op jit(solution)/shard_map/ppermute | solution.py:331
  154.5 6.3 %collective-permute-done.27.two_ref = bf16[144,1408]{1,0:T(8,128)(2,1)S(1)} collective-permute-done((bf16[144,1408]{1,0:T(8,128)(2,1)S(1)}, bf16[144,1408]{1,0:T(8,128)(2,1)S(1)}, u32[]{:S(2)}, u32[]{:S(2)}) %collective-permute-start.27) | collective-permute-done | bytes 405536 | tf_op jit(solution)/shard_map/ppermute | solution.py:331
  163.0 3.4 %collective-permute-start.29 = (bf16[72,672]{1,0:T(8,128)(2,1)S(1)}, bf16[72,672]{1,0:T(8,128)(2,1)S(1)}, u32[]{:S(2)}, u32[]{:S(2)}) collective-permute-start(bf16[72,672]{1,0:T(8,128)(2,1)S(1)} %get-tuple-element.53), channel_id=1, source_target_pairs={{0,134},{2,128},{4,130},{6,132},{128,6},{130,0},{132,2},{134,4},{1... | collective-permute-start | bytes 290312 | tf_op jit(solution)/shard_map/ppermute | solution.py:481
  169.4 3.7 %collective-permute-start.30 = (bf16[72,672]{1,0:T(8,128)(2,1)S(1)}, bf16[72,672]{1,0:T(8,128)(2,1)S(1)}, u32[]{:S(2)}, u32[]{:S(2)}) collective-permute-start(bf16[72,672]{1,0:T(8,128)(2,1)S(1)} %get-tuple-element.54), channel_id=1, source_target_pairs={{0,4},{2,6},{4,0},{6,2},{1,5},{3,7},{5,1},{7,3},{8,12},{10,14},{12... | collective-permute-start | bytes 290312 | tf_op jit(solution)/shard_map/ppermute | solution.py:331
  174.0 2.4 %collective-permute-done.30.refs_4_ = bf16[72,672]{1,0:T(8,128)(2,1)S(1)} collective-permute-done((bf16[72,672]{1,0:T(8,128)(2,1)S(1)}, bf16[72,672]{1,0:T(8,128)(2,1)S(1)}, u32[]{:S(2)}, u32[]{:S(2)}) %collective-permute-start.30) | collective-permute-done | bytes 96800 | tf_op jit(solution)/shard_map/ppermute | solution.py:331
  176.4 3.8 %collective-permute-done.31.refs_5_ = bf16[72,672]{1,0:T(8,128)(2,1)S(1)} collective-permute-done((bf16[72,672]{1,0:T(8,128)(2,1)S(1)}, bf16[72,672]{1,0:T(8,128)(2,1)S(1)}, u32[]{:S(2)}, u32[]{:S(2)}) %collective-permute-start.31) | collective-permute-done | bytes 96800 | tf_op jit(solution)/shard_map/ppermute | solution.py:481
  180.2 1.7 finish.1
  (77 shorter events, 27.5 us)
Async XLA Ops:
  4.2 23.6 %collective-permute-start = (bf16[2,1152,128]{2,1,0:T(8,128)(2,1)S(1)}, bf16[2,1152,128]{2,1,0:T(8,128)(2,1)S(1)}, u32[]{:S(2)}, u32[]{:S(2)}) collective-permute-start(bf16[2,1152,128]{2,1,0:T(8,128)(2,1)S(1)} %get-tuple-element.31), channel_id=1, source_target_pairs={{0,2},{2,4},{4,6},{6,0},{1,3},{3,5},{5,7},{7,1},{8,10},{10,12},{12... | collective-permute-start | bytes 1769480 | tf_op jit(solution)/shard_map/ppermute | solution.py:331
  5.8 22.0 %collective-permute-start.1 = (bf16[2,1152,128]{2,1,0:T(8,128)(2,1)S(1)}, bf16[2,1152,128]{2,1,0:T(8,128)(2,1)S(1)}, u32[]{:S(2)}, u32[]{:S(2)}) collective-permute-start(bf16[2,1152,128]{2,1,0:T(8,128)(2,1)S(1)} %get-tuple-element.32), channel_id=1, source_target_pairs={{0,6},{2,0},{4,2},{6,4},{1,7},{3,1},{5,3},{7,5},{8,14},{10,8},{12,... | collective-permute-start | bytes 1769480 | tf_op jit(solution)/shard_map/ppermute | solution.py:331
  6.5 27.4 %collective-permute-start.2 = (bf16[2,1152,128]{2,1,0:T(8,128)(2,1)S(1)}, bf16[2,1152,128]{2,1,0:T(8,128)(2,1)S(1)}, u32[]{:S(2)}, u32[]{:S(2)}) collective-permute-start(bf16[2,1152,128]{2,1,0:T(8,128)(2,1)S(1)} %get-tuple-element.33), channel_id=1, source_target_pairs={{0,4},{2,6},{4,0},{6,2},{1,5},{3,7},{5,1},{7,3},{8,12},{10,14},{12... | collective-permute-start | bytes 1769480 | tf_op jit(solution)/shard_map/ppermute | solution.py:331
  8.6 25.4 %collective-permute-start.3 = (bf16[2,1152,128]{2,1,0:T(8,128)(2,1)S(1)}, bf16[2,1152,128]{2,1,0:T(8,128)(2,1)S(1)}, u32[]{:S(2)}, u32[]{:S(2)}) collective-permute-start(bf16[2,1152,128]{2,1,0:T(8,128)(2,1)S(1)} %get-tuple-element.30.refs_0_), channel_id=1, source_target_pairs={{0,1},{1,0},{2,3},{3,2},{4,5},{5,4},{6,7},{7,6},{8,9},{9,8},{10,11... | collective-permute-start | bytes 1769480 | tf_op jit(solution)/shard_map/ppermute | solution.py:331
  34.0 30.7 %collective-permute-start.8 = (bf16[672,1024]{1,0:T(8,128)(2,1)S(1)}, bf16[672,1024]{1,0:T(8,128)(2,1)S(1)}, u32[]{:S(2)}, u32[]{:S(2)}) collective-permute-start(bf16[672,1024]{1,0:T(8,128)(2,1)S(1)} %gate.1.refs_2_), channel_id=1, source_target_pairs={{0,6},{2,0},{4,2},{6,4},{1,7},{3,1},{5,3},{7,5},{8,14},{10,8},{12,... | collective-permute-start | bytes 4128776 | tf_op jit(solution)/shard_map/ppermute | solution.py:331
  34.9 31.2 %collective-permute-start.7 = (bf16[672,1024]{1,0:T(8,128)(2,1)S(1)}, bf16[672,1024]{1,0:T(8,128)(2,1)S(1)}, u32[]{:S(2)}, u32[]{:S(2)}) collective-permute-start(bf16[672,1024]{1,0:T(8,128)(2,1)S(1)} %gate.1.refs_2_), channel_id=1, source_target_pairs={{0,2},{2,4},{4,6},{6,0},{1,3},{3,5},{5,7},{7,1},{8,10},{10,12},{12... | collective-permute-start | bytes 4128776 | tf_op jit(solution)/shard_map/ppermute | solution.py:331
  36.0 31.0 %collective-permute-start.4 = (bf16[2,1152,128]{2,1,0:T(8,128)(2,1)S(1)}, bf16[2,1152,128]{2,1,0:T(8,128)(2,1)S(1)}, u32[]{:S(2)}, u32[]{:S(2)}) collective-permute-start(bf16[2,1152,128]{2,1,0:T(8,128)(2,1)S(1)} %collective-permute-done.refs_0_.refs_1_), channel_id=1, source_target_pairs={{0,1},{1,0},{2,3},{3,2},{4,5},{5,4},{6,7},{7,6},{8,9},{9,8},{10,11... | collective-permute-start | bytes 1769480 | tf_op jit(solution)/shard_map/ppermute | solution.py:331
  39.0 28.0 %collective-permute-start.5 = (bf16[2,1152,128]{2,1,0:T(8,128)(2,1)S(1)}, bf16[2,1152,128]{2,1,0:T(8,128)(2,1)S(1)}, u32[]{:S(2)}, u32[]{:S(2)}) collective-permute-start(bf16[2,1152,128]{2,1,0:T(8,128)(2,1)S(1)} %collective-permute-done.1.refs_1_.refs_2_), channel_id=1, source_target_pairs={{0,1},{1,0},{2,3},{3,2},{4,5},{5,4},{6,7},{7,6},{8,9},{9,8},{10,11... | collective-permute-start | bytes 1769480 | tf_op jit(solution)/shard_map/ppermute | solution.py:331
  39.5 36.6 %collective-permute-start.6 = (bf16[2,1152,128]{2,1,0:T(8,128)(2,1)S(1)}, bf16[2,1152,128]{2,1,0:T(8,128)(2,1)S(1)}, u32[]{:S(2)}, u32[]{:S(2)}) collective-permute-start(bf16[2,1152,128]{2,1,0:T(8,128)(2,1)S(1)} %collective-permute-done.2.refs_2_.refs_3_), channel_id=1, source_target_pairs={{0,1},{1,0},{2,3},{3,2},{4,5},{5,4},{6,7},{7,6},{8,9},{9,8},{10,11... | collective-permute-start | bytes 1769480 | tf_op jit(solution)/shard_map/ppermute | solution.py:331
  64.8 23.1 %collective-permute-start.10 = (bf16[336,1024]{1,0:T(8,128)(2,1)S(1)}, bf16[336,1024]{1,0:T(8,128)(2,1)S(1)}, u32[]{:S(2)}, u32[]{:S(2)}) collective-permute-start(bf16[336,1024]{1,0:T(8,128)(2,1)S(1)} %slice.9), channel_id=1, source_target_pairs={{0,6},{2,0},{4,2},{6,4},{1,7},{3,1},{5,3},{7,5},{8,14},{10,8},{12,... | collective-permute-start | bytes 2064392 | tf_op jit(solution)/shard_map/ppermute | solution.py:331
  66.1 21.7 %collective-permute-start.9 = (bf16[336,1024]{1,0:T(8,128)(2,1)S(1)}, bf16[336,1024]{1,0:T(8,128)(2,1)S(1)}, u32[]{:S(2)}, u32[]{:S(2)}) collective-permute-start(bf16[336,1024]{1,0:T(8,128)(2,1)S(1)} %slice.8), channel_id=1, source_target_pairs={{0,2},{2,4},{4,6},{6,0},{1,3},{3,5},{5,7},{7,1},{8,10},{10,12},{12... | collective-permute-start | bytes 2064392 | tf_op jit(solution)/shard_map/ppermute | solution.py:331
  81.8 11.2 %collective-permute-start.20 = (bf16[1152,1408]{1,0:T(8,128)(2,1)S(1)}, bf16[1152,1408]{1,0:T(8,128)(2,1)S(1)}, u32[]{:S(2)}, u32[]{:S(2)}) collective-permute-start(bf16[1152,1408]{1,0:T(8,128)(2,1)S(1)} %get-tuple-element.34.refs_10_), channel_id=1, source_target_pairs={{0,8},{8,0},{1,9},{9,1},{2,10},{10,2},{3,11},{11,3},{4,12},{12,4},... | collective-permute-start | bytes 9732104 | tf_op jit(solution)/shard_map/ppermute | solution.py:331
  92.4 12.4 %collective-permute-start.11 = (bf16[1152,1408]{1,0:T(8,128)(2,1)S(1)}, bf16[1152,1408]{1,0:T(8,128)(2,1)S(1)}, u32[]{:S(2)}, u32[]{:S(2)}) collective-permute-start(bf16[1152,1408]{1,0:T(8,128)(2,1)S(1)} %terms.6.refs_3_), channel_id=1, source_target_pairs={{0,8},{8,0},{1,9},{9,1},{2,10},{10,2},{3,11},{11,3},{4,12},{12,4},... | collective-permute-start | bytes 9732104 | tf_op jit(solution)/shard_map/ppermute | solution.py:331
  94.2 15.5 %collective-permute-start.21 = (bf16[144,1408]{1,0:T(8,128)(2,1)S(1)}, bf16[144,1408]{1,0:T(8,128)(2,1)S(1)}, u32[]{:S(2)}, u32[]{:S(2)}) collective-permute-start(bf16[144,1408]{1,0:T(8,128)(2,1)S(1)} %get-tuple-element.46), channel_id=1, source_target_pairs={{0,16},{16,32},{32,48},{48,64},{64,80},{80,96},{96,112},{112,0},{1... | collective-permute-start | bytes 1216520 | tf_op jit(solution)/shard_map/ppermute | solution.py:331
  96.2 13.8 %collective-permute-start.22 = (bf16[144,1408]{1,0:T(8,128)(2,1)S(1)}, bf16[144,1408]{1,0:T(8,128)(2,1)S(1)}, u32[]{:S(2)}, u32[]{:S(2)}) collective-permute-start(bf16[144,1408]{1,0:T(8,128)(2,1)S(1)} %get-tuple-element.47), channel_id=1, source_target_pairs={{0,112},{16,0},{32,16},{48,32},{64,48},{80,64},{96,80},{112,96},{1... | collective-permute-start | bytes 1216520 | tf_op jit(solution)/shard_map/ppermute | solution.py:331
  106.1 12.6 %collective-permute-start.12 = (bf16[144,1408]{1,0:T(8,128)(2,1)S(1)}, bf16[144,1408]{1,0:T(8,128)(2,1)S(1)}, u32[]{:S(2)}, u32[]{:S(2)}) collective-permute-start(bf16[144,1408]{1,0:T(8,128)(2,1)S(1)} %get-tuple-element.38), channel_id=1, source_target_pairs={{0,112},{16,0},{32,16},{48,32},{64,48},{80,64},{96,80},{112,96},{1... | collective-permute-start | bytes 1216520 | tf_op jit(solution)/shard_map/ppermute | solution.py:331
  108.1 13.5 %collective-permute-start.13 = (bf16[144,1408]{1,0:T(8,128)(2,1)S(1)}, bf16[144,1408]{1,0:T(8,128)(2,1)S(1)}, u32[]{:S(2)}, u32[]{:S(2)}) collective-permute-start(bf16[144,1408]{1,0:T(8,128)(2,1)S(1)} %get-tuple-element.39), channel_id=1, source_target_pairs={{0,16},{16,32},{32,48},{48,64},{64,80},{80,96},{96,112},{112,0},{1... | collective-permute-start | bytes 1216520 | tf_op jit(solution)/shard_map/ppermute | solution.py:331
  110.9 19.5 %collective-permute-start.23 = (bf16[144,1408]{1,0:T(8,128)(2,1)S(1)}, bf16[144,1408]{1,0:T(8,128)(2,1)S(1)}, u32[]{:S(2)}, u32[]{:S(2)}) collective-permute-start(bf16[144,1408]{1,0:T(8,128)(2,1)S(1)} %get-tuple-element.48), channel_id=1, source_target_pairs={{0,16},{16,32},{32,48},{48,64},{64,80},{80,96},{96,112},{112,0},{1... | collective-permute-start | bytes 1216520 | tf_op jit(solution)/shard_map/ppermute | solution.py:331
  111.3 19.0 %collective-permute-start.24 = (bf16[144,1408]{1,0:T(8,128)(2,1)S(1)}, bf16[144,1408]{1,0:T(8,128)(2,1)S(1)}, u32[]{:S(2)}, u32[]{:S(2)}) collective-permute-start(bf16[144,1408]{1,0:T(8,128)(2,1)S(1)} %get-tuple-element.49), channel_id=1, source_target_pairs={{0,112},{16,0},{32,16},{48,32},{64,48},{80,64},{96,80},{112,96},{1... | collective-permute-start | bytes 1216520 | tf_op jit(solution)/shard_map/ppermute | solution.py:331
  122.5 12.7 %collective-permute-start.14 = (bf16[144,1408]{1,0:T(8,128)(2,1)S(1)}, bf16[144,1408]{1,0:T(8,128)(2,1)S(1)}, u32[]{:S(2)}, u32[]{:S(2)}) collective-permute-start(bf16[144,1408]{1,0:T(8,128)(2,1)S(1)} %get-tuple-element.40), channel_id=1, source_target_pairs={{0,112},{16,0},{32,16},{48,32},{64,48},{80,64},{96,80},{112,96},{1... | collective-permute-start | bytes 1216520 | tf_op jit(solution)/shard_map/ppermute | solution.py:331
  123.3 15.7 %collective-permute-start.15 = (bf16[144,1408]{1,0:T(8,128)(2,1)S(1)}, bf16[144,1408]{1,0:T(8,128)(2,1)S(1)}, u32[]{:S(2)}, u32[]{:S(2)}) collective-permute-start(bf16[144,1408]{1,0:T(8,128)(2,1)S(1)} %get-tuple-element.41), channel_id=1, source_target_pairs={{0,16},{16,32},{32,48},{48,64},{64,80},{80,96},{96,112},{112,0},{1... | collective-permute-start | bytes 1216520 | tf_op jit(solution)/shard_map/ppermute | solution.py:331
  131.2 14.7 %collective-permute-start.25 = (bf16[144,1408]{1,0:T(8,128)(2,1)S(1)}, bf16[144,1408]{1,0:T(8,128)(2,1)S(1)}, u32[]{:S(2)}, u32[]{:S(2)}) collective-permute-start(bf16[144,1408]{1,0:T(8,128)(2,1)S(1)} %get-tuple-element.50), channel_id=1, source_target_pairs={{0,16},{16,32},{32,48},{48,64},{64,80},{80,96},{96,112},{112,0},{1... | collective-permute-start | bytes 1216520 | tf_op jit(solution)/shard_map/ppermute | solution.py:331
  139.9 12.4 %collective-permute-start.16 = (bf16[144,1408]{1,0:T(8,128)(2,1)S(1)}, bf16[144,1408]{1,0:T(8,128)(2,1)S(1)}, u32[]{:S(2)}, u32[]{:S(2)}) collective-permute-start(bf16[144,1408]{1,0:T(8,128)(2,1)S(1)} %get-tuple-element.42), channel_id=1, source_target_pairs={{0,112},{16,0},{32,16},{48,32},{64,48},{80,64},{96,80},{112,96},{1... | collective-permute-start | bytes 1216520 | tf_op jit(solution)/shard_map/ppermute | solution.py:331
  140.0 20.7 %collective-permute-start.27 = (bf16[144,1408]{1,0:T(8,128)(2,1)S(1)}, bf16[144,1408]{1,0:T(8,128)(2,1)S(1)}, u32[]{:S(2)}, u32[]{:S(2)}) collective-permute-start(bf16[144,1408]{1,0:T(8,128)(2,1)S(1)} %get-tuple-element.51), channel_id=1, source_target_pairs={{0,112},{16,0},{32,16},{48,32},{64,48},{80,64},{96,80},{112,96},{1... | collective-permute-start | bytes 1216520 | tf_op jit(solution)/shard_map/ppermute | solution.py:331
  146.6 14.1 %collective-permute-start.26 = (bf16[144,1408]{1,0:T(8,128)(2,1)S(1)}, bf16[144,1408]{1,0:T(8,128)(2,1)S(1)}, u32[]{:S(2)}, u32[]{:S(2)}) collective-permute-start(bf16[144,1408]{1,0:T(8,128)(2,1)S(1)} %loads.15), channel_id=1, source_target_pairs={{0,16},{16,32},{32,48},{48,64},{64,80},{80,96},{96,112},{112,0},{1... | collective-permute-start | bytes 1216520 | tf_op jit(solution)/shard_map/ppermute | solution.py:331
  146.7 19.7 %collective-permute-start.18 = (bf16[144,1408]{1,0:T(8,128)(2,1)S(1)}, bf16[144,1408]{1,0:T(8,128)(2,1)S(1)}, u32[]{:S(2)}, u32[]{:S(2)}) collective-permute-start(bf16[144,1408]{1,0:T(8,128)(2,1)S(1)} %get-tuple-element.43), channel_id=1, source_target_pairs={{0,16},{16,32},{32,48},{48,64},{64,80},{80,96},{96,112},{112,0},{1... | collective-permute-start | bytes 1216520 | tf_op jit(solution)/shard_map/ppermute | solution.py:331
  153.0 14.3 %collective-permute-start.17 = (bf16[144,1408]{1,0:T(8,128)(2,1)S(1)}, bf16[144,1408]{1,0:T(8,128)(2,1)S(1)}, u32[]{:S(2)}, u32[]{:S(2)}) collective-permute-start(bf16[144,1408]{1,0:T(8,128)(2,1)S(1)} %loads.11), channel_id=1, source_target_pairs={{0,112},{16,0},{32,16},{48,32},{64,48},{80,64},{96,80},{112,96},{1... | collective-permute-start | bytes 1216520 | tf_op jit(solution)/shard_map/ppermute | solution.py:331
  161.7 7.6 %collective-permute-start.28 = (bf16[72,672]{1,0:T(8,128)(2,1)S(1)}, bf16[72,672]{1,0:T(8,128)(2,1)S(1)}, u32[]{:S(2)}, u32[]{:S(2)}) collective-permute-start(bf16[72,672]{1,0:T(8,128)(2,1)S(1)} %get-tuple-element.52), channel_id=1, source_target_pairs={{0,6},{2,0},{4,2},{6,4},{1,7},{3,1},{5,3},{7,5},{8,14},{10,8},{12,... | collective-permute-start | bytes 290312 | tf_op jit(solution)/shard_map/ppermute | solution.py:331
  163.0 10.0 %collective-permute-start.29 = (bf16[72,672]{1,0:T(8,128)(2,1)S(1)}, bf16[72,672]{1,0:T(8,128)(2,1)S(1)}, u32[]{:S(2)}, u32[]{:S(2)}) collective-permute-start(bf16[72,672]{1,0:T(8,128)(2,1)S(1)} %get-tuple-element.53), channel_id=1, source_target_pairs={{0,134},{2,128},{4,130},{6,132},{128,6},{130,0},{132,2},{134,4},{1... | collective-permute-start | bytes 290312 | tf_op jit(solution)/shard_map/ppermute | solution.py:481
  166.4 7.1 %collective-permute-start.32 = (bf16[72,672]{1,0:T(8,128)(2,1)S(1)}, bf16[72,672]{1,0:T(8,128)(2,1)S(1)}, u32[]{:S(2)}, u32[]{:S(2)}) collective-permute-start(bf16[72,672]{1,0:T(8,128)(2,1)S(1)} %get-tuple-element.56), channel_id=1, source_target_pairs={{0,2},{2,4},{4,6},{6,0},{1,3},{3,5},{5,7},{7,1},{8,10},{10,12},{12... | collective-permute-start | bytes 290312 | tf_op jit(solution)/shard_map/ppermute | solution.py:331
  166.4 7.1 %collective-permute-start.33 = (bf16[72,672]{1,0:T(8,128)(2,1)S(1)}, bf16[72,672]{1,0:T(8,128)(2,1)S(1)}, u32[]{:S(2)}, u32[]{:S(2)}) collective-permute-start(bf16[72,672]{1,0:T(8,128)(2,1)S(1)} %get-tuple-element.57), channel_id=1, source_target_pairs={{0,130},{2,132},{4,134},{6,128},{128,2},{130,4},{132,6},{134,0},{1... | collective-permute-start | bytes 290312 | tf_op jit(solution)/shard_map/ppermute | solution.py:481
  173.1 7.2 %collective-permute-start.31 = (bf16[72,672]{1,0:T(8,128)(2,1)S(1)}, bf16[72,672]{1,0:T(8,128)(2,1)S(1)}, u32[]{:S(2)}, u32[]{:S(2)}) collective-permute-start(bf16[72,672]{1,0:T(8,128)(2,1)S(1)} %get-tuple-element.55), channel_id=1, source_target_pairs={{0,132},{2,134},{4,128},{6,130},{128,4},{130,6},{132,0},{134,2},{1... | collective-permute-start | bytes 290312 | tf_op jit(solution)/shard_map/ppermute | solution.py:481
  (10 other events, 81.3 us)

commit v7 on v6

--- a/solution.py
+++ b/solution.py
@@ -332,7 +332,7 @@
 
 
 def load_kernel(streams, spot_ref, *refs):
-    outs = refs[3 * streams :]
+    outs = refs[len(refs) - streams :]
     for at, out_ref in enumerate(outs):
         parts = refs[3 * at : 3 * at + 3]
         total = parts[0][...].astype(jnp.float32) + parts[1][...].astype(jnp.float32)
@@ -341,7 +341,7 @@
         out_ref[...] = total.astype(NARROW)
 
 
-def loads(place, aheads, keep, got, moving):
+def loads(place, aheads, keep, got, moving, after=()):
     streams = len(moving)
     width = keep.shape[1]
 
@@ -360,6 +360,9 @@
         else:
             in_specs.append(whole)
             operands.append(there)
+    for there in after:
+        in_specs.append(pl.BlockSpec(memory_space=pl.ANY))
+        operands.append(there)
     shape = jax.ShapeDtypeStruct((PIECE, width), NARROW)
     return pl.pallas_call(
         functools.partial(load_kernel, streams),
@@ -470,7 +473,8 @@
             way = 1 - 2 * at
             aheads = [(4 - slot) * way, (slot - 3) * way]
             count = 2 if slot < 3 else 1
-            sums = loads(place, aheads[:count], keep, got, moving[at][:count])
+            after = moving[0][1:] if slot == 3 and at == 1 else []
+            sums = loads(place, aheads[:count], keep, got, moving[at][:count], after)
             for stream, load in enumerate(sums):
                 moving[at][stream] = shifted(load, "z", RINGS, -way if stream else way)
     blocks = {}

time: 182 us -> 182 us (level)
  waiting for transfers between devices: 82.8 us -> 76.5 us
  starting transfers between devices: 46.6 us -> 52.3 us
    ppermute x30, waiting for transfers between devices: 78.4 us -> 72.4 us  [shifted(): return lax.ppermute(x, axis, [(at, (at + by) % size) for at in range(size)])]
    ppermute x30, starting transfers between devices: 40.9 us -> 46.3 us  [shifted(): return lax.ppermute(x, axis, [(at, (at + by) % size) for at in range(size)])]
  transfers between devices with their start and end apart: 34 -> 34, of which waited for: 16 -> 17; matrix products, arithmetic and copies ran while one was open for 0% -> 0% of each run, Pallas kernels for 24% -> 24%
where the time goes in v7:
time: 182 us; the launch traced here: 181 us
  waiting for transfers between devices  76.5 us (42%)
  starting transfers between devices  52.3 us (29%)
  Pallas kernels  48.3 us (27%)
  local copies, waits for them, and re-layouts  3 us (2%)
    ppermute x30, waiting for transfers between devices, shifted(): return lax.ppermute(x, axis, [(at, (at + by) % size) for at in range(size)])  72.4 us
    ppermute x30, starting transfers between devices, shifted(): return lax.ppermute(x, axis, [(at, (at + by) % size) for at in range(size)])  46.3 us
    pallas_call x4, Pallas kernels, term_call(): pl.pallas_call(functools.partial(kernel, count), out_shape=out_shape, gri...  20.5 us
    pallas_call x1, Pallas kernels, head_grads(): pl.pallas_call(head_kernel, out_shape=jax.ShapeDtypeStruct(shape, NARROW)...  13.4 us
    pallas_call x8, Pallas kernels, loads(): pl.pallas_call(functools.partial(load_kernel, streams), out_shape=(shape,...  7.34 us
    ppermute x4, starting transfers between devices, on_device(): other = lax.ppermute(other, ('xl', 'y'), across)  6.08 us
    ppermute x4, waiting for transfers between devices, on_device(): other = lax.ppermute(other, ('xl', 'y'), across)  4.1 us
  transfers between devices with their start and end apart: 34, of which 17 were waited for; matrix products, arithmetic and copies ran while one was open for 0% of the time, Pallas kernels for 24%

profile of v7, /device:TPU:8, one launch (start us, length us, event | category | flops | bytes accessed | tf_op | source)
XLA Modules:
  0.0 181.4 jit_solution(10363311717689205175)
XLA Ops:
  0.8 3.4 %turn.1 = (bf16[2,1152,128]{2,1,0:T(8,128)(2,1)S(1)}, bf16[2,1152,128]{2,1,0:T(8,128)(2,1)S(1)}, bf16[2,1152,128]{2,1,0:T(8,128)(2,1)S(1)}, bf16[2,1152,128]{2,1,0:T(8,128)(2,1)S(1)}) custom-call(s32[12]{0:T(128)S(1)} %stack.51.place_ref.spot_ref.refs_2_.refs_5_, bf16[2,64,9216]{2,1,0:T(8,128)(2,1)} %far_ref.1, bf16[2,64,9216]{2,1,0:T(8,128)(2,1)} %far_ref.1), custom_call_target="tpu_custom_call" | custom-call | flops 1000 | bytes 10500000 | tf_op jit(solution)/shard_map/turn/pallas_call | solution.py:163
  6.5 2.0 %collective-permute-start.2 = (bf16[2,1152,128]{2,1,0:T(8,128)(2,1)S(1)}, bf16[2,1152,128]{2,1,0:T(8,128)(2,1)S(1)}, u32[]{:S(2)}, u32[]{:S(2)}) collective-permute-start(bf16[2,1152,128]{2,1,0:T(8,128)(2,1)S(1)} %get-tuple-element.33), channel_id=1, source_target_pairs={{0,4},{2,6},{4,0},{6,2},{1,5},{3,7},{5,1},{7,3},{8,12},{10,14},{12... | collective-permute-start | bytes 1769480 | tf_op jit(solution)/shard_map/ppermute | solution.py:331
  8.6 3.0 %collective-permute-start.3 = (bf16[2,1152,128]{2,1,0:T(8,128)(2,1)S(1)}, bf16[2,1152,128]{2,1,0:T(8,128)(2,1)S(1)}, u32[]{:S(2)}, u32[]{:S(2)}) collective-permute-start(bf16[2,1152,128]{2,1,0:T(8,128)(2,1)S(1)} %get-tuple-element.30.refs_0_), channel_id=1, source_target_pairs={{0,1},{1,0},{2,3},{3,2},{4,5},{5,4},{6,7},{7,6},{8,9},{9,8},{10,11... | collective-permute-start | bytes 1769480 | tf_op jit(solution)/shard_map/ppermute | solution.py:331
  11.6 2.8 %copy-done = bf16[2,6,512,512]{3,2,1,0:T(8,128)(2,1)S(1)} copy-done((bf16[2,6,512,512]{3,2,1,0:T(8,128)(2,1)S(1)}, bf16[2,6,512,512]{3,2,1,0:T(8,128)(2,1)}, u32[]{:S(2)}) %copy-start) | copy-done | bytes 6291480
  14.4 13.4 %head_grads.1 = bf16[7,96,1024]{2,1,0:T(8,128)(2,1)S(1)} custom-call(s32[2,4]{1,0:T(2,128)S(1)} %copy-done.3, bf16[2,576,512]{2,1,0:T(8,128)(2,1)S(1)} %bitcast.16, bf16[2,96,512]{2,1,0:T(8,128)(2,1)S(1)} %bitcast.17, bf16[2,6,512,512]{3,2,1,0:T(8,128)(2,1)S(1)} %copy-done, bf16[2,1152,128]{2,1,0:T(8,128)(2,1)S(1)} %get-tuple-element.30.refs_0_), custom_call_target="tpu_custom_call" | custom-call | flops 1000 | bytes 49000000 | tf_op jit(solution)/shard_map/head_grads/pallas_call | solution.py:115
  27.8 6.1 %collective-permute-done.2.refs_2_.refs_3_ = bf16[2,1152,128]{2,1,0:T(8,128)(2,1)S(1)} collective-permute-done((bf16[2,1152,128]{2,1,0:T(8,128)(2,1)S(1)}, bf16[2,1152,128]{2,1,0:T(8,128)(2,1)S(1)}, u32[]{:S(2)}, u32[]{:S(2)}) %collective-permute-start.2) | collective-permute-done | bytes 589856 | tf_op jit(solution)/shard_map/ppermute | solution.py:331
  36.0 3.0 %collective-permute-start.4 = (bf16[2,1152,128]{2,1,0:T(8,128)(2,1)S(1)}, bf16[2,1152,128]{2,1,0:T(8,128)(2,1)S(1)}, u32[]{:S(2)}, u32[]{:S(2)}) collective-permute-start(bf16[2,1152,128]{2,1,0:T(8,128)(2,1)S(1)} %collective-permute-done.refs_0_.refs_1_), channel_id=1, source_target_pairs={{0,1},{1,0},{2,3},{3,2},{4,5},{5,4},{6,7},{7,6},{8,9},{9,8},{10,11... | collective-permute-start | bytes 1769480 | tf_op jit(solution)/shard_map/ppermute | solution.py:331
  39.5 3.0 %collective-permute-start.6 = (bf16[2,1152,128]{2,1,0:T(8,128)(2,1)S(1)}, bf16[2,1152,128]{2,1,0:T(8,128)(2,1)S(1)}, u32[]{:S(2)}, u32[]{:S(2)}) collective-permute-start(bf16[2,1152,128]{2,1,0:T(8,128)(2,1)S(1)} %collective-permute-done.2.refs_2_.refs_3_), channel_id=1, source_target_pairs={{0,1},{1,0},{2,3},{3,2},{4,5},{5,4},{6,7},{7,6},{8,9},{9,8},{10,11... | collective-permute-start | bytes 1769480 | tf_op jit(solution)/shard_map/ppermute | solution.py:331
  42.6 22.1 %collective-permute-done.8.refs_9_.refs_10_ = bf16[672,1024]{1,0:T(8,128)(2,1)S(1)} collective-permute-done((bf16[672,1024]{1,0:T(8,128)(2,1)S(1)}, bf16[672,1024]{1,0:T(8,128)(2,1)S(1)}, u32[]{:S(2)}, u32[]{:S(2)}) %collective-permute-start.8) | collective-permute-done | bytes 1376288 | tf_op jit(solution)/shard_map/ppermute | solution.py:331
  67.0 9.1 %collective-permute-done.6.refs_7_ = bf16[2,1152,128]{2,1,0:T(8,128)(2,1)S(1)} collective-permute-done((bf16[2,1152,128]{2,1,0:T(8,128)(2,1)S(1)}, bf16[2,1152,128]{2,1,0:T(8,128)(2,1)S(1)}, u32[]{:S(2)}, u32[]{:S(2)}) %collective-permute-start.6) | collective-permute-done | bytes 589856 | tf_op jit(solution)/shard_map/ppermute | solution.py:331
  76.1 5.7 %terms.4 = (bf16[1152,1408]{1,0:T(8,128)(2,1)S(1)}, bf16[1152,1024]{1,0:T(8,128)(2,1)S(1)}) custom-call(s32[12]{0:T(128)S(1)} %stack.51.place_ref.spot_ref.refs_2_.refs_5_, bf16[2,1152,128]{2,1,0:T(8,128)(2,1)S(1)} %get-tuple-element.30.refs_0_, bf16[2,1152,128]{2,1,0:T(8,128)(2,1)S(1)} %collective-permute-done.refs_0_.refs_1_, ...), custom_call_target="tpu_custom_call" | custom-call | flops 1000 | bytes 21000000 | tf_op jit(solution)/shard_map/terms/pallas_call | solution.py:223
  82.1 5.7 %terms.5 = (bf16[1152,1408]{1,0:T(8,128)(2,1)S(1)}, bf16[1152,1024]{1,0:T(8,128)(2,1)S(1)}) custom-call(s32[12]{0:T(128)S(1)} %stack.51.place_ref.spot_ref.refs_2_.refs_5_, bf16[2,1152,128]{2,1,0:T(8,128)(2,1)S(1)} %get-tuple-element.30.refs_0_, bf16[2,1152,128]{2,1,0:T(8,128)(2,1)S(1)} %collective-permute-done.refs_0_.refs_1_, ...), custom_call_target="tpu_custom_call" | custom-call | flops 1000 | bytes 21000000 | tf_op jit(solution)/shard_map/terms/pallas_call | solution.py:223
  87.8 4.6 %terms.6.refs_3_ = bf16[1152,1408]{1,0:T(8,128)(2,1)S(1)} custom-call(bf16[1152,1024]{1,0:T(8,128)(2,1)S(1)} %get-tuple-element.36.whole_ref, bf16[336,1024]{1,0:T(8,128)(2,1)S(1)} %collective-permute-done.9.refs_0_, bf16[336,1024]{1,0:T(8,128)(2,1)S(1)} %collective-permute-done.10.refs_1_, bf16[672,1024]{1,0:T(8,128)(2,1)S(1)} %gate.1.refs_2_, ...), custom_call_target="tpu_custom_call" | custom-call | flops 1000 | bytes 21000000 | tf_op jit(solution)/shard_map/terms/pallas_call | solution.py:223
  94.2 2.0 %collective-permute-start.18 = (bf16[144,1408]{1,0:T(8,128)(2,1)S(1)}, bf16[144,1408]{1,0:T(8,128)(2,1)S(1)}, u32[]{:S(2)}, u32[]{:S(2)}) collective-permute-start(bf16[144,1408]{1,0:T(8,128)(2,1)S(1)} %get-tuple-element.43), channel_id=1, source_target_pairs={{0,16},{16,32},{32,48},{48,64},{64,80},{80,96},{96,112},{112,0},{1... | collective-permute-start | bytes 1216520 | tf_op jit(solution)/shard_map/ppermute | solution.py:331
  96.2 4.0 %collective-permute-start.19 = (bf16[144,1408]{1,0:T(8,128)(2,1)S(1)}, bf16[144,1408]{1,0:T(8,128)(2,1)S(1)}, u32[]{:S(2)}, u32[]{:S(2)}) collective-permute-start(bf16[144,1408]{1,0:T(8,128)(2,1)S(1)} %get-tuple-element.44), channel_id=1, source_target_pairs={{0,112},{16,0},{32,16},{48,32},{64,48},{80,64},{96,80},{112,96},{1... | collective-permute-start | bytes 1216520 | tf_op jit(solution)/shard_map/ppermute | solution.py:331
  100.3 4.5 %terms.7.refs_0_.refs_3_.keep_ref = bf16[1152,1408]{1,0:T(8,128)(2,1)S(1)} custom-call(bf16[1152,1024]{1,0:T(8,128)(2,1)S(1)} %get-tuple-element.35.whole_ref, bf16[336,1024]{1,0:T(8,128)(2,1)S(1)} %collective-permute-done.9.refs_0_, bf16[336,1024]{1,0:T(8,128)(2,1)S(1)} %collective-permute-done.10.refs_1_, bf16[672,1024]{1,0:T(8,128)(2,1)S(1)} %gate.1.refs_2_, ...), custom_call_target="tpu_custom_call" | custom-call | flops 1000 | bytes 21000000 | tf_op jit(solution)/shard_map/terms/pallas_call | solution.py:223
  106.1 2.0 %collective-permute-start.12 = (bf16[144,1408]{1,0:T(8,128)(2,1)S(1)}, bf16[144,1408]{1,0:T(8,128)(2,1)S(1)}, u32[]{:S(2)}, u32[]{:S(2)}) collective-permute-start(bf16[144,1408]{1,0:T(8,128)(2,1)S(1)} %get-tuple-element.38), channel_id=1, source_target_pairs={{0,112},{16,0},{32,16},{48,32},{64,48},{80,64},{96,80},{112,96},{1... | collective-permute-start | bytes 1216520 | tf_op jit(solution)/shard_map/ppermute | solution.py:331
  111.3 3.4 %collective-permute-start.21 = (bf16[144,1408]{1,0:T(8,128)(2,1)S(1)}, bf16[144,1408]{1,0:T(8,128)(2,1)S(1)}, u32[]{:S(2)}, u32[]{:S(2)}) collective-permute-start(bf16[144,1408]{1,0:T(8,128)(2,1)S(1)} %get-tuple-element.46), channel_id=1, source_target_pairs={{0,112},{16,0},{32,16},{48,32},{64,48},{80,64},{96,80},{112,96},{1... | collective-permute-start | bytes 1216520 | tf_op jit(solution)/shard_map/ppermute | solution.py:331
  114.7 4.0 %collective-permute-done.12.refs_2_ = bf16[144,1408]{1,0:T(8,128)(2,1)S(1)} collective-permute-done((bf16[144,1408]{1,0:T(8,128)(2,1)S(1)}, bf16[144,1408]{1,0:T(8,128)(2,1)S(1)}, u32[]{:S(2)}, u32[]{:S(2)}) %collective-permute-start.12) | collective-permute-done | bytes 405536 | tf_op jit(solution)/shard_map/ppermute | solution.py:331
  118.7 2.9 %collective-permute-done.13.refs_5_ = bf16[144,1408]{1,0:T(8,128)(2,1)S(1)} collective-permute-done((bf16[144,1408]{1,0:T(8,128)(2,1)S(1)}, bf16[144,1408]{1,0:T(8,128)(2,1)S(1)}, u32[]{:S(2)}, u32[]{:S(2)}) %collective-permute-start.13) | collective-permute-done | bytes 405536 | tf_op jit(solution)/shard_map/ppermute | solution.py:331
  124.6 5.7 %collective-permute-done.20.refs_2_ = bf16[144,1408]{1,0:T(8,128)(2,1)S(1)} collective-permute-done((bf16[144,1408]{1,0:T(8,128)(2,1)S(1)}, bf16[144,1408]{1,0:T(8,128)(2,1)S(1)}, u32[]{:S(2)}, u32[]{:S(2)}) %collective-permute-start.20) | collective-permute-done | bytes 405536 | tf_op jit(solution)/shard_map/ppermute | solution.py:331
  131.5 3.2 %collective-permute-start.22 = (bf16[144,1408]{1,0:T(8,128)(2,1)S(1)}, bf16[144,1408]{1,0:T(8,128)(2,1)S(1)}, u32[]{:S(2)}, u32[]{:S(2)}) collective-permute-start(bf16[144,1408]{1,0:T(8,128)(2,1)S(1)} %get-tuple-element.47), channel_id=1, source_target_pairs={{0,112},{16,0},{32,16},{48,32},{64,48},{80,64},{96,80},{112,96},{1... | collective-permute-start | bytes 1216520 | tf_op jit(solution)/shard_map/ppermute | solution.py:331
  136.1 2.9 %collective-permute-done.15.refs_5_ = bf16[144,1408]{1,0:T(8,128)(2,1)S(1)} collective-permute-done((bf16[144,1408]{1,0:T(8,128)(2,1)S(1)}, bf16[144,1408]{1,0:T(8,128)(2,1)S(1)}, u32[]{:S(2)}, u32[]{:S(2)}) %collective-permute-start.15) | collective-permute-done | bytes 405536 | tf_op jit(solution)/shard_map/ppermute | solution.py:331
  140.7 5.2 %collective-permute-done.26.refs_2_ = bf16[144,1408]{1,0:T(8,128)(2,1)S(1)} collective-permute-done((bf16[144,1408]{1,0:T(8,128)(2,1)S(1)}, bf16[144,1408]{1,0:T(8,128)(2,1)S(1)}, u32[]{:S(2)}, u32[]{:S(2)}) %collective-permute-start.26) | collective-permute-done | bytes 405536 | tf_op jit(solution)/shard_map/ppermute | solution.py:331
  146.8 5.7 %collective-permute-done.16.refs_2_ = bf16[144,1408]{1,0:T(8,128)(2,1)S(1)} collective-permute-done((bf16[144,1408]{1,0:T(8,128)(2,1)S(1)}, bf16[144,1408]{1,0:T(8,128)(2,1)S(1)}, u32[]{:S(2)}, u32[]{:S(2)}) %collective-permute-start.16) | collective-permute-done | bytes 405536 | tf_op jit(solution)/shard_map/ppermute | solution.py:331
  153.2 3.8 %collective-permute-start.23 = (bf16[144,1408]{1,0:T(8,128)(2,1)S(1)}, bf16[144,1408]{1,0:T(8,128)(2,1)S(1)}, u32[]{:S(2)}, u32[]{:S(2)}) collective-permute-start(bf16[144,1408]{1,0:T(8,128)(2,1)S(1)} %loads.14), channel_id=1, source_target_pairs={{0,112},{16,0},{32,16},{48,32},{64,48},{80,64},{96,80},{112,96},{1... | collective-permute-start | bytes 1216520 | tf_op jit(solution)/shard_map/ppermute | solution.py:331
  157.2 3.0 %collective-permute-done.27.one_ref = bf16[144,1408]{1,0:T(8,128)(2,1)S(1)} collective-permute-done((bf16[144,1408]{1,0:T(8,128)(2,1)S(1)}, bf16[144,1408]{1,0:T(8,128)(2,1)S(1)}, u32[]{:S(2)}, u32[]{:S(2)}) %collective-permute-start.27) | collective-permute-done | bytes 405536 | tf_op jit(solution)/shard_map/ppermute | solution.py:331
  162.5 3.4 %collective-permute-start.29 = (bf16[72,672]{1,0:T(8,128)(2,1)S(1)}, bf16[72,672]{1,0:T(8,128)(2,1)S(1)}, u32[]{:S(2)}, u32[]{:S(2)}) collective-permute-start(bf16[72,672]{1,0:T(8,128)(2,1)S(1)} %get-tuple-element.53), channel_id=1, source_target_pairs={{0,134},{2,128},{4,130},{6,132},{128,6},{130,0},{132,2},{134,4},{1... | collective-permute-start | bytes 290312 | tf_op jit(solution)/shard_map/ppermute | solution.py:485
  169.0 3.6 %collective-permute-start.30 = (bf16[72,672]{1,0:T(8,128)(2,1)S(1)}, bf16[72,672]{1,0:T(8,128)(2,1)S(1)}, u32[]{:S(2)}, u32[]{:S(2)}) collective-permute-start(bf16[72,672]{1,0:T(8,128)(2,1)S(1)} %get-tuple-element.54), channel_id=1, source_target_pairs={{0,4},{2,6},{4,0},{6,2},{1,5},{3,7},{5,1},{7,3},{8,12},{10,14},{12... | collective-permute-start | bytes 290312 | tf_op jit(solution)/shard_map/ppermute | solution.py:331
  173.9 2.1 %collective-permute-done.30.refs_4_ = bf16[72,672]{1,0:T(8,128)(2,1)S(1)} collective-permute-done((bf16[72,672]{1,0:T(8,128)(2,1)S(1)}, bf16[72,672]{1,0:T(8,128)(2,1)S(1)}, u32[]{:S(2)}, u32[]{:S(2)}) %collective-permute-start.30) | collective-permute-done | bytes 96800 | tf_op jit(solution)/shard_map/ppermute | solution.py:331
  176.0 3.7 %collective-permute-done.31.refs_5_ = bf16[72,672]{1,0:T(8,128)(2,1)S(1)} collective-permute-done((bf16[72,672]{1,0:T(8,128)(2,1)S(1)}, bf16[72,672]{1,0:T(8,128)(2,1)S(1)}, u32[]{:S(2)}, u32[]{:S(2)}) %collective-permute-start.31) | collective-permute-done | bytes 96800 | tf_op jit(solution)/shard_map/ppermute | solution.py:485
  179.7 1.7 finish.1
  (77 shorter events, 29.5 us)
Async XLA Ops:
  4.2 23.6 %collective-permute-start = (bf16[2,1152,128]{2,1,0:T(8,128)(2,1)S(1)}, bf16[2,1152,128]{2,1,0:T(8,128)(2,1)S(1)}, u32[]{:S(2)}, u32[]{:S(2)}) collective-permute-start(bf16[2,1152,128]{2,1,0:T(8,128)(2,1)S(1)} %get-tuple-element.31), channel_id=1, source_target_pairs={{0,2},{2,4},{4,6},{6,0},{1,3},{3,5},{5,7},{7,1},{8,10},{10,12},{12... | collective-permute-start | bytes 1769480 | tf_op jit(solution)/shard_map/ppermute | solution.py:331
  5.8 22.0 %collective-permute-start.1 = (bf16[2,1152,128]{2,1,0:T(8,128)(2,1)S(1)}, bf16[2,1152,128]{2,1,0:T(8,128)(2,1)S(1)}, u32[]{:S(2)}, u32[]{:S(2)}) collective-permute-start(bf16[2,1152,128]{2,1,0:T(8,128)(2,1)S(1)} %get-tuple-element.32), channel_id=1, source_target_pairs={{0,6},{2,0},{4,2},{6,4},{1,7},{3,1},{5,3},{7,5},{8,14},{10,8},{12,... | collective-permute-start | bytes 1769480 | tf_op jit(solution)/shard_map/ppermute | solution.py:331
  6.5 27.4 %collective-permute-start.2 = (bf16[2,1152,128]{2,1,0:T(8,128)(2,1)S(1)}, bf16[2,1152,128]{2,1,0:T(8,128)(2,1)S(1)}, u32[]{:S(2)}, u32[]{:S(2)}) collective-permute-start(bf16[2,1152,128]{2,1,0:T(8,128)(2,1)S(1)} %get-tuple-element.33), channel_id=1, source_target_pairs={{0,4},{2,6},{4,0},{6,2},{1,5},{3,7},{5,1},{7,3},{8,12},{10,14},{12... | collective-permute-start | bytes 1769480 | tf_op jit(solution)/shard_map/ppermute | solution.py:331
  8.6 25.4 %collective-permute-start.3 = (bf16[2,1152,128]{2,1,0:T(8,128)(2,1)S(1)}, bf16[2,1152,128]{2,1,0:T(8,128)(2,1)S(1)}, u32[]{:S(2)}, u32[]{:S(2)}) collective-permute-start(bf16[2,1152,128]{2,1,0:T(8,128)(2,1)S(1)} %get-tuple-element.30.refs_0_), channel_id=1, source_target_pairs={{0,1},{1,0},{2,3},{3,2},{4,5},{5,4},{6,7},{7,6},{8,9},{9,8},{10,11... | collective-permute-start | bytes 1769480 | tf_op jit(solution)/shard_map/ppermute | solution.py:331
  34.0 30.7 %collective-permute-start.8 = (bf16[672,1024]{1,0:T(8,128)(2,1)S(1)}, bf16[672,1024]{1,0:T(8,128)(2,1)S(1)}, u32[]{:S(2)}, u32[]{:S(2)}) collective-permute-start(bf16[672,1024]{1,0:T(8,128)(2,1)S(1)} %gate.1.refs_2_), channel_id=1, source_target_pairs={{0,6},{2,0},{4,2},{6,4},{1,7},{3,1},{5,3},{7,5},{8,14},{10,8},{12,... | collective-permute-start | bytes 4128776 | tf_op jit(solution)/shard_map/ppermute | solution.py:331
  34.9 31.2 %collective-permute-start.7 = (bf16[672,1024]{1,0:T(8,128)(2,1)S(1)}, bf16[672,1024]{1,0:T(8,128)(2,1)S(1)}, u32[]{:S(2)}, u32[]{:S(2)}) collective-permute-start(bf16[672,1024]{1,0:T(8,128)(2,1)S(1)} %gate.1.refs_2_), channel_id=1, source_target_pairs={{0,2},{2,4},{4,6},{6,0},{1,3},{3,5},{5,7},{7,1},{8,10},{10,12},{12... | collective-permute-start | bytes 4128776 | tf_op jit(solution)/shard_map/ppermute | solution.py:331
  36.0 31.0 %collective-permute-start.4 = (bf16[2,1152,128]{2,1,0:T(8,128)(2,1)S(1)}, bf16[2,1152,128]{2,1,0:T(8,128)(2,1)S(1)}, u32[]{:S(2)}, u32[]{:S(2)}) collective-permute-start(bf16[2,1152,128]{2,1,0:T(8,128)(2,1)S(1)} %collective-permute-done.refs_0_.refs_1_), channel_id=1, source_target_pairs={{0,1},{1,0},{2,3},{3,2},{4,5},{5,4},{6,7},{7,6},{8,9},{9,8},{10,11... | collective-permute-start | bytes 1769480 | tf_op jit(solution)/shard_map/ppermute | solution.py:331
  39.0 28.0 %collective-permute-start.5 = (bf16[2,1152,128]{2,1,0:T(8,128)(2,1)S(1)}, bf16[2,1152,128]{2,1,0:T(8,128)(2,1)S(1)}, u32[]{:S(2)}, u32[]{:S(2)}) collective-permute-start(bf16[2,1152,128]{2,1,0:T(8,128)(2,1)S(1)} %collective-permute-done.1.refs_1_.refs_2_), channel_id=1, source_target_pairs={{0,1},{1,0},{2,3},{3,2},{4,5},{5,4},{6,7},{7,6},{8,9},{9,8},{10,11... | collective-permute-start | bytes 1769480 | tf_op jit(solution)/shard_map/ppermute | solution.py:331
  39.5 36.6 %collective-permute-start.6 = (bf16[2,1152,128]{2,1,0:T(8,128)(2,1)S(1)}, bf16[2,1152,128]{2,1,0:T(8,128)(2,1)S(1)}, u32[]{:S(2)}, u32[]{:S(2)}) collective-permute-start(bf16[2,1152,128]{2,1,0:T(8,128)(2,1)S(1)} %collective-permute-done.2.refs_2_.refs_3_), channel_id=1, source_target_pairs={{0,1},{1,0},{2,3},{3,2},{4,5},{5,4},{6,7},{7,6},{8,9},{9,8},{10,11... | collective-permute-start | bytes 1769480 | tf_op jit(solution)/shard_map/ppermute | solution.py:331
  64.8 23.1 %collective-permute-start.10 = (bf16[336,1024]{1,0:T(8,128)(2,1)S(1)}, bf16[336,1024]{1,0:T(8,128)(2,1)S(1)}, u32[]{:S(2)}, u32[]{:S(2)}) collective-permute-start(bf16[336,1024]{1,0:T(8,128)(2,1)S(1)} %slice.9), channel_id=1, source_target_pairs={{0,6},{2,0},{4,2},{6,4},{1,7},{3,1},{5,3},{7,5},{8,14},{10,8},{12,... | collective-permute-start | bytes 2064392 | tf_op jit(solution)/shard_map/ppermute | solution.py:331
  66.1 21.7 %collective-permute-start.9 = (bf16[336,1024]{1,0:T(8,128)(2,1)S(1)}, bf16[336,1024]{1,0:T(8,128)(2,1)S(1)}, u32[]{:S(2)}, u32[]{:S(2)}) collective-permute-start(bf16[336,1024]{1,0:T(8,128)(2,1)S(1)} %slice.8), channel_id=1, source_target_pairs={{0,2},{2,4},{4,6},{6,0},{1,3},{3,5},{5,7},{7,1},{8,10},{10,12},{12... | collective-permute-start | bytes 2064392 | tf_op jit(solution)/shard_map/ppermute | solution.py:331
  81.8 11.2 %collective-permute-start.17 = (bf16[1152,1408]{1,0:T(8,128)(2,1)S(1)}, bf16[1152,1408]{1,0:T(8,128)(2,1)S(1)}, u32[]{:S(2)}, u32[]{:S(2)}) collective-permute-start(bf16[1152,1408]{1,0:T(8,128)(2,1)S(1)} %get-tuple-element.34.refs_10_), channel_id=1, source_target_pairs={{0,8},{8,0},{1,9},{9,1},{2,10},{10,2},{3,11},{11,3},{4,12},{12,4},... | collective-permute-start | bytes 9732104 | tf_op jit(solution)/shard_map/ppermute | solution.py:331
  92.4 12.4 %collective-permute-start.11 = (bf16[1152,1408]{1,0:T(8,128)(2,1)S(1)}, bf16[1152,1408]{1,0:T(8,128)(2,1)S(1)}, u32[]{:S(2)}, u32[]{:S(2)}) collective-permute-start(bf16[1152,1408]{1,0:T(8,128)(2,1)S(1)} %terms.6.refs_3_), channel_id=1, source_target_pairs={{0,8},{8,0},{1,9},{9,1},{2,10},{10,2},{3,11},{11,3},{4,12},{12,4},... | collective-permute-start | bytes 9732104 | tf_op jit(solution)/shard_map/ppermute | solution.py:331
  94.2 15.5 %collective-permute-start.18 = (bf16[144,1408]{1,0:T(8,128)(2,1)S(1)}, bf16[144,1408]{1,0:T(8,128)(2,1)S(1)}, u32[]{:S(2)}, u32[]{:S(2)}) collective-permute-start(bf16[144,1408]{1,0:T(8,128)(2,1)S(1)} %get-tuple-element.43), channel_id=1, source_target_pairs={{0,16},{16,32},{32,48},{48,64},{64,80},{80,96},{96,112},{112,0},{1... | collective-permute-start | bytes 1216520 | tf_op jit(solution)/shard_map/ppermute | solution.py:331
  96.2 13.8 %collective-permute-start.19 = (bf16[144,1408]{1,0:T(8,128)(2,1)S(1)}, bf16[144,1408]{1,0:T(8,128)(2,1)S(1)}, u32[]{:S(2)}, u32[]{:S(2)}) collective-permute-start(bf16[144,1408]{1,0:T(8,128)(2,1)S(1)} %get-tuple-element.44), channel_id=1, source_target_pairs={{0,112},{16,0},{32,16},{48,32},{64,48},{80,64},{96,80},{112,96},{1... | collective-permute-start | bytes 1216520 | tf_op jit(solution)/shard_map/ppermute | solution.py:331
  106.1 12.6 %collective-permute-start.12 = (bf16[144,1408]{1,0:T(8,128)(2,1)S(1)}, bf16[144,1408]{1,0:T(8,128)(2,1)S(1)}, u32[]{:S(2)}, u32[]{:S(2)}) collective-permute-start(bf16[144,1408]{1,0:T(8,128)(2,1)S(1)} %get-tuple-element.38), channel_id=1, source_target_pairs={{0,112},{16,0},{32,16},{48,32},{64,48},{80,64},{96,80},{112,96},{1... | collective-permute-start | bytes 1216520 | tf_op jit(solution)/shard_map/ppermute | solution.py:331
  108.1 13.5 %collective-permute-start.13 = (bf16[144,1408]{1,0:T(8,128)(2,1)S(1)}, bf16[144,1408]{1,0:T(8,128)(2,1)S(1)}, u32[]{:S(2)}, u32[]{:S(2)}) collective-permute-start(bf16[144,1408]{1,0:T(8,128)(2,1)S(1)} %get-tuple-element.39), channel_id=1, source_target_pairs={{0,16},{16,32},{32,48},{48,64},{64,80},{80,96},{96,112},{112,0},{1... | collective-permute-start | bytes 1216520 | tf_op jit(solution)/shard_map/ppermute | solution.py:331
  110.9 19.5 %collective-permute-start.20 = (bf16[144,1408]{1,0:T(8,128)(2,1)S(1)}, bf16[144,1408]{1,0:T(8,128)(2,1)S(1)}, u32[]{:S(2)}, u32[]{:S(2)}) collective-permute-start(bf16[144,1408]{1,0:T(8,128)(2,1)S(1)} %get-tuple-element.45), channel_id=1, source_target_pairs={{0,16},{16,32},{32,48},{48,64},{64,80},{80,96},{96,112},{112,0},{1... | collective-permute-start | bytes 1216520 | tf_op jit(solution)/shard_map/ppermute | solution.py:331
  111.3 19.0 %collective-permute-start.21 = (bf16[144,1408]{1,0:T(8,128)(2,1)S(1)}, bf16[144,1408]{1,0:T(8,128)(2,1)S(1)}, u32[]{:S(2)}, u32[]{:S(2)}) collective-permute-start(bf16[144,1408]{1,0:T(8,128)(2,1)S(1)} %get-tuple-element.46), channel_id=1, source_target_pairs={{0,112},{16,0},{32,16},{48,32},{64,48},{80,64},{96,80},{112,96},{1... | collective-permute-start | bytes 1216520 | tf_op jit(solution)/shard_map/ppermute | solution.py:331
  122.5 13.6 %collective-permute-start.14 = (bf16[144,1408]{1,0:T(8,128)(2,1)S(1)}, bf16[144,1408]{1,0:T(8,128)(2,1)S(1)}, u32[]{:S(2)}, u32[]{:S(2)}) collective-permute-start(bf16[144,1408]{1,0:T(8,128)(2,1)S(1)} %get-tuple-element.40), channel_id=1, source_target_pairs={{0,112},{16,0},{32,16},{48,32},{64,48},{80,64},{96,80},{112,96},{1... | collective-permute-start | bytes 1216520 | tf_op jit(solution)/shard_map/ppermute | solution.py:331
  123.3 15.7 %collective-permute-start.15 = (bf16[144,1408]{1,0:T(8,128)(2,1)S(1)}, bf16[144,1408]{1,0:T(8,128)(2,1)S(1)}, u32[]{:S(2)}, u32[]{:S(2)}) collective-permute-start(bf16[144,1408]{1,0:T(8,128)(2,1)S(1)} %get-tuple-element.41), channel_id=1, source_target_pairs={{0,16},{16,32},{32,48},{48,64},{64,80},{80,96},{96,112},{112,0},{1... | collective-permute-start | bytes 1216520 | tf_op jit(solution)/shard_map/ppermute | solution.py:331
  131.2 14.7 %collective-permute-start.26 = (bf16[144,1408]{1,0:T(8,128)(2,1)S(1)}, bf16[144,1408]{1,0:T(8,128)(2,1)S(1)}, u32[]{:S(2)}, u32[]{:S(2)}) collective-permute-start(bf16[144,1408]{1,0:T(8,128)(2,1)S(1)} %get-tuple-element.51), channel_id=1, source_target_pairs={{0,16},{16,32},{32,48},{48,64},{64,80},{80,96},{96,112},{112,0},{1... | collective-permute-start | bytes 1216520 | tf_op jit(solution)/shard_map/ppermute | solution.py:331
  131.5 15.3 %collective-permute-start.22 = (bf16[144,1408]{1,0:T(8,128)(2,1)S(1)}, bf16[144,1408]{1,0:T(8,128)(2,1)S(1)}, u32[]{:S(2)}, u32[]{:S(2)}) collective-permute-start(bf16[144,1408]{1,0:T(8,128)(2,1)S(1)} %get-tuple-element.47), channel_id=1, source_target_pairs={{0,112},{16,0},{32,16},{48,32},{64,48},{80,64},{96,80},{112,96},{1... | collective-permute-start | bytes 1216520 | tf_op jit(solution)/shard_map/ppermute | solution.py:331
  139.9 12.7 %collective-permute-start.16 = (bf16[144,1408]{1,0:T(8,128)(2,1)S(1)}, bf16[144,1408]{1,0:T(8,128)(2,1)S(1)}, u32[]{:S(2)}, u32[]{:S(2)}) collective-permute-start(bf16[144,1408]{1,0:T(8,128)(2,1)S(1)} %get-tuple-element.42), channel_id=1, source_target_pairs={{0,112},{16,0},{32,16},{48,32},{64,48},{80,64},{96,80},{112,96},{1... | collective-permute-start | bytes 1216520 | tf_op jit(solution)/shard_map/ppermute | solution.py:331
  146.6 13.6 %collective-permute-start.27 = (bf16[144,1408]{1,0:T(8,128)(2,1)S(1)}, bf16[144,1408]{1,0:T(8,128)(2,1)S(1)}, u32[]{:S(2)}, u32[]{:S(2)}) collective-permute-start(bf16[144,1408]{1,0:T(8,128)(2,1)S(1)} %loads.15), channel_id=1, source_target_pairs={{0,16},{16,32},{32,48},{48,64},{64,80},{80,96},{96,112},{112,0},{1... | collective-permute-start | bytes 1216520 | tf_op jit(solution)/shard_map/ppermute | solution.py:331
  146.7 19.4 %collective-permute-start.24 = (bf16[144,1408]{1,0:T(8,128)(2,1)S(1)}, bf16[144,1408]{1,0:T(8,128)(2,1)S(1)}, u32[]{:S(2)}, u32[]{:S(2)}) collective-permute-start(bf16[144,1408]{1,0:T(8,128)(2,1)S(1)} %get-tuple-element.48), channel_id=1, source_target_pairs={{0,16},{16,32},{32,48},{48,64},{64,80},{80,96},{96,112},{112,0},{1... | collective-permute-start | bytes 1216520 | tf_op jit(solution)/shard_map/ppermute | solution.py:331
  153.2 14.1 %collective-permute-start.23 = (bf16[144,1408]{1,0:T(8,128)(2,1)S(1)}, bf16[144,1408]{1,0:T(8,128)(2,1)S(1)}, u32[]{:S(2)}, u32[]{:S(2)}) collective-permute-start(bf16[144,1408]{1,0:T(8,128)(2,1)S(1)} %loads.14), channel_id=1, source_target_pairs={{0,112},{16,0},{32,16},{48,32},{64,48},{80,64},{96,80},{112,96},{1... | collective-permute-start | bytes 1216520 | tf_op jit(solution)/shard_map/ppermute | solution.py:331
  161.2 7.8 %collective-permute-start.28 = (bf16[72,672]{1,0:T(8,128)(2,1)S(1)}, bf16[72,672]{1,0:T(8,128)(2,1)S(1)}, u32[]{:S(2)}, u32[]{:S(2)}) collective-permute-start(bf16[72,672]{1,0:T(8,128)(2,1)S(1)} %get-tuple-element.52), channel_id=1, source_target_pairs={{0,6},{2,0},{4,2},{6,4},{1,7},{3,1},{5,3},{7,5},{8,14},{10,8},{12,... | collective-permute-start | bytes 290312 | tf_op jit(solution)/shard_map/ppermute | solution.py:331
  162.5 10.1 %collective-permute-start.29 = (bf16[72,672]{1,0:T(8,128)(2,1)S(1)}, bf16[72,672]{1,0:T(8,128)(2,1)S(1)}, u32[]{:S(2)}, u32[]{:S(2)}) collective-permute-start(bf16[72,672]{1,0:T(8,128)(2,1)S(1)} %get-tuple-element.53), channel_id=1, source_target_pairs={{0,134},{2,128},{4,130},{6,132},{128,6},{130,0},{132,2},{134,4},{1... | collective-permute-start | bytes 290312 | tf_op jit(solution)/shard_map/ppermute | solution.py:485
  165.9 7.6 %collective-permute-start.32 = (bf16[72,672]{1,0:T(8,128)(2,1)S(1)}, bf16[72,672]{1,0:T(8,128)(2,1)S(1)}, u32[]{:S(2)}, u32[]{:S(2)}) collective-permute-start(bf16[72,672]{1,0:T(8,128)(2,1)S(1)} %get-tuple-element.56), channel_id=1, source_target_pairs={{0,2},{2,4},{4,6},{6,0},{1,3},{3,5},{5,7},{7,1},{8,10},{10,12},{12... | collective-permute-start | bytes 290312 | tf_op jit(solution)/shard_map/ppermute | solution.py:331
  166.1 7.4 %collective-permute-start.33 = (bf16[72,672]{1,0:T(8,128)(2,1)S(1)}, bf16[72,672]{1,0:T(8,128)(2,1)S(1)}, u32[]{:S(2)}, u32[]{:S(2)}) collective-permute-start(bf16[72,672]{1,0:T(8,128)(2,1)S(1)} %get-tuple-element.57), channel_id=1, source_target_pairs={{0,130},{2,132},{4,134},{6,128},{128,2},{130,4},{132,6},{134,0},{1... | collective-permute-start | bytes 290312 | tf_op jit(solution)/shard_map/ppermute | solution.py:485
  172.5 7.2 %collective-permute-start.31 = (bf16[72,672]{1,0:T(8,128)(2,1)S(1)}, bf16[72,672]{1,0:T(8,128)(2,1)S(1)}, u32[]{:S(2)}, u32[]{:S(2)}) collective-permute-start(bf16[72,672]{1,0:T(8,128)(2,1)S(1)} %get-tuple-element.55), channel_id=1, source_target_pairs={{0,132},{2,134},{4,128},{6,130},{128,4},{130,6},{132,0},{134,2},{1... | collective-permute-start | bytes 290312 | tf_op jit(solution)/shard_map/ppermute | solution.py:485
  (10 other events, 80.9 us)
